TPU v7x, 32 devices: a whole 2x2x4 slice. The times are simulated.
32 devices in a mesh: rows: 8 (over z, y), cols: 4 (over x, core).
Axes of the slice: x: 2, y: 2, z: 4, core: 2. Of those that a mesh axis runs over, the one named last changes fastest.
Arguments:
- series: float32 [300, 16384], P(None, ('rows', 'cols')), may hold values from -6 to 6
- point_order: int32 [16384], P('rows'), may hold values from 0 to 16383, as said below
- step_block: int32 [8], replicated, may hold values from 0 to 15, as said below
- panel: float32 [16384, 8192], P('rows', 'cols'), may hold values from -0.09375 to 0.09375
- diag_inverse: float32 [16384, 1024], P('rows'), may hold values from -0.09375 to 1.09375
Outputs:
- solved: float32 [8192, 300], P(('rows', 'cols'))
- residual: float32 [16384, 300], P(('rows', 'cols'))
Inputs may be any that keep to these rules, and one draw needn't show every extreme that they name: Within each group of 2048 consecutive points, point_order is a permutation of the same group's indices. `step_block`: step k lies in block rows k * 2 + c to k * 2 + c + 1, with c = 0; the first step takes the first row of its range and the last step the last row of its range.
All inputs are finite; a program needn't handle non-finite values.
Results may differ from a plain program's by a relative error of at most 0.00014.
Values sent between devices are 32-bit elements; how exact they have to be, the bound alone decides.
No kernel may reach another device: no remote copies, remote signals or barrier semaphores. Data moves between devices by JAX's collectives and lax.ppermute only.
A program may use at most 128 MiB of HBM per device.

v0:
```python
import jax
import jax.numpy as jnp
from jax import lax
from jax.sharding import PartitionSpec as P

STEPS = 8


def from_root(value, axis, source):
    kept = jnp.where(lax.axis_index(axis) == source, value, 0).astype(value.dtype)
    return lax.psum(kept, axis)


def body(series, point_order, step_block, panel, diag_inverse):
    highest = lax.Precision.HIGHEST
    gathered = lax.all_gather(series, "cols", axis=1, tiled=True)
    group_rows = gathered.shape[1]
    date_count = gathered.shape[0]
    block_size = diag_inverse.shape[1]
    local_blocks = group_rows // block_size
    per_column = panel.shape[1] // block_size
    local_index = point_order % group_rows
    right_side = jnp.take(gathered, local_index, axis=1).T
    column_index = lax.axis_index("cols")
    row_index = lax.axis_index("rows")
    flat_index = row_index * lax.axis_size("cols") + column_index
    out_rows = STEPS * block_size // (lax.axis_size("rows") * lax.axis_size("cols"))
    out_first = flat_index * out_rows
    target_section = out_first // block_size
    target_offset = out_first % block_size

    def product_rows(first_row, count, section_index, solution):
        local_column = (section_index - column_index * per_column) * block_size
        factor = lax.dynamic_slice(panel, (first_row, local_column), (count, block_size))
        return jnp.dot(factor, solution, precision=highest, preferred_element_type=jnp.float32)

    running = jnp.zeros((group_rows, date_count), jnp.float32)
    kept = jnp.zeros((out_rows, date_count), jnp.float32)
    for section in range(STEPS):
        slot_start = step_block[section] % local_blocks * block_size
        owner = step_block[section] // local_blocks
        partial_value = lax.dynamic_slice(
            running, (slot_start, jnp.int32(0)), (block_size, date_count)
        )
        summed = lax.psum(partial_value, "cols")
        pivot = (
            lax.dynamic_slice(right_side, (slot_start, jnp.int32(0)), (block_size, date_count))
            - summed
        )
        inverse = lax.dynamic_slice(
            diag_inverse, (slot_start, jnp.int32(0)), (block_size, block_size)
        )
        local_solution = jnp.dot(
            inverse, pivot, precision=highest, preferred_element_type=jnp.float32
        )
        solution = from_root(local_solution, "rows", owner)
        piece = lax.dynamic_slice(solution, (target_offset, jnp.int32(0)), (out_rows, date_count))
        kept = jnp.where(target_section == section, piece, kept)
        add_first_row = jnp.int32(0)
        add_section_index = section
        owned = add_section_index // per_column == column_index
        running = lax.cond(
            owned,
            lambda acc: acc + product_rows(add_first_row, group_rows, add_section_index, solution),
            lambda acc: acc,
            running,
        )
    share = lax.psum_scatter(running, "cols", scatter_dimension=0, tiled=True)
    share_rows = share.shape[0]
    own_side = lax.dynamic_slice(
        right_side, (column_index * share_rows, jnp.int32(0)), (share_rows, date_count)
    )
    return (kept, own_side - share)


def solution(mesh):
    in_specs = (P(None, ("rows", "cols")), P("rows"), P(), P("rows", "cols"), P("rows", None))
    out_specs = (P(("rows", "cols"), None), P(("rows", "cols"), None))
    return jax.shard_map(body, mesh=mesh, in_specs=in_specs, out_specs=out_specs, check_vma=False)
```

profile of v0, /device:TPU:14, one launch (start us, length us, event | category | flops | bytes accessed | tf_op | source)
XLA Modules:
  0.0 1235.4 jit_solution(12376499332361540423)
XLA Ops:
  7.2 2.2 copy.7
  9.5 1.6 fusion.97
  15.1 23.2 %all-gather.2.cloned.1.call-done = f32[300,2048]{0,1:T(8,128)} async-done(((f32[300,512]{0,1:T(8,128)}), f32[300,2048]{0,1:T(8,128)}) %all-gather.2.cloned.1.call-update) | async-done | bytes 2457616 | tf_op jit(solution)/shard_map/all_gather | solution.py:16
  38.3 10.9 gather_fusion
  49.3 2.1 broadcast_select_fusion
  51.4 1.6 copy-done
  53.0 7.7 fusion.83
  62.5 81.0 %all-reduce.16.cloned.1.call-done = f32[1024,300]{0,1:T(8,128)} async-done(((f32[1024,300]{0,1:T(8,128)}), f32[1024,300]{0,1:T(8,128)}) %all-reduce.16.cloned.1.call-update) | async-done | bytes 1228816 | tf_op jit(solution)/shard_map/psum | solution.py:11
  143.8 1.2 constant_dynamic-slice_fusion.4
  145.0 3.0 copy.33
  149.1 50.5 %all-reduce.18.cloned.1.call-done = f32[1024,300]{1,0:T(8,128)} async-done(((f32[1024,300]{1,0:T(8,128)}), f32[1024,300]{1,0:T(8,128)}) %all-reduce.18.cloned.1.call-update) | async-done | bytes 1228816 | tf_op jit(solution)/shard_map/psum | solution.py:45
  199.6 8.5 fusion.65
  210.2 80.6 %all-reduce.20.cloned.1.call-done = f32[1024,300]{0,1:T(8,128)} async-done(((f32[1024,300]{0,1:T(8,128)}), f32[1024,300]{0,1:T(8,128)}) %all-reduce.20.cloned.1.call-update) | async-done | bytes 1228816 | tf_op jit(solution)/shard_map/psum | solution.py:11
  290.9 1.2 constant_dynamic-slice_fusion.3
  292.0 3.0 copy.34
  296.0 51.0 %all-reduce.22.cloned.1.call-done = f32[1024,300]{1,0:T(8,128)} async-done(((f32[1024,300]{1,0:T(8,128)}), f32[1024,300]{1,0:T(8,128)}) %all-reduce.22.cloned.1.call-update) | async-done | bytes 1228816 | tf_op jit(solution)/shard_map/psum | solution.py:45
  346.9 8.5 fusion.68
  357.4 80.8 %all-reduce.24.cloned.1.call-done = f32[1024,300]{0,1:T(8,128)} async-done(((f32[1024,300]{0,1:T(8,128)}), f32[1024,300]{0,1:T(8,128)}) %all-reduce.24.cloned.1.call-update) | async-done | bytes 1228816 | tf_op jit(solution)/shard_map/psum | solution.py:11
  439.4 3.0 copy.35
  443.3 50.5 %all-reduce.26.cloned.1.call-done = f32[1024,300]{1,0:T(8,128)} async-done(((f32[1024,300]{1,0:T(8,128)}), f32[1024,300]{1,0:T(8,128)}) %all-reduce.26.cloned.1.call-update) | async-done | bytes 1228816 | tf_op jit(solution)/shard_map/psum | solution.py:45
  493.8 8.5 fusion.71
  504.3 80.8 %all-reduce.28.cloned.1.call-done = f32[1024,300]{0,1:T(8,128)} async-done(((f32[1024,300]{0,1:T(8,128)}), f32[1024,300]{0,1:T(8,128)}) %all-reduce.28.cloned.1.call-update) | async-done | bytes 1228816 | tf_op jit(solution)/shard_map/psum | solution.py:11
  586.3 3.0 copy.36
  590.4 50.3 %all-reduce.30.cloned.1.call-done = f32[1024,300]{1,0:T(8,128)} async-done(((f32[1024,300]{1,0:T(8,128)}), f32[1024,300]{1,0:T(8,128)}) %all-reduce.30.cloned.1.call-update) | async-done | bytes 1228816 | tf_op jit(solution)/shard_map/psum | solution.py:45
  640.6 8.5 fusion.74
  651.3 80.6 %all-reduce.32.cloned.1.call-done = f32[1024,300]{0,1:T(8,128)} async-done(((f32[1024,300]{0,1:T(8,128)}), f32[1024,300]{0,1:T(8,128)}) %all-reduce.32.cloned.1.call-update) | async-done | bytes 1228816 | tf_op jit(solution)/shard_map/psum | solution.py:11
  731.9 11.2 conditional.12
  731.9 11.2 fusion.23
  743.2 1.2 constant_dynamic-slice_fusion
  744.4 3.0 copy.37
  748.3 40.6 %all-reduce.34.cloned.1.call-done = f32[1024,300]{1,0:T(8,128)} async-done(((f32[1024,300]{1,0:T(8,128)}), f32[1024,300]{1,0:T(8,128)}) %all-reduce.34.cloned.1.call-update) | async-done | bytes 1228816 | tf_op jit(solution)/shard_map/psum | solution.py:45
  788.9 8.5 fusion.77
  799.5 80.7 %all-reduce.36.cloned.1.call-done = f32[1024,300]{0,1:T(8,128)} async-done(((f32[1024,300]{0,1:T(8,128)}), f32[1024,300]{0,1:T(8,128)}) %all-reduce.36.cloned.1.call-update) | async-done | bytes 1228816 | tf_op jit(solution)/shard_map/psum | solution.py:11
  880.2 11.2 conditional.13
  880.2 11.2 fusion.29
  891.5 1.2 constant_dynamic-slice_fusion.6
  892.6 3.0 copy.38
  896.6 40.6 %all-reduce.38.cloned.1.call-done = f32[1024,300]{1,0:T(8,128)} async-done(((f32[1024,300]{1,0:T(8,128)}), f32[1024,300]{1,0:T(8,128)}) %all-reduce.38.cloned.1.call-update) | async-done | bytes 1228816 | tf_op jit(solution)/shard_map/psum | solution.py:45
  937.2 8.5 fusion.80
  947.7 80.8 %all-reduce.40.cloned.1.call-done = f32[1024,300]{0,1:T(8,128)} async-done(((f32[1024,300]{0,1:T(8,128)}), f32[1024,300]{0,1:T(8,128)}) %all-reduce.40.cloned.1.call-update) | async-done | bytes 1228816 | tf_op jit(solution)/shard_map/psum | solution.py:11
  1029.7 3.0 copy.39
  1033.6 51.3 %all-reduce.42.cloned.1.call-done = f32[1024,300]{1,0:T(8,128)} async-done(((f32[1024,300]{1,0:T(8,128)}), f32[1024,300]{1,0:T(8,128)}) %all-reduce.42.cloned.1.call-update) | async-done | bytes 1228816 | tf_op jit(solution)/shard_map/psum | solution.py:45
  1084.9 8.5 fusion.62
  1093.5 82.7 %all-reduce.44.cloned.1.call-done = f32[1024,300]{0,1:T(8,128)} async-done(((f32[1024,300]{0,1:T(8,128)}), f32[1024,300]{0,1:T(8,128)}) %all-reduce.44.cloned.1.call-update) | async-done | bytes 1228816 | tf_op jit(solution)/shard_map/psum | solution.py:11
  1176.2 2.3 copy.23
  1178.6 2.5 select_select_fusion
  1181.2 44.8 %reduce-scatter.2.cloned.1.call-done = f32[512,300]{1,0:T(8,128)} async-done(((f32[2048,300]{1,0:T(8,128)}), f32[512,300]{1,0:T(8,128)}) %reduce-scatter.2.cloned.1.call-update) | async-done | bytes 614416 | tf_op jit(solution)/shard_map/reduce_scatter | solution.py:68
  1225.9 1.5 dynamic-slice_subtract_fusion.28
  (48 shorter events, 9.4 us)
Async XLA Ops:
  7.2 31.2 %all-gather.2.cloned.1.call-start = ((), (), s32[]{:S(2)}) async-start(), calls=%async_computation.1 | async-start | bytes 3932160 | tf_op jit(solution)/shard_map/all_gather | solution.py:16
  9.5 134.1 %all-reduce.16.cloned.1.call-start = ((), (), s32[]{:S(2)}) async-start(), calls=%async_computation.2 | async-start | bytes 2490368 | tf_op jit(solution)/shard_map/psum | solution.py:11
  51.4 1.7 copy-start
  60.7 138.8 %all-reduce.18.cloned.1.call-start = ((), (), s32[]{:S(2)}) async-start(), calls=%async_computation.3 | async-start | bytes 3145728 | tf_op jit(solution)/shard_map/psum | solution.py:45
  148.0 142.9 %all-reduce.20.cloned.1.call-start = ((), (), s32[]{:S(2)}) async-start(), calls=%async_computation.4 | async-start | bytes 2490368 | tf_op jit(solution)/shard_map/psum | solution.py:11
  208.1 138.8 %all-reduce.22.cloned.1.call-start = ((), (), s32[]{:S(2)}) async-start(), calls=%async_computation.5 | async-start | bytes 3145728 | tf_op jit(solution)/shard_map/psum | solution.py:45
  295.0 143.2 %all-reduce.24.cloned.1.call-start = ((), (), s32[]{:S(2)}) async-start(), calls=%async_computation.6 | async-start | bytes 2490368 | tf_op jit(solution)/shard_map/psum | solution.py:11
  355.5 138.3 %all-reduce.26.cloned.1.call-start = ((), (), s32[]{:S(2)}) async-start(), calls=%async_computation.7 | async-start | bytes 3145728 | tf_op jit(solution)/shard_map/psum | solution.py:45
  442.4 142.7 %all-reduce.28.cloned.1.call-start = ((), (), s32[]{:S(2)}) async-start(), calls=%async_computation.8 | async-start | bytes 2490368 | tf_op jit(solution)/shard_map/psum | solution.py:11
  502.3 138.3 %all-reduce.30.cloned.1.call-start = ((), (), s32[]{:S(2)}) async-start(), calls=%async_computation.9 | async-start | bytes 3145728 | tf_op jit(solution)/shard_map/psum | solution.py:45
  589.3 142.7 %all-reduce.32.cloned.1.call-start = ((), (), s32[]{:S(2)}) async-start(), calls=%async_computation.10 | async-start | bytes 2490368 | tf_op jit(solution)/shard_map/psum | solution.py:11
  649.2 139.7 %all-reduce.34.cloned.1.call-start = ((), (), s32[]{:S(2)}) async-start(), calls=%async_computation.11 | async-start | bytes 3145728 | tf_op jit(solution)/shard_map/psum | solution.py:45
  747.3 132.9 %all-reduce.36.cloned.1.call-start = ((), (), s32[]{:S(2)}) async-start(), calls=%async_computation.12 | async-start | bytes 2490368 | tf_op jit(solution)/shard_map/psum | solution.py:11
  797.4 139.8 %all-reduce.38.cloned.1.call-start = ((), (), s32[]{:S(2)}) async-start(), calls=%async_computation.13 | async-start | bytes 3145728 | tf_op jit(solution)/shard_map/psum | solution.py:45
  895.6 132.9 %all-reduce.40.cloned.1.call-start = ((), (), s32[]{:S(2)}) async-start(), calls=%async_computation.14 | async-start | bytes 2490368 | tf_op jit(solution)/shard_map/psum | solution.py:11
  945.7 139.2 %all-reduce.42.cloned.1.call-start = ((), (), s32[]{:S(2)}) async-start(), calls=%async_computation.15 | async-start | bytes 3145728 | tf_op jit(solution)/shard_map/psum | solution.py:45
  1032.6 143.6 %all-reduce.44.cloned.1.call-start = ((), (), s32[]{:S(2)}) async-start(), calls=%async_computation.16 | async-start | bytes 2490368 | tf_op jit(solution)/shard_map/psum | solution.py:11
  1093.5 132.5 %reduce-scatter.2.cloned.1.call-start = ((), (), s32[]{:S(2)}) async-start(), calls=%async_computation.17 | async-start | bytes 3932160 | tf_op jit(solution)/shard_map/reduce_scatter | solution.py:68
Sparse Core Ops, SparseCore 0:
  9.6 28.6 all-gather.1
  60.9 82.6 all-reduce.15
  148.1 51.4 all-reduce.17
  208.2 82.6 all-reduce.19
  295.1 51.7 all-reduce.21
  355.6 82.5 all-reduce.23
  442.5 51.2 all-reduce.25
  502.5 82.6 all-reduce.27
  589.4 51.2 all-reduce.29
  649.3 82.6 all-reduce.31
  747.5 41.4 all-reduce.33
  797.6 82.6 all-reduce.35
  895.7 41.4 all-reduce.37
  945.8 82.6 all-reduce.39
  1032.8 52.1 all-reduce.41
  1093.6 82.6 all-reduce.43
  1178.7 47.1 reduce-scatter.1
where the time goes:
time: 1250 us; the launch traced here: 1240 us
  waiting for transfers between devices  1050 us (84%)
  matrix products  89.7 us (7%)
  local copies, waits for them, and re-layouts  49 us (4%)
  between operations  35.5 us (3%)
    psum x8, waiting for transfers between devices, from_root(): return lax.psum(kept, axis)  648 us
    psum x7, waiting for transfers between devices, body(): summed = lax.psum(partial_value, 'cols')  335 us
    dot_general x8, matrix products, body(): jnp.dot(inverse, pivot, precision=highest, preferred_element_type=jnp.flo...  67.2 us
    reduce_scatter x1, waiting for transfers between devices, body(): share = lax.psum_scatter(running, 'cols', scatter_dimension=0, tiled=True)  44.8 us
    unnamed x11, local copies, waits for them, and re-layouts  25.6 us
  transfers between devices with their start and end apart: 17, of which 17 were waited for; matrix products, arithmetic and copies ran while one was open for 0% of the time, Pallas kernels for 0%

commit v1 on v0

v1 whole, which is shorter than its diff:
```python
import jax
import jax.numpy as jnp
from jax import lax
from jax.experimental import pallas as pl
from jax.experimental.pallas import tpu as pltpu
from jax.sharding import PartitionSpec as P

STEPS = 8
CHUNKS = 4
LINE_CHUNKS = 4
TILE = 512


def split_hi(value):
    return lax.reduce_precision(value, 8, 7)


def halves(value):
    high = value.astype(jnp.bfloat16)
    return high, (value - high.astype(jnp.float32)).astype(jnp.bfloat16)


def one_hot(index, depth):
    return (lax.broadcasted_iota(jnp.int32, (depth, index.shape[0]), 0) == index[None, :]).astype(jnp.bfloat16)


def picked(values, index):
    chosen = one_hot(index, values.shape[1])
    high = split_hi(values)
    low = split_hi(values - high)
    return (jnp.dot(high.astype(jnp.bfloat16), chosen, preferred_element_type=jnp.float32)
            + jnp.dot(low.astype(jnp.bfloat16), chosen, preferred_element_type=jnp.float32))


def dot_nt(left, right):
    return lax.dot_general(left, right, (((1,), (1,)), ((), ())), preferred_element_type=jnp.float32)


def in_vmem(value):
    return pltpu.with_memory_space_constraint(value, pltpu.VMEM)


def in_hbm(value):
    return pltpu.with_memory_space_constraint(value, pltpu.HBM)


def vmem_shape(shape, dtype):
    return pltpu.VMEM(shape, dtype)


def hbm_shape(shape, dtype):
    return pltpu.HBM(shape, dtype)


def factor_kernel(info, inverse_ref, panel_ref, *rest):
    high_ref, low_ref, inverse_high, inverse_low = rest[-4:]
    tile = pl.program_id(0)

    @pl.when(tile == 0)
    def _():
        high, low = halves(inverse_ref[...])
        inverse_high[...] = high
        inverse_low[...] = low

    @pl.when(tile <= info[1])
    def _():
        high, low = halves(panel_ref[...])
        value = (jnp.dot(inverse_high[...], high, preferred_element_type=jnp.float32)
                 + jnp.dot(inverse_low[...], high, preferred_element_type=jnp.float32)
                 + jnp.dot(inverse_high[...], low, preferred_element_type=jnp.float32))
        high, low = halves(value.T)
        high_ref[...] = high
        low_ref[...] = low


def chain_factors(info, diag_inverse, panel, tile, waited):
    block = diag_inverse.shape[1]
    depth = panel.shape[1]
    shape = vmem_shape((depth, block), jnp.bfloat16)
    return pl.pallas_call(
        factor_kernel,
        out_shape=[shape, shape],
        grid_spec=pltpu.PrefetchScalarGridSpec(
            num_scalar_prefetch=1,
            grid=(depth // tile,),
            in_specs=[
                pl.BlockSpec((block, block), lambda t, info: (info[0], 0)),
                pl.BlockSpec((block, tile), lambda t, info: (info[0], jnp.minimum(t, info[1]))),
            ] + [pl.BlockSpec(memory_space=pl.ANY)] * len(waited),
            out_specs=[pl.BlockSpec((tile, block), lambda t, info: (jnp.minimum(t, info[1]), 0))] * 2,
            scratch_shapes=[pltpu.VMEM((block, block), jnp.bfloat16)] * 2,
        ),
        compiler_params=pltpu.CompilerParams(vmem_limit_bytes=44 << 20),
        cost_estimate=pl.CostEstimate(
            flops=6 * block * block * depth, bytes_accessed=4 * block * (block + 2 * depth), transcendentals=0),
    )(info, in_hbm(diag_inverse), in_hbm(panel), *waited)


def start_kernel(info, *refs):
    shares, (place_ref, source_ref), (out_ref, inverse_ref, side, high, low, sem) = refs[:-8], refs[-8:-6], refs[-6:]
    dates, points = shares[0].shape
    lanes = high.shape[1]
    chunks, width, block = out_ref.shape
    tile = 256
    steps = block // tile

    @pl.when(info[1] == 1)
    def _():
        def inverse_rows(step):
            rows = pl.ds(pl.multiple_of(step * tile, tile), tile)
            source = pl.ds(pl.multiple_of(info[0] * block + step * tile, tile), tile)
            return pltpu.make_async_copy(source_ref.at[source], inverse_ref.at[rows], sem.at[step])

        for step in range(steps):
            inverse_rows(step).start()
        side[...] = jnp.zeros_like(side)
        for index, share in enumerate(shares):
            columns = pl.ds(index * points, points)
            first, second = halves(share[...])
            side[pl.ds(0, dates), columns] = first
            side[pl.ds(lanes, dates), columns] = second

        def order(step, carry):
            columns = pl.ds(pl.multiple_of(step * tile, tile), tile)
            places = lax.broadcasted_iota(jnp.int32, (side.shape[1], tile), 0)
            chosen = jnp.where(places == place_ref[:, columns], 1.0, 0.0).astype(jnp.bfloat16)
            both = jnp.dot(side[...], chosen, preferred_element_type=jnp.float32)
            first, second = halves((both[:lanes] + both[lanes:]).T)
            high[columns] = first
            low[columns] = second
            return carry

        def multiply(step, carry):
            rows = pl.ds(pl.multiple_of(step * tile, tile), tile)
            inverse_rows(step).wait()
            first, second = halves(inverse_ref[rows])
            value = (jnp.dot(first, high[...], preferred_element_type=jnp.float32)
                     + jnp.dot(second, high[...], preferred_element_type=jnp.float32)
                     + jnp.dot(first, low[...], preferred_element_type=jnp.float32)).T
            for chunk in range(chunks):
                out_ref[chunk, :, rows] = value[chunk * width:(chunk + 1) * width]
            return carry

        lax.fori_loop(0, steps, order, 0)
        lax.fori_loop(0, steps, multiply, 0)


def start_values(info, shares, place, diag_inverse, chunks, width, waited):
    block = diag_inverse.shape[1]
    dates, points = shares[0].shape
    lanes = -(-max(dates, chunks * width) // 128) * 128
    count = len(shares) + 2
    ordered = pltpu.VMEM((block, lanes), jnp.bfloat16)

    def kernel(info, *refs):
        start_kernel(info, *refs[:count], *refs[-6:])

    whole = pl.BlockSpec(memory_space=pltpu.VMEM)
    return pl.pallas_call(
        kernel,
        out_shape=vmem_shape((chunks, width, block), jnp.float32),
        in_specs=[pl.BlockSpec(memory_space=pltpu.SMEM)] + [whole] * (count - 1)
        + [pl.BlockSpec(memory_space=pl.ANY)] * (1 + len(waited)),
        out_specs=whole,
        scratch_shapes=[
            pltpu.VMEM((block, block), jnp.float32),
            pltpu.VMEM((2 * lanes, len(shares) * points), jnp.bfloat16),
            ordered,
            ordered,
            pltpu.SemaphoreType.DMA((block // 256,)),
        ],
        compiler_params=pltpu.CompilerParams(vmem_limit_bytes=28 << 20),
        cost_estimate=pl.CostEstimate(
            flops=10 * dates * block * block, bytes_accessed=4 * block * (block + 2 * dates), transcendentals=0),
    )(info, *map(in_vmem, shares), in_vmem(place), in_hbm(diag_inverse), *waited)


def slot_kernel(slot, chunks, sent, info, *refs):
    refs = list(refs)
    chain_ref = refs.pop(0) if sent[0] else None
    side_ref = refs.pop(0) if sent[1] else None
    up_ref = refs.pop(0) if sent[2] else None
    start_ref, start_rest_ref, high_ref, low_ref, out_ref, pair_ref, store_ref, sem = refs
    width, block = out_ref.shape
    first, second = pair_ref.at[pl.ds(0, width)], pair_ref.at[pl.ds(width, width)]
    chunk = slot - info[8]
    stored = (chunk >= 0) & (chunk < chunks)

    def keep_pair(action):
        @pl.when(stored & (info[1] == 2))
        def _():
            for stream in range(2):
                action(pltpu.make_async_copy(
                    pair_ref.at[pl.ds(stream * width, width)], store_ref.at[chunk, stream], sem.at[stream]))

    def keep_line(action):
        @pl.when(stored & (info[1] != 2))
        def _():
            action(pltpu.make_async_copy(out_ref, store_ref.at[chunk, info[9]], sem.at[0]))

    @pl.when(info[0] == 1)
    def _():
        out_ref[...] = side_ref[...] if sent[1] else jnp.zeros_like(out_ref)

    @pl.when(info[0] == 0)
    def _():
        out_ref[...] = jnp.zeros_like(out_ref)

    for code, ref in enumerate((side_ref, chain_ref, None if up_ref is None else up_ref.at[pl.ds(0, width)])):
        if ref is not None:
            @pl.when(info[1] == code)
            def _(ref=ref):
                first[...] = ref[...]
    for code, ref in enumerate((None if up_ref is None else up_ref.at[pl.ds(width, width)], chain_ref)):
        if ref is not None:
            @pl.when(info[2] == code)
            def _(ref=ref):
                second[...] = ref[...]

    keep_pair(lambda copy: copy.start())

    if any(sent):
        def step(tile, carry):
            per_stream = block // TILE
            rows = pl.ds(pl.multiple_of(tile // per_stream * width, 16), width)
            columns = pl.ds(pl.multiple_of(tile % per_stream * TILE, TILE), TILE)
            factor = pl.ds(pl.multiple_of(tile * TILE, TILE), TILE)
            high, low = halves(pair_ref[rows, columns])
            both = jnp.dot(jnp.concatenate([high, low], axis=0), high_ref[factor], preferred_element_type=jnp.float32)
            rest = jnp.dot(high, low_ref[factor], preferred_element_type=jnp.float32)
            out_ref[...] += (both[:width] + both[width:]) + rest
            return carry

        lax.fori_loop(0, info[3], step, 0)

    at = jnp.clip(slot - info[6], 0, chunks - 1)
    for code, ref in enumerate((start_ref, start_rest_ref)):
        @pl.when((info[4] == 1) & (info[10] == code))
        def _(ref=ref):
            out_ref[...] = ref[at] - out_ref[...]

    @pl.when(info[5] == 1)
    def _():
        second[...] = out_ref[...]

    if sent[1]:
        @pl.when(info[7] == 1)
        def _():
            out_ref[...] = side_ref[...]

    keep_line(lambda copy: copy.start())
    keep_line(lambda copy: copy.wait())
    keep_pair(lambda copy: copy.wait())


def advance(slot, info, received, start, start_rest, high, low, store, waited):
    chunks, width, block = start.shape
    sent = tuple(value is not None for value in received)
    operands = [in_vmem(value) for value in received if value is not None]
    operands += [in_vmem(start), in_vmem(start_rest), in_vmem(high), in_vmem(low)]
    count = len(operands)
    extra = list(waited) + ([] if store is None else [in_hbm(store)])

    def kernel(info, *refs):
        slot_kernel(slot, chunks, sent, info, *refs[:count], *refs[-4:])

    return pl.pallas_call(
        kernel,
        out_shape=[vmem_shape((width, block), jnp.float32), vmem_shape((2 * width, block), jnp.float32),
                   hbm_shape((chunks, 2, width, block), jnp.float32)],
        in_specs=[pl.BlockSpec(memory_space=pltpu.SMEM)] + [pl.BlockSpec(memory_space=pltpu.VMEM)] * count
        + [pl.BlockSpec(memory_space=pl.ANY)] * len(extra),
        out_specs=[pl.BlockSpec(memory_space=pltpu.VMEM)] * 2 + [pl.BlockSpec(memory_space=pl.ANY)],
        scratch_shapes=[pltpu.SemaphoreType.DMA((2,))],
        input_output_aliases={} if store is None else {count + len(extra): 2},
        compiler_params=pltpu.CompilerParams(vmem_limit_bytes=16 << 20),
        cost_estimate=pl.CostEstimate(
            flops=6 * width * block * high.shape[0], bytes_accessed=32 * width * block, transcendentals=0),
    )(info, *operands, *extra)


def fetch(chunk, info, store, arrays, waited):
    _, _, width, block = store.shape
    count = len(arrays)

    def kernel(info, store_ref, *refs):
        out_ref, sem = refs[-2:]

        def copies(action):
            @pl.when(info[0] == 0)
            def _():
                action(pltpu.make_async_copy(store_ref.at[chunk, info[1]], out_ref, sem))

        copies(lambda copy: copy.start())
        copies(lambda copy: copy.wait())
        for index in range(count):
            @pl.when(info[0] == index + 1)
            def _(index=index):
                out_ref[...] = refs[index][...]

    return pl.pallas_call(
        kernel,
        out_shape=vmem_shape((width, block), jnp.float32),
        in_specs=[pl.BlockSpec(memory_space=pltpu.SMEM), pl.BlockSpec(memory_space=pl.ANY)]
        + [pl.BlockSpec(memory_space=pltpu.VMEM)] * count + [pl.BlockSpec(memory_space=pl.ANY)] * len(waited),
        out_specs=pl.BlockSpec(memory_space=pltpu.VMEM),
        scratch_shapes=[pltpu.SemaphoreType.DMA],
        compiler_params=pltpu.CompilerParams(vmem_limit_bytes=16 << 20),
        cost_estimate=pl.CostEstimate(flops=0, bytes_accessed=0, transcendentals=0),
    )(info, in_hbm(store), *map(in_vmem, arrays), *waited)


def solved_shares(info, store, shares):
    chunks, _, width, block = store.shape
    size = block // shares

    def kernel(info, store_ref, *refs):
        outs, sem = refs[:-1], refs[-1]

        def copies(action):
            for chunk in range(chunks):
                for turn in range(shares):
                    columns = pl.ds(pl.multiple_of(info[1 + turn] * size, size), size)
                    action(pltpu.make_async_copy(store_ref.at[chunk, info[0], :, columns],
                                                 outs[turn].at[pl.ds(chunk * width, width)], sem.at[chunk, turn]))

        copies(lambda copy: copy.start())
        copies(lambda copy: copy.wait())

    return pl.pallas_call(
        kernel,
        out_shape=[vmem_shape((chunks * width, size), jnp.float32)] * shares,
        in_specs=[pl.BlockSpec(memory_space=pltpu.SMEM), pl.BlockSpec(memory_space=pl.ANY)],
        out_specs=[pl.BlockSpec(memory_space=pltpu.VMEM)] * shares,
        scratch_shapes=[pltpu.SemaphoreType.DMA((chunks, shares))],
        compiler_params=pltpu.CompilerParams(vmem_limit_bytes=16 << 20),
        cost_estimate=pl.CostEstimate(flops=0, bytes_accessed=0, transcendentals=0),
    )(info, in_hbm(store))


def turn_kernel(info, chunks, width, store_ref, *refs):
    lines, crossed, series_ref = refs[:chunks], refs[chunks:2 * chunks], refs[2 * chunks]
    high, low, side_high, side_low, raw, side, sem = refs[-7:]
    block = raw.shape[2]
    dates = series_ref.shape[0]
    total = chunks * width

    def copies(action):
        for chunk in range(chunks):
            rows = pl.ds(chunk * width, width)

            @pl.when(info[0] == 1)
            def _(chunk=chunk, rows=rows):
                for stream in range(2):
                    action(pltpu.make_async_copy(
                        store_ref.at[chunk, stream], raw.at[stream, rows], sem.at[2 * chunk + stream]))

            @pl.when(info[0] == 0)
            def _(chunk=chunk, rows=rows):
                action(pltpu.make_async_copy(lines[chunk], raw.at[info[1], rows], sem.at[2 * chunk]))
                action(pltpu.make_async_copy(crossed[chunk], raw.at[1 - info[1], rows], sem.at[2 * chunk + 1]))

    copies(lambda copy: copy.start())
    lanes = side.shape[0]
    side[...] = jnp.zeros_like(side)
    side[pl.ds(0, dates)] = series_ref[...]
    first, second = halves(side[...].T)
    side_high[...] = first
    side_low[...] = second
    raw[:, pl.ds(total, lanes - total)] = jnp.zeros((2, lanes - total, block), jnp.float32)
    copies(lambda copy: copy.wait())
    for stream in range(2):
        first, second = halves(raw[stream].T)
        high[pl.ds(stream * block, block)] = first
        low[pl.ds(stream * block, block)] = second


def turned(info, store, sources, series, waited):
    chunks, _, width, block = store.shape
    dates, points = series.shape
    lanes = -(-max(dates, chunks * width) // 128) * 128
    count = 2 + len(sources)

    def kernel(info, *refs):
        turn_kernel(info, chunks, width, *refs[:count], *refs[count + len(waited):])

    whole = pl.BlockSpec(memory_space=pltpu.VMEM)
    solved = vmem_shape((2 * block, lanes), jnp.bfloat16)
    side = vmem_shape((points, lanes), jnp.bfloat16)
    return pl.pallas_call(
        kernel,
        out_shape=[solved, solved, side, side],
        in_specs=[pl.BlockSpec(memory_space=pltpu.SMEM)] + [pl.BlockSpec(memory_space=pl.ANY)] * (1 + len(sources))
        + [whole] + [pl.BlockSpec(memory_space=pl.ANY)] * len(waited),
        out_specs=[whole] * 4,
        scratch_shapes=[
            pltpu.VMEM((2, lanes, block), jnp.float32),
            pltpu.VMEM((lanes, points), jnp.float32),
            pltpu.SemaphoreType.DMA((2 * chunks,)),
        ],
        compiler_params=pltpu.CompilerParams(vmem_limit_bytes=16 << 20),
        cost_estimate=pl.CostEstimate(flops=0, bytes_accessed=0, transcendentals=0),
    )(info, in_hbm(store), *sources, in_vmem(series), *waited)


def residual_kernel(info, first_tile, tiles, high, low, side_high, side_low, place_ref, panel_ref, *rest):
    out_ref, held, sem = rest[-3:]
    steps, rows = held.shape[:2]
    total = out_ref.shape[0]
    per_tile = steps // tiles

    def source_rows(step):
        start = info[2 + first_tile + step // per_tile] * (per_tile * rows) + step % per_tile * rows
        return pl.ds(pl.multiple_of(start, rows), rows)

    def panel_rows(step):
        return pltpu.make_async_copy(panel_ref.at[source_rows(step)], held.at[step], sem.at[step])

    for step in range(steps):
        panel_rows(step).start()

    def multiply(step, carry):
        panel_rows(step).wait()
        factor_high, factor_low = halves(held[step])
        product = (jnp.dot(factor_high, high[...], preferred_element_type=jnp.float32)
                   + jnp.dot(factor_high, low[...], preferred_element_type=jnp.float32)
                   + jnp.dot(factor_low, high[...], preferred_element_type=jnp.float32))
        places = lax.broadcasted_iota(jnp.int32, (rows, side_high.shape[0]), 1)
        chosen = jnp.where(places == place_ref[source_rows(step)], 1.0, 0.0).astype(jnp.bfloat16)
        value = (jnp.dot(chosen, side_high[...], preferred_element_type=jnp.float32)
                 + jnp.dot(chosen, side_low[...], preferred_element_type=jnp.float32)) - product
        out_ref[:, pl.ds(pl.multiple_of(step * rows, rows), rows)] = value.T[:total]
        return carry

    lax.fori_loop(0, steps, multiply, 0)


def residual_tiles(info, first_tile, tiles, size, total, parts, place, panel, waited):
    depth = panel.shape[1]
    rows = 256
    steps = tiles * size // rows

    def kernel(info, *refs):
        residual_kernel(info, first_tile, tiles, *refs[:6], *refs[-3:])

    whole = pl.BlockSpec(memory_space=pltpu.VMEM)
    return pl.pallas_call(
        kernel,
        out_shape=vmem_shape((total, tiles * size), jnp.float32),
        in_specs=[pl.BlockSpec(memory_space=pltpu.SMEM)] + [whole] * 5
        + [pl.BlockSpec(memory_space=pl.ANY)] * (1 + len(waited)),
        out_specs=whole,
        scratch_shapes=[pltpu.VMEM((steps, rows, depth), jnp.float32), pltpu.SemaphoreType.DMA((steps,))],
        compiler_params=pltpu.CompilerParams(vmem_limit_bytes=36 << 20),
        cost_estimate=pl.CostEstimate(
            flops=6 * total * tiles * size * depth, bytes_accessed=4 * tiles * size * depth, transcendentals=0),
    )(info, *map(in_vmem, parts), in_vmem(place), in_hbm(panel), *waited)


def add_kernel(left_ref, right_ref, out_ref):
    out_ref[...] = left_ref[...] + right_ref[:, pl.ds(0, out_ref.shape[1])]


def added(left, right):
    whole = pl.BlockSpec(memory_space=pltpu.VMEM)
    return pl.pallas_call(
        add_kernel,
        out_shape=vmem_shape(left.shape, left.dtype),
        in_specs=[whole] * 2,
        out_specs=whole,
        compiler_params=pltpu.CompilerParams(vmem_limit_bytes=16 << 20),
    )(in_vmem(left), in_vmem(right))


def make_line_body(row_count, col_count):
    levels = row_count // 2
    chunks = LINE_CHUNKS

    def flat(level, side, col):
        return (2 * level + side) * col_count + col

    def body(series, point_order, step_block, panel, diag_inverse):
        f32 = jnp.float32
        dates, own_points = series.shape
        block = diag_inverse.shape[1]
        group_rows, depth = panel.shape
        local_blocks = group_rows // block
        width = -(-dates // (16 * chunks)) * 16
        padded = width * chunks
        row = lax.axis_index("rows")
        col = lax.axis_index("cols")
        level, side = row // 2, row % 2

        def send(value, pairs):
            return lax.ppermute(value, ("rows", "cols"), pairs)

        def solver(step):
            return flat(step // 2, step % 2, max(step - 1, 0) // 2)

        def busy(start, slot):
            return 0 <= slot - start < chunks

        above, same = level > col, level == col
        second_solver = same & (side == 1)
        last = (side == 0) & (level == col + 1)
        origin = (row == 0) & (col == 0)
        is_solver = second_solver | last | origin

        shares = [series]
        for turn in range(1, col_count):
            pairs = []
            for step in range(STEPS):
                here = max(step - 1, 0) // 2
                pairs.append((flat(step // 2, step % 2, (here + turn) % col_count), flat(step // 2, step % 2, here)))
            shares.append(send(series, pairs))

        per_tile = 256
        top = levels - 1
        last_factor = jnp.where(above, depth // per_tile - 1, jnp.where(second_solver, block // per_tile - 1, 0))
        slot_index = step_block[row] % local_blocks
        local_order = point_order % group_rows
        block_order = lax.dynamic_slice(local_order, (slot_index * block,), (block,))
        place = (block_order // own_points - col) % col_count * own_points + block_order % own_points
        first_direct = 2 * top + 2
        arrived = jnp.where(origin, 0, jnp.where((col == top) & (level == top - 1), first_direct, 3 * col - level + 1))
        from_direct = (col == top) & (level < top - 1)
        stored_at = jnp.where(above, level + col + 1, jnp.where(from_direct, first_direct + 4 * chunks, arrived))
        own_place = jnp.where(local_order // own_points != col, -1, local_order % own_points)[:, None]
        def pack(*values):
            return jnp.stack([jnp.asarray(value).astype(jnp.int32) for value in values])

        factor_info = pack(slot_index, last_factor)
        start_info = pack(slot_index, origin)
        rest_info = pack(slot_index, is_solver & jnp.logical_not(origin))
        slot_info = pack(
            (above | second_solver) & (col > 0),
            jnp.where(above, 2, jnp.where(second_solver, 1, 0)),
            last,
            jnp.where(above, depth // TILE, jnp.where(second_solver, block // TILE, 0)),
            is_solver,
            second_solver,
            jnp.where(origin, 0, level + col + 1),
            jnp.logical_not(above | second_solver | origin),
            stored_at,
            side,
            jnp.logical_not(origin),
        )
        fetch_info = pack(jnp.where(from_direct, level + 1, 0), side)
        late_info = pack(jnp.where((col == top) & (level == top - 1), top, jnp.where(from_direct, level + 1, 0)), side)
        solved_info = pack(side, *[(col + turn) % col_count for turn in range(col_count)])
        residual_info = pack(above, side, col ^ 3, col ^ 1, col ^ 2, col)
        place = place[None, :]
        waited = [place, start_info, rest_info, slot_info, fetch_info, late_info, solved_info, residual_info, own_place]

        high, low = chain_factors(factor_info, diag_inverse, panel, per_tile, waited)
        start = start_values(start_info, shares, place, diag_inverse, chunks, width, [])

        chain_pairs = [(solver(step), solver(step + 1)) for step in range(STEPS - 1)]
        side_pairs = [(0, 0)]
        down_pairs, cross_pairs = [], []
        for c in range(col_count):
            for z in range(levels):
                for y in range(2):
                    if z > c:
                        side_pairs.append((flat(z, y, c), flat(z, y, c + 1)))
                        continue
                    cross_pairs.append((flat(z, y, c), flat(z, 1 - y, c)))
                    if z and (c < levels - 1 or z == c):
                        down_pairs.append((flat(z, y, c), flat(z - 1, y, c)))
        direct_pairs = [[(flat(top, y, top), flat(z, y, top)) for y in range(2)] for z in range(top)]
        late_pairs = direct_pairs[top - 1]
        mine, crossed, direct = [], [], []

        def send_direct():
            direct.append([send(out, direct_pairs[z]) for z in range(top - 1)])

        def cross(info, arrays, waited):
            mine.append(fetch(len(mine), info, store, arrays, mine[-1:] + waited))
            crossed.append(send(mine[-1], cross_pairs))

        out = pair = store = None
        start_rest = start
        last_solve = STEPS - 1 + chunks - 1
        for slot in range(last_solve + 1):
            received = [None, None, None]
            if slot:
                ups = [(flat(z, y, c), flat(z + 1, y, c)) for c in range(col_count) for z in range(c, levels - 1)
                       for y in range(2) if busy(z + c + 1, slot - 1)]
                received = [send(out, chain_pairs), send(out, side_pairs + down_pairs),
                            send(pair, ups) if ups else None]
            if slot >= first_direct:
                send_direct()
            out, pair, store = advance(slot, slot_info, received, start, start_rest, high, low, store,
                                       mine[-1:] + crossed[:-1][-1:])
            if slot == 0:
                start_rest = start_values(rest_info, shares, place, diag_inverse, chunks, width, [out])
            if slot >= first_direct:
                cross(fetch_info, direct[-1], [])

        send_direct()
        late = send(out, late_pairs)
        pieces = solved_shares(solved_info, store, col_count)
        delivered = []
        for turn in range(1, col_count):
            pairs = [(flat(z, y, z), flat(z, y, (z + turn) % col_count)) for z in range(levels) for y in range(2)]
            delivered.append(send(pieces[turn], pairs))
        cross(late_info, direct[-1] + [late], [pieces[0]])
        near = [(at * col_count + here, at * col_count + (here ^ 1))
                for at in range(row_count) for here in range(col_count)]
        far = [(at * col_count + here, at * col_count + (here ^ 2))
               for at in range(row_count) for here in range(col_count)]

        size = group_rows // col_count
        parts = turned(residual_info, store, mine + crossed, series, delivered)
        give = residual_tiles(residual_info, 0, 2, size, padded, parts, own_place, panel, [])
        moved = send(give, near)
        passed = residual_tiles(residual_info, 2, 1, size, padded, parts, own_place, panel, [give])
        passed = added(passed, moved)
        moved_far = send(passed, far)
        own = residual_tiles(residual_info, 3, 1, size, padded, parts, own_place, panel, [passed])
        solved = pieces[0]
        for turn in range(1, col_count):
            solved = jnp.where((col - level) % col_count == turn, delivered[turn - 1], solved)

        residual = ((own + moved[:, size:]) + moved_far)[:dates]
        return solved[:dates].T, residual.T

    return body


def make_body(row_count, col_count):
    base = row_count - STEPS

    def body(series, point_order, step_block, panel, diag_inverse):
        f32 = jnp.float32
        dates, own_points = series.shape
        block = diag_inverse.shape[1]
        group_rows = panel.shape[0]
        local_blocks = group_rows // block
        per = panel.shape[1] // block
        width = -(-dates // (8 * CHUNKS)) * 8
        padded = width * CHUNKS

        def column(step):
            return step // per

        solver_col = [0] + [column(step - 1) for step in range(1, STEPS)]

        def arrival(start, distance):
            if distance >= 1:
                return start + -(-distance // 2)
            return start + 1 + (-distance) // 2

        def fits(hop):
            for step in range(STEPS):
                for earlier in range(step):
                    due = hop * step - (solver_col[step] - column(earlier))
                    if arrival(hop * earlier, step - earlier) > due:
                        return False
            return True

        hop = 1
        while not fits(hop):
            hop += 1

        def flat(row, col):
            return row * col_count + col

        def busy(start, slot):
            return 0 <= slot - start < CHUNKS

        row = lax.axis_index("rows")
        col = lax.axis_index("cols")
        step_here = row - base
        has_step = step_here >= 0
        step_safe = jnp.maximum(step_here, 0)
        solver_here = jnp.where(step_safe == 0, 0, (step_safe - 1) // per)
        is_solver = has_step & (col == solver_here)

        def send(value, pairs):
            return lax.ppermute(value, ("rows", "cols"), pairs)

        first_row = step_block[step_safe] % local_blocks * block
        inverse = lax.dynamic_slice(diag_inverse, (first_row, jnp.int32(0)), (block, block))
        factor = lax.dynamic_slice(panel, (first_row, jnp.int32(0)), (block, per * block))
        chain_factor = lax.dot_general(
            factor, inverse, (((0,), (1,)), ((), ())),
            precision=lax.Precision.HIGH, preferred_element_type=f32)

        shares = [series]
        for turn in range(1, col_count):
            pairs = [
                (flat(base + step, (solver_col[step] + turn) % col_count), flat(base + step, solver_col[step]))
                for step in range(STEPS)
            ]
            shares.append(send(series, pairs))
        gathered = jnp.concatenate(shares, axis=1)
        local_order = point_order % group_rows

        block_order = lax.dynamic_slice(local_order, (first_row,), (block,))
        place = (block_order // own_points - col) % col_count * own_points + block_order % own_points
        side = picked(gathered, place)
        start_value = lax.dot_general(
            side, inverse, (((1,), (1,)), ((), ())),
            precision=lax.Precision.HIGH, preferred_element_type=f32)
        start_value = jnp.pad(start_value, ((0, padded - dates), (0, 0))).reshape(CHUNKS, width, block)

        zero = jnp.zeros((width, block), f32)
        held = [jnp.zeros((CHUNKS + 1, width, block), f32) for _ in range(per)]
        latest = [zero] * per
        outgoing = None
        streams = [col * per + index for index in range(per)]
        gaps = [step_here - stream for stream in streams]
        starts = [hop * stream for stream in streams]

        def arrival_here(start, gap):
            return jnp.where(gap >= 1, start + (gap + 1) // 2, start + 1 + (-gap) // 2)

        arrivals = [arrival_here(start, gap) for start, gap in zip(starts, gaps)]
        due = hop * step_here - (solver_here - col)

        def pick_chunk(values, chunk):
            return lax.dynamic_index_in_dim(values, jnp.clip(chunk, 0, CHUNKS - 1), 0, keepdims=False)

        last_slot = max(arrival(hop * step, place_row - base - step)
                        for step in range(STEPS) for place_row in range(row_count)) + CHUNKS - 1
        for slot in range(last_slot + 1):
            before = slot - 1
            one_up, two_up, level, one_down, added = [], [], [], [], []
            if before >= 0:
                for step in range(STEPS):
                    source = flat(base + step, solver_col[step])
                    if busy(hop * step, before):
                        if step + 1 < STEPS:
                            one_up.append((source, flat(base + step + 1, column(step))))
                        if step + 2 < STEPS:
                            two_up.append((source, flat(base + step + 2, column(step))))
                        if solver_col[step] != column(step):
                            level.append((source, flat(base + step, column(step))))
                        if base + step >= 1:
                            one_down.append((source, flat(base + step - 1, column(step))))
                    for from_col in range(solver_col[step]):
                        if busy(hop * step - (solver_col[step] - from_col), before):
                            added.append((flat(base + step, from_col), flat(base + step, from_col + 1)))
            from_one_up = send(outgoing, one_up) if one_up else zero
            incoming = send(outgoing, added) if added else zero
            from_two_up = send(outgoing, two_up) if two_up else zero
            from_level = send(outgoing, level) if level else zero
            from_one_down = send(outgoing, one_down) if one_down else zero
            received_up, received_down = [], []
            for index in range(per):
                upward, downward = [], []
                for stream in range(index, STEPS, per):
                    for at in range(row_count):
                        gap = at - base - stream
                        if busy(arrival(hop * stream, gap), before):
                            if gap >= 1 and at + 2 < row_count:
                                upward.append((flat(at, column(stream)), flat(at + 2, column(stream))))
                            if gap <= 0 and at >= 2:
                                downward.append((flat(at, column(stream)), flat(at - 2, column(stream))))
                received_up.append(send(latest[index], upward) if upward else zero)
                received_down.append(send(latest[index], downward) if downward else zero)

            inputs = []
            for index in range(per):
                gap = gaps[index]
                up = jnp.where(gap == 1, from_one_up, jnp.where(gap == 2, from_two_up, received_up[index]))
                same = jnp.where(col == solver_here, zero if outgoing is None else outgoing, from_level)
                down = jnp.where(gap == 0, same, jnp.where(gap == -1, from_one_down, received_down[index]))
                got = jnp.where(gap >= 1, up, down)
                chunk = slot - arrivals[index]
                valid = (chunk >= 0) & (chunk < CHUNKS)
                needed = slot - due
                ready = jnp.where(needed == chunk, up, pick_chunk(held[index], needed))
                inputs.append(jnp.where((gap >= 1) & has_step, ready, 0))
                held[index] = lax.dynamic_update_index_in_dim(
                    held[index], got, jnp.where(valid, chunk, CHUNKS), 0)
                latest[index] = got
            if slot <= hop * (STEPS - 1) + CHUNKS - 1:
                total = incoming + jnp.dot(
                    jnp.concatenate(inputs, axis=1), chain_factor,
                    precision=lax.Precision.HIGH, preferred_element_type=f32)
                outgoing = jnp.where(is_solver, pick_chunk(start_value, slot - due) - total, total)

        whole = [values[:CHUNKS].reshape(padded, block)[:dates] for values in held]
        out_rows = STEPS * block // (row_count * col_count)

        def wanted(at):
            return at * col_count * out_rows // block

        source_col = row * col_count * out_rows // block // per
        stream_index = row * col_count * out_rows // block % per
        chosen = whole[0]
        for index in range(1, per):
            chosen = jnp.where(stream_index == index, whole[index], chosen)

        def piece(target):
            first = (row * col_count + target) * out_rows % block
            return lax.dynamic_slice(chosen, (jnp.int32(0), first), (dates, out_rows))

        solved = piece(col)
        for turn in range(1, col_count):
            pairs = [
                (flat(at, column(wanted(at))), flat(at, (column(wanted(at)) + turn) % col_count))
                for at in range(row_count)
            ]
            moved = send(piece((col + turn) % col_count), pairs)
            solved = jnp.where((col - source_col) % col_count == turn, moved, solved)

        away = local_order // own_points != col
        own_place = jnp.where(away, -1, local_order % own_points)
        product = lax.dot_general(
            jnp.concatenate(whole, axis=1), panel, (((1,), (1,)), ((), ())),
            precision=lax.Precision.HIGH, preferred_element_type=f32)
        left = picked(series, own_place) - product
        distance = 1
        parts = left.reshape(dates, col_count, group_rows // col_count)
        pieces = [parts[:, index] for index in range(col_count)]
        while distance < col_count:
            bit = (col // distance) % 2
            keep, give = [], []
            for index in range(0, len(pieces), 2):
                keep.append(jnp.where(bit == 0, pieces[index], pieces[index + 1]))
                give.append(jnp.where(bit == 0, pieces[index + 1], pieces[index]))
            pairs = [(flat(at, here), flat(at, here ^ distance)) for at in range(row_count) for here in range(col_count)]
            moved = send(jnp.concatenate(give, axis=1) if len(give) > 1 else give[0], pairs)
            size = group_rows // col_count
            pieces = [value + moved[:, index * size:(index + 1) * size] for index, value in enumerate(keep)]
            distance *= 2
        return solved.T, pieces[0].T

    return body


def solution(mesh):
    in_specs = (P(None, ("rows", "cols")), P("rows"), P(), P("rows", "cols"), P("rows", None))
    out_specs = (P(("rows", "cols"), None), P(("rows", "cols"), None))
    row_count, col_count = mesh.shape["rows"], mesh.shape["cols"]
    lines = row_count == STEPS and 2 * col_count == STEPS
    body = (make_line_body if lines else make_body)(row_count, col_count)
    return jax.shard_map(body, mesh=mesh, in_specs=in_specs, out_specs=out_specs, check_vma=False)
```

time: 1250 us -> 288 us (0.23)
  waiting for transfers between devices: 1050 us -> 151 us
  matrix products: 89.7 us -> 0 us
  starting transfers between devices: 2.59 us -> 66.4 us
  Pallas kernels: 0 us -> 56.4 us
  local copies, waits for them, and re-layouts: 49 us -> 2.95 us
  between operations: 35.5 us -> 3.68 us
    psum x15 -> x0, waiting for transfers between devices: 983 us -> none  [the longest x8 648 us: from_root(): return lax.psum(kept, axis)]
    ppermute x0 -> x49, waiting for transfers between devices: none -> 151 us  [send(): return lax.ppermute(value, ('rows', 'cols'), pairs)]
    dot_general x10 -> x0, matrix products: 89.7 us -> none  [the longest x8 67.2 us: body(): jnp.dot(inverse, pivot, precision=highest, preferred_element_type=jnp.flo...]
    ppermute x0 -> x49, starting transfers between devices: none -> 66.4 us  [send(): return lax.ppermute(value, ('rows', 'cols'), pairs)]
    pallas_call x0 -> x24, Pallas kernels: none -> 56.4 us  [the longest x3 23.8 us: residual_tiles(): pl.pallas_call(kernel, out_shape=vmem_shape((total, tiles * size), jnp.fl...]
    reduce_scatter x1 -> x0, waiting for transfers between devices: 44.8 us -> none  [body(): share = lax.psum_scatter(running, 'cols', scatter_dimension=0, tiled=True)]
    unnamed x11 -> x16, local copies, waits for them, and re-layouts: 25.6 us -> 1.08 us
    all_gather x1 -> x0, waiting for transfers between devices: 23.2 us -> none  [body(): gathered = lax.all_gather(series, 'cols', axis=1, tiled=True)]
  transfers between devices with their start and end apart: 17 -> 49, of which waited for: 17 -> 14; matrix products, arithmetic and copies ran while one was open for 0% -> 2% of each run, Pallas kernels for 0% -> 11%
where the time goes in v1:
time: 288 us; the launch traced here: 286 us
  waiting for transfers between devices  151 us (52%)
  starting transfers between devices  66.4 us (23%)
  Pallas kernels  56.4 us (20%)
  other arithmetic  5.22 us (2%)
  between operations  3.68 us (1%)
  local copies, waits for them, and re-layouts  2.95 us (1%)
    ppermute x49, waiting for transfers between devices, send(): return lax.ppermute(value, ('rows', 'cols'), pairs)  151 us
    ppermute x49, starting transfers between devices, send(): return lax.ppermute(value, ('rows', 'cols'), pairs)  66.4 us
    pallas_call x3, Pallas kernels, residual_tiles(): pl.pallas_call(kernel, out_shape=vmem_shape((total, tiles * size), jnp.fl...  23.8 us
    pallas_call x11, Pallas kernels, advance(): pl.pallas_call(kernel, out_shape=[vmem_shape((width, block), jnp.float32)...  13.4 us
    pallas_call x4, Pallas kernels, fetch(): pl.pallas_call(kernel, out_shape=vmem_shape((width, block), jnp.float32),...  6.11 us
    pallas_call x1, Pallas kernels, chain_factors(): pl.pallas_call(factor_kernel, out_shape=[shape, shape], grid_spec=pltpu.P...  5.98 us
  transfers between devices with their start and end apart: 49, of which 14 were waited for; matrix products, arithmetic and copies ran while one was open for 2% of the time, Pallas kernels for 11%

profile of v1, /device:TPU:14, one launch (start us, length us, event | category | flops | bytes accessed | tf_op | source)
XLA Modules:
  0.0 285.6 jit_solution(690200985131376763)
XLA Ops:
  0.6 1.9 collective-permute-start
  9.0 6.0 %shard_map.69 = (bf16[2048,1024]{1,0:T(8,128)(2,1)S(1)}, bf16[2048,1024]{1,0:T(8,128)(2,1)S(1)}) custom-call(s32[2]{0:T(128)S(1)} %get-tuple-element.86.info, f32[2048,1024]{1,0:T(8,128)} %refs_5_.6, f32[2048,2048]{1,0:T(8,128)} %refs_5_.9, s32[1,1024]{1,0:T(1,128)S(1)} %bitcast.33, s32[2]{0:T(128)S(1)} %get-tuple-element.84.info.rest_1_, ...), custom_call_target="tpu_custom_call" | custom-call | flops 12884901888 | bytes 20971520 | tf_op jit(solution)/shard_map/pallas_call | solution.py:80
  15.0 1.6 collective-permute-done.refs_1_
  17.2 1.5 shard_map.70
  19.3 4.2 %collective-permute-start.4 = (f32[80,1024]{1,0:T(8,128)S(1)}, f32[80,1024]{1,0:T(8,128)S(1)}, u32[]{:S(2)}, u32[]{:S(2)}) collective-permute-start(f32[80,1024]{1,0:T(8,128)S(1)} %get-tuple-element.44.refs_6_), channel_id=1, source_target_pairs={{0,0},{8,9},{12,13},{16,17},{20,21},{24,25},{28,29},{17,18},{21,22... | collective-permute-start | bytes 983048 | tf_op jit(solution)/shard_map/ppermute | solution.py:495
  24.1 18.6 %collective-permute-done.4.refs_1_ = f32[80,1024]{1,0:T(8,128)S(1)} collective-permute-done((f32[80,1024]{1,0:T(8,128)S(1)}, f32[80,1024]{1,0:T(8,128)S(1)}, u32[]{:S(2)}, u32[]{:S(2)}) %collective-permute-start.4) | collective-permute-done | bytes 327712 | tf_op jit(solution)/shard_map/ppermute | solution.py:495
  44.9 1.9 collective-permute-start.6
  46.8 12.8 %collective-permute-done.6.refs_1_ = f32[80,1024]{1,0:T(8,128)S(1)} collective-permute-done((f32[80,1024]{1,0:T(8,128)S(1)}, f32[80,1024]{1,0:T(8,128)S(1)}, u32[]{:S(2)}, u32[]{:S(2)}) %collective-permute-start.6) | collective-permute-done | bytes 327712 | tf_op jit(solution)/shard_map/ppermute | solution.py:495
  61.8 1.9 collective-permute-start.9
  63.7 9.7 %collective-permute-done.9.refs_1_ = f32[80,1024]{1,0:T(8,128)S(1)} collective-permute-done((f32[80,1024]{1,0:T(8,128)S(1)}, f32[80,1024]{1,0:T(8,128)S(1)}, u32[]{:S(2)}, u32[]{:S(2)}) %collective-permute-start.9) | collective-permute-done | bytes 327712 | tf_op jit(solution)/shard_map/ppermute | solution.py:495
  75.6 1.9 collective-permute-start.12
  77.5 9.7 %collective-permute-done.12.refs_1_ = f32[80,1024]{1,0:T(8,128)S(1)} collective-permute-done((f32[80,1024]{1,0:T(8,128)S(1)}, f32[80,1024]{1,0:T(8,128)S(1)}, u32[]{:S(2)}, u32[]{:S(2)}) %collective-permute-start.12) | collective-permute-done | bytes 327712 | tf_op jit(solution)/shard_map/ppermute | solution.py:495
  89.3 2.1 collective-permute-start.15
  91.4 9.5 %collective-permute-done.15.refs_1_ = f32[80,1024]{1,0:T(8,128)S(1)} collective-permute-done((f32[80,1024]{1,0:T(8,128)S(1)}, f32[80,1024]{1,0:T(8,128)S(1)}, u32[]{:S(2)}, u32[]{:S(2)}) %collective-permute-start.15) | collective-permute-done | bytes 327712 | tf_op jit(solution)/shard_map/ppermute | solution.py:495
  103.1 1.9 collective-permute-start.18
  105.0 18.6 %collective-permute-done.18.refs_1_ = f32[80,1024]{1,0:T(8,128)S(1)} collective-permute-done((f32[80,1024]{1,0:T(8,128)S(1)}, f32[80,1024]{1,0:T(8,128)S(1)}, u32[]{:S(2)}, u32[]{:S(2)}) %collective-permute-start.18) | collective-permute-done | bytes 327712 | tf_op jit(solution)/shard_map/ppermute | solution.py:495
  123.6 1.5 shard_map.77
  126.4 1.9 collective-permute-start.21
  128.4 17.0 %collective-permute-done.21.refs_1_ = f32[80,1024]{1,0:T(8,128)S(1)} collective-permute-done((f32[80,1024]{1,0:T(8,128)S(1)}, f32[80,1024]{1,0:T(8,128)S(1)}, u32[]{:S(2)}, u32[]{:S(2)}) %collective-permute-start.21) | collective-permute-done | bytes 327712 | tf_op jit(solution)/shard_map/ppermute | solution.py:495
  145.4 1.4 shard_map.78
  148.2 1.9 collective-permute-start.24
  150.2 17.1 %collective-permute-done.24.refs_1_ = f32[80,1024]{1,0:T(8,128)S(1)} collective-permute-done((f32[80,1024]{1,0:T(8,128)S(1)}, f32[80,1024]{1,0:T(8,128)S(1)}, u32[]{:S(2)}, u32[]{:S(2)}) %collective-permute-start.24) | collective-permute-done | bytes 327712 | tf_op jit(solution)/shard_map/ppermute | solution.py:495
  167.3 1.5 shard_map.79
  171.5 1.9 collective-permute-start.27
  174.9 1.5 shard_map.80.refs_7_.refs_2_.refs_1_
  176.4 10.7 %collective-permute-start.35 = (f32[80,1024]{1,0:T(8,128)S(1)}, f32[80,1024]{1,0:T(8,128)S(1)}, u32[]{:S(2)}, u32[]{:S(2)}) collective-permute-start(f32[80,1024]{1,0:T(8,128)S(1)} %shard_map.80.refs_7_.refs_2_.refs_1_), channel_id=1, source_target_pairs={{0,4},{4,0},{1,5},{5,1},{9,13},{13,9},{2,6},{6,2},{10,14},{14,10},... | collective-permute-start | bytes 983048 | tf_op jit(solution)/shard_map/ppermute | solution.py:495
  187.1 3.5 %collective-permute-done.27.refs_1_ = f32[80,1024]{1,0:T(8,128)S(1)} collective-permute-done((f32[80,1024]{1,0:T(8,128)S(1)}, f32[80,1024]{1,0:T(8,128)S(1)}, u32[]{:S(2)}, u32[]{:S(2)}) %collective-permute-start.27) | collective-permute-done | bytes 327712 | tf_op jit(solution)/shard_map/ppermute | solution.py:495
  190.6 2.3 shard_map.81
  193.6 1.9 collective-permute-start.32
  196.9 1.5 shard_map.82.refs_6_.refs_2_
  198.5 18.8 %collective-permute-done.32.refs_1_ = f32[80,1024]{1,0:T(8,128)S(1)} collective-permute-done((f32[80,1024]{1,0:T(8,128)S(1)}, f32[80,1024]{1,0:T(8,128)S(1)}, u32[]{:S(2)}, u32[]{:S(2)}) %collective-permute-start.32) | collective-permute-done | bytes 327712 | tf_op jit(solution)/shard_map/ppermute | solution.py:495
  217.3 1.5 shard_map.83
  220.9 1.9 collective-permute-start.44
  222.9 2.1 shard_map.84
  225.0 1.5 shard_map.85.refs_3_
  226.5 3.9 %collective-permute-start.45 = (f32[80,1024]{1,0:T(8,128)S(1)}, f32[80,1024]{1,0:T(8,128)S(1)}, u32[]{:S(2)}, u32[]{:S(2)}) collective-permute-start(f32[80,1024]{1,0:T(8,128)S(1)} %shard_map.85.refs_3_), channel_id=1, source_target_pairs={{0,4},{4,0},{1,5},{5,1},{9,13},{13,9},{2,6},{6,2},{10,14},{14,10},... | collective-permute-start | bytes 983048 | tf_op jit(solution)/shard_map/ppermute | solution.py:495
  233.1 1.5 shard_map.86.refs_4_
  234.7 1.9 collective-permute-start.46
  236.7 3.6 %collective-permute-done.38.refs_10_ = f32[320,256]{1,0:T(8,128)S(1)} collective-permute-done((f32[320,256]{1,0:T(8,128)S(1)}, f32[320,256]{1,0:T(8,128)S(1)}, u32[]{:S(2)}, u32[]{:S(2)}) %collective-permute-start.38) | collective-permute-done | bytes 327712 | tf_op jit(solution)/shard_map/ppermute | solution.py:495
  240.2 3.4 %collective-permute-done.46.refs_8_ = f32[80,1024]{1,0:T(8,128)S(1)} collective-permute-done((f32[80,1024]{1,0:T(8,128)S(1)}, f32[80,1024]{1,0:T(8,128)S(1)}, u32[]{:S(2)}, u32[]{:S(2)}) %collective-permute-start.46) | collective-permute-done | bytes 327712 | tf_op jit(solution)/shard_map/ppermute | solution.py:495
  243.7 2.9 %shard_map.87 = (bf16[2048,384]{1,0:T(8,128)(2,1)S(1)}, bf16[2048,384]{1,0:T(8,128)(2,1)S(1)}, bf16[512,384]{1,0:T(8,128)(2,1)S(1)}, bf16[512,384]{1,0:T(8,128)(2,1)S(1)}) custom-call(s32[6]{0:T(128)S(1)} %stack.177.rest_7_.info, f32[4,2,80,1024]{3,2,1,0:T(8,128)} %get-tuple-element.72.store_ref.refs_0_, f32[80,1024]{1,0:T(8,128)S(1)} %shard_map.80.refs_7_.refs_2_.refs_1_, ...), custom_call_target="tpu_custom_call" | custom-call | tf_op jit(solution)/shard_map/pallas_call | solution.py:390
  246.6 10.8 %shard_map.88.refs_6_ = f32[320,1024]{1,0:T(8,128)S(1)} custom-call(s32[6]{0:T(128)S(1)} %stack.177.rest_7_.info, bf16[2048,384]{1,0:T(8,128)(2,1)S(1)} %get-tuple-element.78.refs_0_, bf16[2048,384]{1,0:T(8,128)(2,1)S(1)} %get-tuple-element.79.refs_1_, bf16[512,384]{1,0:T(8,128)(2,1)S(1)} %get-tuple-element.80.refs_2_, ...), custom_call_target="tpu_custom_call" | custom-call | flops 4026531840 | bytes 8388608 | tf_op jit(solution)/shard_map/pallas_call | solution.py:447
  257.5 6.5 %shard_map.89.left_ref = f32[320,512]{1,0:T(8,128)S(1)} custom-call(s32[6]{0:T(128)S(1)} %stack.177.rest_7_.info, bf16[2048,384]{1,0:T(8,128)(2,1)S(1)} %get-tuple-element.78.refs_0_, bf16[2048,384]{1,0:T(8,128)(2,1)S(1)} %get-tuple-element.79.refs_1_, bf16[512,384]{1,0:T(8,128)(2,1)S(1)} %get-tuple-element.80.refs_2_, ...), custom_call_target="tpu_custom_call" | custom-call | flops 2013265920 | bytes 4194304 | tf_op jit(solution)/shard_map/pallas_call | solution.py:447
  266.0 1.6 collective-permute-start.48
  267.6 2.2 fusion.1
  269.8 6.5 %shard_map.91 = f32[320,512]{1,0:T(8,128)S(1)} custom-call(s32[6]{0:T(128)S(1)} %stack.177.rest_7_.info, bf16[2048,384]{1,0:T(8,128)(2,1)S(1)} %get-tuple-element.78.refs_0_, bf16[2048,384]{1,0:T(8,128)(2,1)S(1)} %copy-done.1, bf16[512,384]{1,0:T(8,128)(2,1)S(1)} %get-tuple-element.80.refs_2_, bf16[512,384]{1,0:T(8,128)(2,1)S(1)} %get-tuple-element.81.refs_3_, ...), custom_call_target="tpu_custom_call" | custom-call | flops 2013265920 | bytes 4194304 | tf_op jit(solution)/shard_map/pallas_call | solution.py:447
  276.3 7.2 %collective-permute-done.48 = f32[320,512]{1,0:T(8,128)} collective-permute-done((f32[320,512]{1,0:T(8,128)}, f32[320,512]{1,0:T(8,128)}, u32[]{:S(2)}, u32[]{:S(2)}) %collective-permute-start.48) | collective-permute-done | bytes 655392 | tf_op jit(solution)/shard_map/ppermute | solution.py:495
  283.5 2.1 fusion
  (104 shorter events, 32.5 us)
Async XLA Ops:
  0.6 15.9 %collective-permute-start = (f32[300,512]{1,0:T(8,128)}, f32[300,512]{1,0:T(8,128)S(1)}, u32[]{:S(2)}, u32[]{:S(2)}) collective-permute-start(f32[300,512]{1,0:T(8,128)} %refs_9_.1), channel_id=1, source_target_pairs={{1,0},{5,4},{9,8},{14,13},{18,17},{23,22},{27,26},{28,31}} | collective-permute-start | bytes 1843208 | tf_op jit(solution)/shard_map/ppermute | solution.py:495
  2.6 14.0 %collective-permute-start.1 = (f32[300,512]{1,0:T(8,128)}, f32[300,512]{1,0:T(8,128)S(1)}, u32[]{:S(2)}, u32[]{:S(2)}) collective-permute-start(f32[300,512]{1,0:T(8,128)} %refs_9_.1), channel_id=1, source_target_pairs={{2,0},{6,4},{10,8},{15,13},{19,17},{20,22},{24,26},{29,31}} | collective-permute-start | bytes 1843208 | tf_op jit(solution)/shard_map/ppermute | solution.py:495
  3.3 13.3 %collective-permute-start.2 = (f32[300,512]{1,0:T(8,128)}, f32[300,512]{1,0:T(8,128)S(1)}, u32[]{:S(2)}, u32[]{:S(2)}) collective-permute-start(f32[300,512]{1,0:T(8,128)} %refs_9_.1), channel_id=1, source_target_pairs={{3,0},{7,4},{11,8},{12,13},{16,17},{21,22},{25,26},{30,31}} | collective-permute-start | bytes 1843208 | tf_op jit(solution)/shard_map/ppermute | solution.py:495
  18.6 5.5 %collective-permute-start.3 = (f32[80,1024]{1,0:T(8,128)S(1)}, f32[80,1024]{1,0:T(8,128)S(1)}, u32[]{:S(2)}, u32[]{:S(2)}) collective-permute-start(f32[80,1024]{1,0:T(8,128)S(1)} %get-tuple-element.44.refs_6_), channel_id=1, source_target_pairs={{0,4},{4,8},{8,13},{13,17},{17,22},{22,26},{26,31}} | collective-permute-start | bytes 983048 | tf_op jit(solution)/shard_map/ppermute | solution.py:495
  19.3 23.4 %collective-permute-start.4 = (f32[80,1024]{1,0:T(8,128)S(1)}, f32[80,1024]{1,0:T(8,128)S(1)}, u32[]{:S(2)}, u32[]{:S(2)}) collective-permute-start(f32[80,1024]{1,0:T(8,128)S(1)} %get-tuple-element.44.refs_6_), channel_id=1, source_target_pairs={{0,0},{8,9},{12,13},{16,17},{20,21},{24,25},{28,29},{17,18},{21,22... | collective-permute-start | bytes 983048 | tf_op jit(solution)/shard_map/ppermute | solution.py:495
  43.5 16.2 %collective-permute-start.7 = (f32[160,1024]{1,0:T(8,128)S(1)}, f32[160,1024]{1,0:T(8,128)S(1)}, u32[]{:S(2)}, u32[]{:S(2)}) collective-permute-start(f32[160,1024]{1,0:T(8,128)S(1)} %get-tuple-element.47), channel_id=1, source_target_pairs={{0,8},{4,12}} | collective-permute-start | bytes 1966088 | tf_op jit(solution)/shard_map/ppermute | solution.py:495
  44.2 2.6 collective-permute-start.5
  44.9 14.8 %collective-permute-start.6 = (f32[80,1024]{1,0:T(8,128)S(1)}, f32[80,1024]{1,0:T(8,128)S(1)}, u32[]{:S(2)}, u32[]{:S(2)}) collective-permute-start(f32[80,1024]{1,0:T(8,128)S(1)} %get-tuple-element.46), channel_id=1, source_target_pairs={{0,0},{8,9},{12,13},{16,17},{20,21},{24,25},{28,29},{17,18},{21,22... | collective-permute-start | bytes 983048 | tf_op jit(solution)/shard_map/ppermute | solution.py:495
  60.4 13.0 %collective-permute-start.10 = (f32[160,1024]{1,0:T(8,128)S(1)}, f32[160,1024]{1,0:T(8,128)S(1)}, u32[]{:S(2)}, u32[]{:S(2)}) collective-permute-start(f32[160,1024]{1,0:T(8,128)S(1)} %get-tuple-element.50), channel_id=1, source_target_pairs={{0,8},{4,12},{8,16},{12,20}} | collective-permute-start | bytes 1966088 | tf_op jit(solution)/shard_map/ppermute | solution.py:495
  61.1 2.6 collective-permute-start.8
  61.8 11.6 %collective-permute-start.9 = (f32[80,1024]{1,0:T(8,128)S(1)}, f32[80,1024]{1,0:T(8,128)S(1)}, u32[]{:S(2)}, u32[]{:S(2)}) collective-permute-start(f32[80,1024]{1,0:T(8,128)S(1)} %get-tuple-element.49), channel_id=1, source_target_pairs={{0,0},{8,9},{12,13},{16,17},{20,21},{24,25},{28,29},{17,18},{21,22... | collective-permute-start | bytes 983048 | tf_op jit(solution)/shard_map/ppermute | solution.py:495
  74.2 13.0 %collective-permute-start.13 = (f32[160,1024]{1,0:T(8,128)S(1)}, f32[160,1024]{1,0:T(8,128)S(1)}, u32[]{:S(2)}, u32[]{:S(2)}) collective-permute-start(f32[160,1024]{1,0:T(8,128)S(1)} %get-tuple-element.53), channel_id=1, source_target_pairs={{0,8},{4,12},{8,16},{12,20},{16,24},{20,28},{9,17},{13,21}} | collective-permute-start | bytes 1966088 | tf_op jit(solution)/shard_map/ppermute | solution.py:495
  74.9 2.6 collective-permute-start.11
  75.6 11.6 %collective-permute-start.12 = (f32[80,1024]{1,0:T(8,128)S(1)}, f32[80,1024]{1,0:T(8,128)S(1)}, u32[]{:S(2)}, u32[]{:S(2)}) collective-permute-start(f32[80,1024]{1,0:T(8,128)S(1)} %get-tuple-element.52), channel_id=1, source_target_pairs={{0,0},{8,9},{12,13},{16,17},{20,21},{24,25},{28,29},{17,18},{21,22... | collective-permute-start | bytes 983048 | tf_op jit(solution)/shard_map/ppermute | solution.py:495
  87.9 13.0 %collective-permute-start.16 = (f32[160,1024]{1,0:T(8,128)S(1)}, f32[160,1024]{1,0:T(8,128)S(1)}, u32[]{:S(2)}, u32[]{:S(2)}) collective-permute-start(f32[160,1024]{1,0:T(8,128)S(1)} %get-tuple-element.56), channel_id=1, source_target_pairs={{0,8},{4,12},{8,16},{12,20},{16,24},{20,28},{9,17},{13,21},{17,25}... | collective-permute-start | bytes 1966088 | tf_op jit(solution)/shard_map/ppermute | solution.py:495
  88.6 2.8 collective-permute-start.14
  89.3 11.6 %collective-permute-start.15 = (f32[80,1024]{1,0:T(8,128)S(1)}, f32[80,1024]{1,0:T(8,128)S(1)}, u32[]{:S(2)}, u32[]{:S(2)}) collective-permute-start(f32[80,1024]{1,0:T(8,128)S(1)} %get-tuple-element.55), channel_id=1, source_target_pairs={{0,0},{8,9},{12,13},{16,17},{20,21},{24,25},{28,29},{17,18},{21,22... | collective-permute-start | bytes 983048 | tf_op jit(solution)/shard_map/ppermute | solution.py:495
  101.7 21.9 %collective-permute-start.19 = (f32[160,1024]{1,0:T(8,128)S(1)}, f32[160,1024]{1,0:T(8,128)S(1)}, u32[]{:S(2)}, u32[]{:S(2)}) collective-permute-start(f32[160,1024]{1,0:T(8,128)S(1)} %get-tuple-element.59), channel_id=1, source_target_pairs={{8,16},{12,20},{16,24},{20,28},{9,17},{13,21},{17,25},{21,29},{18,... | collective-permute-start | bytes 1966088 | tf_op jit(solution)/shard_map/ppermute | solution.py:495
  102.4 2.6 collective-permute-start.17
  103.1 20.5 %collective-permute-start.18 = (f32[80,1024]{1,0:T(8,128)S(1)}, f32[80,1024]{1,0:T(8,128)S(1)}, u32[]{:S(2)}, u32[]{:S(2)}) collective-permute-start(f32[80,1024]{1,0:T(8,128)S(1)} %get-tuple-element.58), channel_id=1, source_target_pairs={{0,0},{8,9},{12,13},{16,17},{20,21},{24,25},{28,29},{17,18},{21,22... | collective-permute-start | bytes 983048 | tf_op jit(solution)/shard_map/ppermute | solution.py:495
  125.0 20.3 %collective-permute-start.22 = (f32[160,1024]{1,0:T(8,128)S(1)}, f32[160,1024]{1,0:T(8,128)S(1)}, u32[]{:S(2)}, u32[]{:S(2)}) collective-permute-start(f32[160,1024]{1,0:T(8,128)S(1)} %get-tuple-element.62), channel_id=1, source_target_pairs={{16,24},{20,28},{9,17},{13,21},{17,25},{21,29},{18,26},{22,30}} | collective-permute-start | bytes 1966088 | tf_op jit(solution)/shard_map/ppermute | solution.py:495
  125.8 2.6 collective-permute-start.20
  126.4 18.9 %collective-permute-start.21 = (f32[80,1024]{1,0:T(8,128)S(1)}, f32[80,1024]{1,0:T(8,128)S(1)}, u32[]{:S(2)}, u32[]{:S(2)}) collective-permute-start(f32[80,1024]{1,0:T(8,128)S(1)} %get-tuple-element.61), channel_id=1, source_target_pairs={{0,0},{8,9},{12,13},{16,17},{20,21},{24,25},{28,29},{17,18},{21,22... | collective-permute-start | bytes 983048 | tf_op jit(solution)/shard_map/ppermute | solution.py:495
  146.8 20.4 %collective-permute-start.25 = (f32[160,1024]{1,0:T(8,128)S(1)}, f32[160,1024]{1,0:T(8,128)S(1)}, u32[]{:S(2)}, u32[]{:S(2)}) collective-permute-start(f32[160,1024]{1,0:T(8,128)S(1)} %get-tuple-element.65), channel_id=1, source_target_pairs={{17,25},{21,29},{18,26},{22,30}} | collective-permute-start | bytes 1966088 | tf_op jit(solution)/shard_map/ppermute | solution.py:495
  148.2 19.0 %collective-permute-start.24 = (f32[80,1024]{1,0:T(8,128)S(1)}, f32[80,1024]{1,0:T(8,128)S(1)}, u32[]{:S(2)}, u32[]{:S(2)}) collective-permute-start(f32[80,1024]{1,0:T(8,128)S(1)} %get-tuple-element.64), channel_id=1, source_target_pairs={{0,0},{8,9},{12,13},{16,17},{20,21},{24,25},{28,29},{17,18},{21,22... | collective-permute-start | bytes 983048 | tf_op jit(solution)/shard_map/ppermute | solution.py:495
  168.8 21.9 %collective-permute-start.28 = (f32[160,1024]{1,0:T(8,128)S(1)}, f32[160,1024]{1,0:T(8,128)S(1)}, u32[]{:S(2)}, u32[]{:S(2)}) collective-permute-start(f32[160,1024]{1,0:T(8,128)S(1)} %get-tuple-element.68), channel_id=1, source_target_pairs={{18,26},{22,30}} | collective-permute-start | bytes 1966088 | tf_op jit(solution)/shard_map/ppermute | solution.py:495
  169.5 4.0 %collective-permute-start.29 = (f32[80,1024]{1,0:T(8,128)S(1)}, f32[80,1024]{1,0:T(8,128)S(1)}, u32[]{:S(2)}, u32[]{:S(2)}) collective-permute-start(f32[80,1024]{1,0:T(8,128)S(1)} %get-tuple-element.64), channel_id=1, source_target_pairs={{27,3},{31,7}} | collective-permute-start | bytes 983048 | tf_op jit(solution)/shard_map/ppermute | solution.py:495
  170.2 4.0 %collective-permute-start.30 = (f32[80,1024]{1,0:T(8,128)S(1)}, f32[80,1024]{1,0:T(8,128)S(1)}, u32[]{:S(2)}, u32[]{:S(2)}) collective-permute-start(f32[80,1024]{1,0:T(8,128)S(1)} %get-tuple-element.64), channel_id=1, source_target_pairs={{27,11},{31,15}} | collective-permute-start | bytes 983048 | tf_op jit(solution)/shard_map/ppermute | solution.py:495
  170.8 5.6 %collective-permute-start.26 = (f32[80,1024]{1,0:T(8,128)S(1)}, f32[80,1024]{1,0:T(8,128)S(1)}, u32[]{:S(2)}, u32[]{:S(2)}) collective-permute-start(f32[80,1024]{1,0:T(8,128)S(1)} %get-tuple-element.67), channel_id=1, source_target_pairs={{0,4},{4,8},{8,13},{13,17},{17,22},{22,26},{26,31}} | collective-permute-start | bytes 983048 | tf_op jit(solution)/shard_map/ppermute | solution.py:495
  171.5 19.1 %collective-permute-start.27 = (f32[80,1024]{1,0:T(8,128)S(1)}, f32[80,1024]{1,0:T(8,128)S(1)}, u32[]{:S(2)}, u32[]{:S(2)}) collective-permute-start(f32[80,1024]{1,0:T(8,128)S(1)} %get-tuple-element.67), channel_id=1, source_target_pairs={{0,0},{8,9},{12,13},{16,17},{20,21},{24,25},{28,29},{17,18},{21,22... | collective-permute-start | bytes 983048 | tf_op jit(solution)/shard_map/ppermute | solution.py:495
  173.5 22.1 %collective-permute-start.33 = (f32[80,1024]{1,0:T(8,128)S(1)}, f32[80,1024]{1,0:T(8,128)S(1)}, u32[]{:S(2)}, u32[]{:S(2)}) collective-permute-start(f32[80,1024]{1,0:T(8,128)S(1)} %get-tuple-element.67), channel_id=1, source_target_pairs={{27,3},{31,7}} | collective-permute-start | bytes 983048 | tf_op jit(solution)/shard_map/ppermute | solution.py:495
  174.2 22.1 %collective-permute-start.34 = (f32[80,1024]{1,0:T(8,128)S(1)}, f32[80,1024]{1,0:T(8,128)S(1)}, u32[]{:S(2)}, u32[]{:S(2)}) collective-permute-start(f32[80,1024]{1,0:T(8,128)S(1)} %get-tuple-element.67), channel_id=1, source_target_pairs={{27,11},{31,15}} | collective-permute-start | bytes 983048 | tf_op jit(solution)/shard_map/ppermute | solution.py:495
  176.4 22.1 %collective-permute-start.35 = (f32[80,1024]{1,0:T(8,128)S(1)}, f32[80,1024]{1,0:T(8,128)S(1)}, u32[]{:S(2)}, u32[]{:S(2)}) collective-permute-start(f32[80,1024]{1,0:T(8,128)S(1)} %shard_map.80.refs_7_.refs_2_.refs_1_), channel_id=1, source_target_pairs={{0,4},{4,0},{1,5},{5,1},{9,13},{13,9},{2,6},{6,2},{10,14},{14,10},... | collective-permute-start | bytes 983048 | tf_op jit(solution)/shard_map/ppermute | solution.py:495
  192.9 5.6 %collective-permute-start.31 = (f32[80,1024]{1,0:T(8,128)S(1)}, f32[80,1024]{1,0:T(8,128)S(1)}, u32[]{:S(2)}, u32[]{:S(2)}) collective-permute-start(f32[80,1024]{1,0:T(8,128)S(1)} %get-tuple-element.70), channel_id=1, source_target_pairs={{0,4},{4,8},{8,13},{13,17},{17,22},{22,26},{26,31}} | collective-permute-start | bytes 983048 | tf_op jit(solution)/shard_map/ppermute | solution.py:495
  193.6 23.7 %collective-permute-start.32 = (f32[80,1024]{1,0:T(8,128)S(1)}, f32[80,1024]{1,0:T(8,128)S(1)}, u32[]{:S(2)}, u32[]{:S(2)}) collective-permute-start(f32[80,1024]{1,0:T(8,128)S(1)} %get-tuple-element.70), channel_id=1, source_target_pairs={{0,0},{8,9},{12,13},{16,17},{20,21},{24,25},{28,29},{17,18},{21,22... | collective-permute-start | bytes 983048 | tf_op jit(solution)/shard_map/ppermute | solution.py:495
  195.6 25.4 %collective-permute-start.39 = (f32[80,1024]{1,0:T(8,128)S(1)}, f32[80,1024]{1,0:T(8,128)S(1)}, u32[]{:S(2)}, u32[]{:S(2)}) collective-permute-start(f32[80,1024]{1,0:T(8,128)S(1)} %get-tuple-element.70), channel_id=1, source_target_pairs={{27,3},{31,7}} | collective-permute-start | bytes 983048 | tf_op jit(solution)/shard_map/ppermute | solution.py:495
  196.3 28.7 %collective-permute-start.40 = (f32[80,1024]{1,0:T(8,128)S(1)}, f32[80,1024]{1,0:T(8,128)S(1)}, u32[]{:S(2)}, u32[]{:S(2)}) collective-permute-start(f32[80,1024]{1,0:T(8,128)S(1)} %get-tuple-element.70), channel_id=1, source_target_pairs={{27,11},{31,15}} | collective-permute-start | bytes 983048 | tf_op jit(solution)/shard_map/ppermute | solution.py:495
  218.9 11.6 %collective-permute-start.41 = (f32[80,1024]{1,0:T(8,128)S(1)}, f32[80,1024]{1,0:T(8,128)S(1)}, u32[]{:S(2)}, u32[]{:S(2)}) collective-permute-start(f32[80,1024]{1,0:T(8,128)S(1)} %get-tuple-element.77), channel_id=1, source_target_pairs={{27,3},{31,7}} | collective-permute-start | bytes 983048 | tf_op jit(solution)/shard_map/ppermute | solution.py:495
  219.6 11.6 %collective-permute-start.42 = (f32[80,1024]{1,0:T(8,128)S(1)}, f32[80,1024]{1,0:T(8,128)S(1)}, u32[]{:S(2)}, u32[]{:S(2)}) collective-permute-start(f32[80,1024]{1,0:T(8,128)S(1)} %get-tuple-element.77), channel_id=1, source_target_pairs={{27,11},{31,15}} | collective-permute-start | bytes 983048 | tf_op jit(solution)/shard_map/ppermute | solution.py:495
  220.2 11.6 %collective-permute-start.43 = (f32[80,1024]{1,0:T(8,128)S(1)}, f32[80,1024]{1,0:T(8,128)S(1)}, u32[]{:S(2)}, u32[]{:S(2)}) collective-permute-start(f32[80,1024]{1,0:T(8,128)S(1)} %get-tuple-element.77), channel_id=1, source_target_pairs={{27,19},{31,23}} | collective-permute-start | bytes 983048 | tf_op jit(solution)/shard_map/ppermute | solution.py:495
  220.9 13.7 %collective-permute-start.44 = (f32[80,1024]{1,0:T(8,128)S(1)}, f32[80,1024]{1,0:T(8,128)S(1)}, u32[]{:S(2)}, u32[]{:S(2)}) collective-permute-start(f32[80,1024]{1,0:T(8,128)S(1)} %shard_map.82.refs_6_.refs_2_), channel_id=1, source_target_pairs={{0,4},{4,0},{1,5},{5,1},{9,13},{13,9},{2,6},{6,2},{10,14},{14,10},... | collective-permute-start | bytes 983048 | tf_op jit(solution)/shard_map/ppermute | solution.py:495
  226.5 10.1 %collective-permute-start.45 = (f32[80,1024]{1,0:T(8,128)S(1)}, f32[80,1024]{1,0:T(8,128)S(1)}, u32[]{:S(2)}, u32[]{:S(2)}) collective-permute-start(f32[80,1024]{1,0:T(8,128)S(1)} %shard_map.85.refs_3_), channel_id=1, source_target_pairs={{0,4},{4,0},{1,5},{5,1},{9,13},{13,9},{2,6},{6,2},{10,14},{14,10},... | collective-permute-start | bytes 983048 | tf_op jit(solution)/shard_map/ppermute | solution.py:495
  230.4 6.2 %collective-permute-start.36 = (f32[320,256]{1,0:T(8,128)S(1)}, f32[320,256]{1,0:T(8,128)S(1)}, u32[]{:S(2)}, u32[]{:S(2)}) collective-permute-start(f32[320,256]{1,0:T(8,128)S(1)} %get-tuple-element.73), channel_id=1, source_target_pairs={{0,3},{4,7},{9,8},{13,12},{18,17},{22,21},{27,26},{31,30}} | collective-permute-start | bytes 983048 | tf_op jit(solution)/shard_map/ppermute | solution.py:495
  231.1 5.5 %collective-permute-start.37 = (f32[320,256]{1,0:T(8,128)S(1)}, f32[320,256]{1,0:T(8,128)S(1)}, u32[]{:S(2)}, u32[]{:S(2)}) collective-permute-start(f32[320,256]{1,0:T(8,128)S(1)} %get-tuple-element.74), channel_id=1, source_target_pairs={{0,2},{4,6},{9,11},{13,15},{18,16},{22,20},{27,25},{31,29}} | collective-permute-start | bytes 983048 | tf_op jit(solution)/shard_map/ppermute | solution.py:495
  231.8 8.4 %collective-permute-start.38 = (f32[320,256]{1,0:T(8,128)S(1)}, f32[320,256]{1,0:T(8,128)S(1)}, u32[]{:S(2)}, u32[]{:S(2)}) collective-permute-start(f32[320,256]{1,0:T(8,128)S(1)} %get-tuple-element.75), channel_id=1, source_target_pairs={{0,1},{4,5},{9,10},{13,14},{18,19},{22,23},{27,24},{31,28}} | collective-permute-start | bytes 983048 | tf_op jit(solution)/shard_map/ppermute | solution.py:495
  234.7 9.0 %collective-permute-start.46 = (f32[80,1024]{1,0:T(8,128)S(1)}, f32[80,1024]{1,0:T(8,128)S(1)}, u32[]{:S(2)}, u32[]{:S(2)}) collective-permute-start(f32[80,1024]{1,0:T(8,128)S(1)} %shard_map.86.refs_4_), channel_id=1, source_target_pairs={{0,4},{4,0},{1,5},{5,1},{9,13},{13,9},{2,6},{6,2},{10,14},{14,10},... | collective-permute-start | bytes 983048 | tf_op jit(solution)/shard_map/ppermute | solution.py:495
  257.5 6.6 %collective-permute-start.47 = (f32[320,1024]{1,0:T(8,128)S(1)}, f32[320,1024]{1,0:T(8,128)S(1)}, u32[]{:S(2)}, u32[]{:S(2)}) collective-permute-start(f32[320,1024]{1,0:T(8,128)S(1)} %shard_map.88.refs_6_), channel_id=1, source_target_pairs={{0,1},{1,0},{2,3},{3,2},{4,5},{5,4},{6,7},{7,6},{8,9},{9,8},{10,11... | collective-permute-start | bytes 3932168 | tf_op jit(solution)/shard_map/ppermute | solution.py:495
  266.0 17.4 %collective-permute-start.48 = (f32[320,512]{1,0:T(8,128)}, f32[320,512]{1,0:T(8,128)}, u32[]{:S(2)}, u32[]{:S(2)}) collective-permute-start(f32[320,512]{1,0:T(8,128)} %shard_map.90.refs_6_), channel_id=1, source_target_pairs={{0,2},{1,3},{2,0},{3,1},{4,6},{5,7},{6,4},{7,5},{8,10},{9,11},{10,... | collective-permute-start | bytes 1966088 | tf_op jit(solution)/shard_map/ppermute | solution.py:495
  (10 other events, 73.9 us)

commit v2 on v1

--- a/solution.py
+++ b/solution.py
@@ -279,35 +279,42 @@
     )(info, *operands, *extra)
 
 
-def fetch(chunk, info, store, arrays, waited):
+def fetch(first_chunk, info, store, arrays, waited):
     _, _, width, block = store.shape
-    count = len(arrays)
+    counts = [len(group) for group in arrays]
+    flat_arrays = [array for group in arrays for array in group]
 
     def kernel(info, store_ref, *refs):
         out_ref, sem = refs[-2:]
 
         def copies(action):
-            @pl.when(info[0] == 0)
-            def _():
-                action(pltpu.make_async_copy(store_ref.at[chunk, info[1]], out_ref, sem))
+            for index in range(len(arrays)):
+                @pl.when(info[1 + index] == 0)
+                def _(index=index):
+                    action(pltpu.make_async_copy(store_ref.at[first_chunk + index, info[0]],
+                                                 out_ref.at[pl.ds(index * width, width)], sem.at[index]))
 
         copies(lambda copy: copy.start())
+        left = list(refs[:len(flat_arrays)])
+        for index, count in enumerate(counts):
+            for place in range(count):
+                ref = left.pop(0)
+
+                @pl.when(info[1 + index] == place + 1)
+                def _(index=index, ref=ref):
+                    out_ref[pl.ds(index * width, width)] = ref[...]
         copies(lambda copy: copy.wait())
-        for index in range(count):
-            @pl.when(info[0] == index + 1)
-            def _(index=index):
-                out_ref[...] = refs[index][...]
 
     return pl.pallas_call(
         kernel,
-        out_shape=vmem_shape((width, block), jnp.float32),
+        out_shape=vmem_shape((len(arrays) * width, block), jnp.float32),
         in_specs=[pl.BlockSpec(memory_space=pltpu.SMEM), pl.BlockSpec(memory_space=pl.ANY)]
-        + [pl.BlockSpec(memory_space=pltpu.VMEM)] * count + [pl.BlockSpec(memory_space=pl.ANY)] * len(waited),
+        + [pl.BlockSpec(memory_space=pltpu.VMEM)] * len(flat_arrays) + [pl.BlockSpec(memory_space=pl.ANY)] * len(waited),
         out_specs=pl.BlockSpec(memory_space=pltpu.VMEM),
-        scratch_shapes=[pltpu.SemaphoreType.DMA],
+        scratch_shapes=[pltpu.SemaphoreType.DMA((len(arrays),))],
         compiler_params=pltpu.CompilerParams(vmem_limit_bytes=16 << 20),
         cost_estimate=pl.CostEstimate(flops=0, bytes_accessed=0, transcendentals=0),
-    )(info, in_hbm(store), *map(in_vmem, arrays), *waited)
+    )(info, in_hbm(store), *map(in_vmem, flat_arrays), *waited)
 
 
 def solved_shares(info, store, shares):
@@ -339,8 +346,9 @@
 
 
 def turn_kernel(info, chunks, width, store_ref, *refs):
-    lines, crossed, series_ref = refs[:chunks], refs[chunks:2 * chunks], refs[2 * chunks]
-    high, low, side_high, side_low, raw, side, sem = refs[-7:]
+    pairs = chunks // 2
+    lines, crossed, series_ref = refs[:pairs], refs[pairs:2 * pairs], refs[2 * pairs]
+    both, side_high, side_low, raw, side, sem = refs[-6:]
     block = raw.shape[2]
     dates = series_ref.shape[0]
     total = chunks * width
@@ -355,10 +363,13 @@
                     action(pltpu.make_async_copy(
                         store_ref.at[chunk, stream], raw.at[stream, rows], sem.at[2 * chunk + stream]))
 
+        for pair in range(pairs):
+            rows = pl.ds(2 * pair * width, 2 * width)
+
             @pl.when(info[0] == 0)
-            def _(chunk=chunk, rows=rows):
-                action(pltpu.make_async_copy(lines[chunk], raw.at[info[1], rows], sem.at[2 * chunk]))
-                action(pltpu.make_async_copy(crossed[chunk], raw.at[1 - info[1], rows], sem.at[2 * chunk + 1]))
+            def _(pair=pair, rows=rows):
+                action(pltpu.make_async_copy(lines[pair], raw.at[info[1], rows], sem.at[2 * pair]))
+                action(pltpu.make_async_copy(crossed[pair], raw.at[1 - info[1], rows], sem.at[2 * pair + 1]))
 
     copies(lambda copy: copy.start())
     lanes = side.shape[0]
@@ -371,8 +382,8 @@
     copies(lambda copy: copy.wait())
     for stream in range(2):
         first, second = halves(raw[stream].T)
-        high[pl.ds(stream * block, block)] = first
-        low[pl.ds(stream * block, block)] = second
+        both[pl.ds(stream * block, block), pl.ds(0, lanes)] = first
+        both[pl.ds(stream * block, block), pl.ds(lanes, lanes)] = second
 
 
 def turned(info, store, sources, series, waited):
@@ -385,14 +396,14 @@
         turn_kernel(info, chunks, width, *refs[:count], *refs[count + len(waited):])
 
     whole = pl.BlockSpec(memory_space=pltpu.VMEM)
-    solved = vmem_shape((2 * block, lanes), jnp.bfloat16)
+    solved = vmem_shape((2 * block, 2 * lanes), jnp.bfloat16)
     side = vmem_shape((points, lanes), jnp.bfloat16)
     return pl.pallas_call(
         kernel,
-        out_shape=[solved, solved, side, side],
+        out_shape=[solved, side, side],
         in_specs=[pl.BlockSpec(memory_space=pltpu.SMEM)] + [pl.BlockSpec(memory_space=pl.ANY)] * (1 + len(sources))
         + [whole] + [pl.BlockSpec(memory_space=pl.ANY)] * len(waited),
-        out_specs=[whole] * 4,
+        out_specs=[whole] * 3,
         scratch_shapes=[
             pltpu.VMEM((2, lanes, block), jnp.float32),
             pltpu.VMEM((lanes, points), jnp.float32),
@@ -403,7 +414,7 @@
     )(info, in_hbm(store), *sources, in_vmem(series), *waited)
 
 
-def residual_kernel(info, first_tile, tiles, high, low, side_high, side_low, place_ref, panel_ref, *rest):
+def residual_kernel(info, first_tile, tiles, both, side_high, side_low, place_ref, panel_ref, *rest):
     out_ref, held, sem = rest[-3:]
     steps, rows = held.shape[:2]
     total = out_ref.shape[0]
@@ -422,9 +433,10 @@
     def multiply(step, carry):
         panel_rows(step).wait()
         factor_high, factor_low = halves(held[step])
-        product = (jnp.dot(factor_high, high[...], preferred_element_type=jnp.float32)
-                   + jnp.dot(factor_high, low[...], preferred_element_type=jnp.float32)
-                   + jnp.dot(factor_low, high[...], preferred_element_type=jnp.float32))
+        lanes = side_high.shape[1]
+        wide = jnp.dot(factor_high, both[...], preferred_element_type=jnp.float32)
+        product = ((wide[:, :lanes] + wide[:, lanes:])
+                   + jnp.dot(factor_low, both[:, pl.ds(0, lanes)], preferred_element_type=jnp.float32))
         places = lax.broadcasted_iota(jnp.int32, (rows, side_high.shape[0]), 1)
         chosen = jnp.where(places == place_ref[source_rows(step)], 1.0, 0.0).astype(jnp.bfloat16)
         value = (jnp.dot(chosen, side_high[...], preferred_element_type=jnp.float32)
@@ -441,13 +453,13 @@
     steps = tiles * size // rows
 
     def kernel(info, *refs):
-        residual_kernel(info, first_tile, tiles, *refs[:6], *refs[-3:])
+        residual_kernel(info, first_tile, tiles, *refs[:5], *refs[-3:])
 
     whole = pl.BlockSpec(memory_space=pltpu.VMEM)
     return pl.pallas_call(
         kernel,
         out_shape=vmem_shape((total, tiles * size), jnp.float32),
-        in_specs=[pl.BlockSpec(memory_space=pltpu.SMEM)] + [whole] * 5
+        in_specs=[pl.BlockSpec(memory_space=pltpu.SMEM)] + [whole] * 4
         + [pl.BlockSpec(memory_space=pl.ANY)] * (1 + len(waited)),
         out_specs=whole,
         scratch_shapes=[pltpu.VMEM((steps, rows, depth), jnp.float32), pltpu.SemaphoreType.DMA((steps,))],
@@ -545,8 +557,9 @@
             side,
             jnp.logical_not(origin),
         )
-        fetch_info = pack(jnp.where(from_direct, level + 1, 0), side)
-        late_info = pack(jnp.where((col == top) & (level == top - 1), top, jnp.where(from_direct, level + 1, 0)), side)
+        usual = jnp.where(from_direct, level + 1, 0)
+        fetch_info = pack(side, usual, usual)
+        late_info = pack(side, usual, jnp.where((col == top) & (level == top - 1), top, usual))
         solved_info = pack(side, *[(col + turn) % col_count for turn in range(col_count)])
         residual_info = pack(above, side, col ^ 3, col ^ 1, col ^ 2, col)
         place = place[None, :]
@@ -575,7 +588,7 @@
             direct.append([send(out, direct_pairs[z]) for z in range(top - 1)])
 
         def cross(info, arrays, waited):
-            mine.append(fetch(len(mine), info, store, arrays, mine[-1:] + waited))
+            mine.append(fetch(2 * len(mine), info, store, arrays, mine[-1:] + waited))
             crossed.append(send(mine[-1], cross_pairs))
 
         out = pair = store = None
@@ -591,11 +604,11 @@
             if slot >= first_direct:
                 send_direct()
             out, pair, store = advance(slot, slot_info, received, start, start_rest, high, low, store,
-                                       mine[-1:] + crossed[:-1][-1:])
+                                       mine[-1:] + (direct[-2] if len(direct) > 1 else []))
             if slot == 0:
                 start_rest = start_values(rest_info, shares, place, diag_inverse, chunks, width, [out])
-            if slot >= first_direct:
-                cross(fetch_info, direct[-1], [])
+            if slot == first_direct + 1:
+                cross(fetch_info, direct, [])
 
         send_direct()
         late = send(out, late_pairs)
@@ -604,7 +617,7 @@
         for turn in range(1, col_count):
             pairs = [(flat(z, y, z), flat(z, y, (z + turn) % col_count)) for z in range(levels) for y in range(2)]
             delivered.append(send(pieces[turn], pairs))
-        cross(late_info, direct[-1] + [late], [pieces[0]])
+        cross(late_info, [direct[-2], direct[-1] + [late]], [pieces[0]])
         near = [(at * col_count + here, at * col_count + (here ^ 1))
                 for at in range(row_count) for here in range(col_count)]
         far = [(at * col_count + here, at * col_count + (here ^ 2))
@@ -612,17 +625,21 @@
 
         size = group_rows // col_count
         parts = turned(residual_info, store, mine + crossed, series, delivered)
-        give = residual_tiles(residual_info, 0, 2, size, padded, parts, own_place, panel, [])
+        def share(tile, waited):
+            return residual_tiles(residual_info, tile, 1, size, padded, parts, own_place, panel, waited)
+
+        first_give = share(0, [])
+        moved_first = send(first_give, near)
+        passed = added(share(2, [first_give]), moved_first)
+        moved_far = send(passed, far)
+        give = share(1, [passed])
         moved = send(give, near)
-        passed = residual_tiles(residual_info, 2, 1, size, padded, parts, own_place, panel, [give])
-        passed = added(passed, moved)
-        moved_far = send(passed, far)
-        own = residual_tiles(residual_info, 3, 1, size, padded, parts, own_place, panel, [passed])
+        own = share(3, [give, moved_far])
         solved = pieces[0]
         for turn in range(1, col_count):
             solved = jnp.where((col - level) % col_count == turn, delivered[turn - 1], solved)
 
-        residual = ((own + moved[:, size:]) + moved_far)[:dates]
+        residual = ((own + moved) + moved_far)[:dates]
         return solved[:dates].T, residual.T
 
     return body

time: 288 us -> 286 us (level)
  starting transfers between devices: 66.4 us -> 52.8 us
  waiting for transfers between devices: 151 us -> 164 us
    ppermute x49 -> x48, starting transfers between devices: 66.4 us -> 52.8 us  [send(): return lax.ppermute(value, ('rows', 'cols'), pairs)]
    ppermute x49 -> x48, waiting for transfers between devices: 151 us -> 164 us  [send(): return lax.ppermute(value, ('rows', 'cols'), pairs)]
    pallas_call x5 -> x3, Pallas kernels: 9 us -> 6.13 us  [the longest x2 3.27 us: fetch(): pl.pallas_call(kernel, out_shape=vmem_shape((len(arrays) * width, block),...]
    pallas_call x3 -> x4, Pallas kernels: 23.8 us -> 24.6 us  [residual_tiles(): pl.pallas_call(kernel, out_shape=vmem_shape((total, tiles * size), jnp.fl...]
  transfers between devices with their start and end apart: 49 -> 48, of which waited for: 14 -> 15; matrix products, arithmetic and copies ran while one was open for 2% -> 2% of each run, Pallas kernels for 11% -> 12%
where the time goes in v2:
time: 286 us; the launch traced here: 284 us
  waiting for transfers between devices  164 us (57%)
  Pallas kernels  54.3 us (19%)
  starting transfers between devices  52.8 us (18%)
  other arithmetic  5.36 us (2%)
  local copies, waits for them, and re-layouts  4.12 us (1%)
  between operations  3.6 us (1%)
    ppermute x48, waiting for transfers between devices, send(): return lax.ppermute(value, ('rows', 'cols'), pairs)  164 us
    ppermute x48, starting transfers between devices, send(): return lax.ppermute(value, ('rows', 'cols'), pairs)  52.8 us
    pallas_call x4, Pallas kernels, residual_tiles(): pl.pallas_call(kernel, out_shape=vmem_shape((total, tiles * size), jnp.fl...  24.6 us
    pallas_call x11, Pallas kernels, advance(): pl.pallas_call(kernel, out_shape=[vmem_shape((width, block), jnp.float32)...  13.4 us
    pallas_call x1, Pallas kernels, chain_factors(): pl.pallas_call(factor_kernel, out_shape=[shape, shape], grid_spec=pltpu.P...  5.98 us
  transfers between devices with their start and end apart: 48, of which 15 were waited for; matrix products, arithmetic and copies ran while one was open for 2% of the time, Pallas kernels for 12%

profile of v2, /device:TPU:14, one launch (start us, length us, event | category | flops | bytes accessed | tf_op | source)
XLA Modules:
  0.0 284.4 jit_solution(6693133665244065253)
XLA Ops:
  0.6 1.9 collective-permute-start
  4.0 1.2 dynamic_slice.6
  9.0 6.0 %shard_map.69 = (bf16[2048,1024]{1,0:T(8,128)(2,1)S(1)}, bf16[2048,1024]{1,0:T(8,128)(2,1)S(1)}) custom-call(s32[2]{0:T(128)S(1)} %pad_add_fusion.1.info, f32[2048,1024]{1,0:T(8,128)} %refs_5_.4, f32[2048,2048]{1,0:T(8,128)} %refs_4_.7, s32[1,1024]{1,0:T(1,128)S(1)} %bitcast.33, s32[2]{0:T(128)S(1)} %get-tuple-element.82.info.rest_1_, ...), custom_call_target="tpu_custom_call" | custom-call | flops 12884901888 | bytes 20971520 | tf_op jit(solution)/shard_map/pallas_call | solution.py:80
  15.0 1.5 collective-permute-done.refs_1_
  17.2 1.5 shard_map.70
  19.3 4.2 %collective-permute-start.4 = (f32[80,1024]{1,0:T(8,128)S(1)}, f32[80,1024]{1,0:T(8,128)S(1)}, u32[]{:S(2)}, u32[]{:S(2)}) collective-permute-start(f32[80,1024]{1,0:T(8,128)S(1)} %get-tuple-element.43.refs_6_), channel_id=1, source_target_pairs={{0,0},{8,9},{12,13},{16,17},{20,21},{24,25},{28,29},{17,18},{21,22... | collective-permute-start | bytes 983048 | tf_op jit(solution)/shard_map/ppermute | solution.py:507
  24.2 18.7 %collective-permute-done.4.refs_1_ = f32[80,1024]{1,0:T(8,128)S(1)} collective-permute-done((f32[80,1024]{1,0:T(8,128)S(1)}, f32[80,1024]{1,0:T(8,128)S(1)}, u32[]{:S(2)}, u32[]{:S(2)}) %collective-permute-start.4) | collective-permute-done | bytes 327712 | tf_op jit(solution)/shard_map/ppermute | solution.py:507
  44.9 1.9 collective-permute-start.6
  46.9 12.8 %collective-permute-done.6.refs_1_ = f32[80,1024]{1,0:T(8,128)S(1)} collective-permute-done((f32[80,1024]{1,0:T(8,128)S(1)}, f32[80,1024]{1,0:T(8,128)S(1)}, u32[]{:S(2)}, u32[]{:S(2)}) %collective-permute-start.6) | collective-permute-done | bytes 327712 | tf_op jit(solution)/shard_map/ppermute | solution.py:507
  61.9 1.9 collective-permute-start.9
  63.8 9.7 %collective-permute-done.9.refs_1_ = f32[80,1024]{1,0:T(8,128)S(1)} collective-permute-done((f32[80,1024]{1,0:T(8,128)S(1)}, f32[80,1024]{1,0:T(8,128)S(1)}, u32[]{:S(2)}, u32[]{:S(2)}) %collective-permute-start.9) | collective-permute-done | bytes 327712 | tf_op jit(solution)/shard_map/ppermute | solution.py:507
  75.6 1.9 collective-permute-start.12
  77.6 9.7 %collective-permute-done.12.refs_1_ = f32[80,1024]{1,0:T(8,128)S(1)} collective-permute-done((f32[80,1024]{1,0:T(8,128)S(1)}, f32[80,1024]{1,0:T(8,128)S(1)}, u32[]{:S(2)}, u32[]{:S(2)}) %collective-permute-start.12) | collective-permute-done | bytes 327712 | tf_op jit(solution)/shard_map/ppermute | solution.py:507
  89.4 2.1 collective-permute-start.15
  91.5 9.7 %collective-permute-done.15.refs_1_ = f32[80,1024]{1,0:T(8,128)S(1)} collective-permute-done((f32[80,1024]{1,0:T(8,128)S(1)}, f32[80,1024]{1,0:T(8,128)S(1)}, u32[]{:S(2)}, u32[]{:S(2)}) %collective-permute-start.15) | collective-permute-done | bytes 327712 | tf_op jit(solution)/shard_map/ppermute | solution.py:507
  103.3 1.9 collective-permute-start.18
  105.2 18.4 %collective-permute-done.18.refs_1_ = f32[80,1024]{1,0:T(8,128)S(1)} collective-permute-done((f32[80,1024]{1,0:T(8,128)S(1)}, f32[80,1024]{1,0:T(8,128)S(1)}, u32[]{:S(2)}, u32[]{:S(2)}) %collective-permute-start.18) | collective-permute-done | bytes 327712 | tf_op jit(solution)/shard_map/ppermute | solution.py:507
  123.6 1.5 shard_map.77
  126.5 1.9 collective-permute-start.21
  128.4 17.0 %collective-permute-done.21.refs_1_ = f32[80,1024]{1,0:T(8,128)S(1)} collective-permute-done((f32[80,1024]{1,0:T(8,128)S(1)}, f32[80,1024]{1,0:T(8,128)S(1)}, u32[]{:S(2)}, u32[]{:S(2)}) %collective-permute-start.21) | collective-permute-done | bytes 327712 | tf_op jit(solution)/shard_map/ppermute | solution.py:507
  145.4 1.5 shard_map.78
  148.3 1.9 collective-permute-start.24
  150.2 17.1 %collective-permute-done.24.refs_1_ = f32[80,1024]{1,0:T(8,128)S(1)} collective-permute-done((f32[80,1024]{1,0:T(8,128)S(1)}, f32[80,1024]{1,0:T(8,128)S(1)}, u32[]{:S(2)}, u32[]{:S(2)}) %collective-permute-start.24) | collective-permute-done | bytes 327712 | tf_op jit(solution)/shard_map/ppermute | solution.py:507
  167.3 1.5 shard_map.79
  171.6 1.9 collective-permute-start.27
  174.9 15.8 %collective-permute-done.27.refs_1_ = f32[80,1024]{1,0:T(8,128)S(1)} collective-permute-done((f32[80,1024]{1,0:T(8,128)S(1)}, f32[80,1024]{1,0:T(8,128)S(1)}, u32[]{:S(2)}, u32[]{:S(2)}) %collective-permute-start.27) | collective-permute-done | bytes 327712 | tf_op jit(solution)/shard_map/ppermute | solution.py:507
  190.7 2.3 shard_map.80
  193.7 1.9 collective-permute-start.32
  197.0 1.6 shard_map.81.refs_6_.refs_5_.refs_1_
  198.7 9.8 %collective-permute-done.32.refs_1_ = f32[80,1024]{1,0:T(8,128)S(1)} collective-permute-done((f32[80,1024]{1,0:T(8,128)S(1)}, f32[80,1024]{1,0:T(8,128)S(1)}, u32[]{:S(2)}, u32[]{:S(2)}) %collective-permute-start.32) | collective-permute-done | bytes 327712 | tf_op jit(solution)/shard_map/ppermute | solution.py:507
  208.4 1.6 shard_map.82
  212.1 2.1 shard_map.83
  214.2 1.9 collective-permute-start.43
  216.1 1.6 shard_map.84.refs_2_
  217.8 3.9 %collective-permute-start.44 = (f32[160,1024]{1,0:T(8,128)S(1)}, f32[160,1024]{1,0:T(8,128)S(1)}, u32[]{:S(2)}, u32[]{:S(2)}) collective-permute-start(f32[160,1024]{1,0:T(8,128)S(1)} %shard_map.84.refs_2_), channel_id=1, source_target_pairs={{0,4},{4,0},{1,5},{5,1},{9,13},{13,9},{2,6},{6,2},{10,14},{14,10},... | collective-permute-start | bytes 1966088 | tf_op jit(solution)/shard_map/ppermute | solution.py:507
  223.1 1.4 collective-permute-start.37
  224.6 7.1 %collective-permute-done.37.refs_6_ = f32[320,256]{1,0:T(8,128)S(1)} collective-permute-done((f32[320,256]{1,0:T(8,128)S(1)}, f32[320,256]{1,0:T(8,128)S(1)}, u32[]{:S(2)}, u32[]{:S(2)}) %collective-permute-start.37) | collective-permute-done | bytes 327712 | tf_op jit(solution)/shard_map/ppermute | solution.py:507
  231.6 1.0 collective-permute-done.43.refs_3_
  232.6 8.1 %collective-permute-done.44.refs_4_ = f32[160,1024]{1,0:T(8,128)S(1)} collective-permute-done((f32[160,1024]{1,0:T(8,128)S(1)}, f32[160,1024]{1,0:T(8,128)S(1)}, u32[]{:S(2)}, u32[]{:S(2)}) %collective-permute-start.44) | collective-permute-done | bytes 655392 | tf_op jit(solution)/shard_map/ppermute | solution.py:507
  240.7 2.9 %shard_map.85 = (bf16[2048,768]{1,0:T(8,128)(2,1)S(1)}, bf16[512,384]{1,0:T(8,128)(2,1)S(1)}, bf16[512,384]{1,0:T(8,128)(2,1)S(1)}) custom-call(s32[6]{0:T(128)S(1)} %stack.179.rest_7_.info, f32[4,2,80,1024]{3,2,1,0:T(8,128)} %get-tuple-element.71.store_ref.refs_0_, f32[160,1024]{1,0:T(8,128)S(1)} %shard_map.81.refs_6_.refs_5_.refs_1_, ...), custom_call_target="tpu_custom_call" | custom-call | tf_op jit(solution)/shard_map/pallas_call | solution.py:401
  243.6 6.0 %shard_map.86.refs_5_ = f32[320,512]{1,0:T(8,128)S(1)} custom-call(s32[6]{0:T(128)S(1)} %stack.179.rest_7_.info, bf16[2048,768]{1,0:T(8,128)(2,1)S(1)} %get-tuple-element.77.refs_0_, bf16[512,384]{1,0:T(8,128)(2,1)S(1)} %get-tuple-element.78.refs_1_, bf16[512,384]{1,0:T(8,128)(2,1)S(1)} %get-tuple-element.79.refs_2_, s32[2048,1]{1,0:T(8,128)S(1)} %copy-done.1, ...), custom_call_target="tpu_custom_call" | custom-call | flops 2013265920 | bytes 4194304 | tf_op jit(solution)/shard_map/pallas_call | solution.py:459
  249.6 6.0 %shard_map.87.left_ref = f32[320,512]{1,0:T(8,128)S(1)} custom-call(s32[6]{0:T(128)S(1)} %stack.179.rest_7_.info, bf16[2048,768]{1,0:T(8,128)(2,1)S(1)} %get-tuple-element.77.refs_0_, bf16[512,384]{1,0:T(8,128)(2,1)S(1)} %get-tuple-element.78.refs_1_, bf16[512,384]{1,0:T(8,128)(2,1)S(1)} %get-tuple-element.79.refs_2_, s32[2048,1]{1,0:T(8,128)S(1)} %copy-done.1, ...), custom_call_target="tpu_custom_call" | custom-call | flops 2013265920 | bytes 4194304 | tf_op jit(solution)/shard_map/pallas_call | solution.py:459
  256.5 6.8 %shard_map.89.refs_5_ = f32[320,512]{1,0:T(8,128)} custom-call(s32[6]{0:T(128)S(1)} %stack.179.rest_7_.info, bf16[2048,768]{1,0:T(8,128)(2,1)S(1)} %get-tuple-element.77.refs_0_, bf16[512,384]{1,0:T(8,128)(2,1)S(1)} %get-tuple-element.78.refs_1_, bf16[512,384]{1,0:T(8,128)(2,1)S(1)} %get-tuple-element.79.refs_2_, s32[2048,1]{1,0:T(8,128)S(1)} %copy-done.1, ...), custom_call_target="tpu_custom_call" | custom-call | flops 2013265920 | bytes 4194304 | tf_op jit(solution)/shard_map/pallas_call | solution.py:459
  263.9 2.0 fusion.1
  265.9 8.0 %collective-permute-done.46.refs_6_ = f32[320,512]{1,0:T(8,128)} collective-permute-done((f32[320,512]{1,0:T(8,128)}, f32[320,512]{1,0:T(8,128)}, u32[]{:S(2)}, u32[]{:S(2)}) %collective-permute-start.46) | collective-permute-done | bytes 655392 | tf_op jit(solution)/shard_map/ppermute | solution.py:507
  274.0 1.2 copy-done.2
  276.2 5.9 %shard_map.90 = f32[320,512]{1,0:T(8,128)S(1)} custom-call(s32[6]{0:T(128)S(1)} %stack.179.rest_7_.info, bf16[2048,768]{1,0:T(8,128)(2,1)S(1)} %get-tuple-element.77.refs_0_, bf16[512,384]{1,0:T(8,128)(2,1)S(1)} %get-tuple-element.78.refs_1_, bf16[512,384]{1,0:T(8,128)(2,1)S(1)} %copy-done.4, s32[2048,1]{1,0:T(8,128)S(1)} %copy-done.2, ...), custom_call_target="tpu_custom_call" | custom-call | flops 2013265920 | bytes 4194304 | tf_op jit(solution)/shard_map/pallas_call | solution.py:459
  282.2 2.3 fusion
  (104 shorter events, 30.5 us)
Async XLA Ops:
  0.6 15.9 %collective-permute-start = (f32[300,512]{1,0:T(8,128)}, f32[300,512]{1,0:T(8,128)S(1)}, u32[]{:S(2)}, u32[]{:S(2)}) collective-permute-start(f32[300,512]{1,0:T(8,128)} %refs_5_.5), channel_id=1, source_target_pairs={{1,0},{5,4},{9,8},{14,13},{18,17},{23,22},{27,26},{28,31}} | collective-permute-start | bytes 1843208 | tf_op jit(solution)/shard_map/ppermute | solution.py:507
  2.6 14.0 %collective-permute-start.1 = (f32[300,512]{1,0:T(8,128)}, f32[300,512]{1,0:T(8,128)S(1)}, u32[]{:S(2)}, u32[]{:S(2)}) collective-permute-start(f32[300,512]{1,0:T(8,128)} %refs_5_.5), channel_id=1, source_target_pairs={{2,0},{6,4},{10,8},{15,13},{19,17},{20,22},{24,26},{29,31}} | collective-permute-start | bytes 1843208 | tf_op jit(solution)/shard_map/ppermute | solution.py:507
  3.3 13.3 %collective-permute-start.2 = (f32[300,512]{1,0:T(8,128)}, f32[300,512]{1,0:T(8,128)S(1)}, u32[]{:S(2)}, u32[]{:S(2)}) collective-permute-start(f32[300,512]{1,0:T(8,128)} %refs_5_.5), channel_id=1, source_target_pairs={{3,0},{7,4},{11,8},{12,13},{16,17},{21,22},{25,26},{30,31}} | collective-permute-start | bytes 1843208 | tf_op jit(solution)/shard_map/ppermute | solution.py:507
  18.6 5.5 %collective-permute-start.3 = (f32[80,1024]{1,0:T(8,128)S(1)}, f32[80,1024]{1,0:T(8,128)S(1)}, u32[]{:S(2)}, u32[]{:S(2)}) collective-permute-start(f32[80,1024]{1,0:T(8,128)S(1)} %get-tuple-element.43.refs_6_), channel_id=1, source_target_pairs={{0,4},{4,8},{8,13},{13,17},{17,22},{22,26},{26,31}} | collective-permute-start | bytes 983048 | tf_op jit(solution)/shard_map/ppermute | solution.py:507
  19.3 23.5 %collective-permute-start.4 = (f32[80,1024]{1,0:T(8,128)S(1)}, f32[80,1024]{1,0:T(8,128)S(1)}, u32[]{:S(2)}, u32[]{:S(2)}) collective-permute-start(f32[80,1024]{1,0:T(8,128)S(1)} %get-tuple-element.43.refs_6_), channel_id=1, source_target_pairs={{0,0},{8,9},{12,13},{16,17},{20,21},{24,25},{28,29},{17,18},{21,22... | collective-permute-start | bytes 983048 | tf_op jit(solution)/shard_map/ppermute | solution.py:507
  43.5 16.2 %collective-permute-start.7 = (f32[160,1024]{1,0:T(8,128)S(1)}, f32[160,1024]{1,0:T(8,128)S(1)}, u32[]{:S(2)}, u32[]{:S(2)}) collective-permute-start(f32[160,1024]{1,0:T(8,128)S(1)} %get-tuple-element.46), channel_id=1, source_target_pairs={{0,8},{4,12}} | collective-permute-start | bytes 1966088 | tf_op jit(solution)/shard_map/ppermute | solution.py:507
  44.2 2.6 collective-permute-start.5
  44.9 14.8 %collective-permute-start.6 = (f32[80,1024]{1,0:T(8,128)S(1)}, f32[80,1024]{1,0:T(8,128)S(1)}, u32[]{:S(2)}, u32[]{:S(2)}) collective-permute-start(f32[80,1024]{1,0:T(8,128)S(1)} %get-tuple-element.45), channel_id=1, source_target_pairs={{0,0},{8,9},{12,13},{16,17},{20,21},{24,25},{28,29},{17,18},{21,22... | collective-permute-start | bytes 983048 | tf_op jit(solution)/shard_map/ppermute | solution.py:507
  60.5 13.0 %collective-permute-start.10 = (f32[160,1024]{1,0:T(8,128)S(1)}, f32[160,1024]{1,0:T(8,128)S(1)}, u32[]{:S(2)}, u32[]{:S(2)}) collective-permute-start(f32[160,1024]{1,0:T(8,128)S(1)} %get-tuple-element.49), channel_id=1, source_target_pairs={{0,8},{4,12},{8,16},{12,20}} | collective-permute-start | bytes 1966088 | tf_op jit(solution)/shard_map/ppermute | solution.py:507
  61.2 2.6 collective-permute-start.8
  61.9 11.6 %collective-permute-start.9 = (f32[80,1024]{1,0:T(8,128)S(1)}, f32[80,1024]{1,0:T(8,128)S(1)}, u32[]{:S(2)}, u32[]{:S(2)}) collective-permute-start(f32[80,1024]{1,0:T(8,128)S(1)} %get-tuple-element.48), channel_id=1, source_target_pairs={{0,0},{8,9},{12,13},{16,17},{20,21},{24,25},{28,29},{17,18},{21,22... | collective-permute-start | bytes 983048 | tf_op jit(solution)/shard_map/ppermute | solution.py:507
  74.2 13.0 %collective-permute-start.13 = (f32[160,1024]{1,0:T(8,128)S(1)}, f32[160,1024]{1,0:T(8,128)S(1)}, u32[]{:S(2)}, u32[]{:S(2)}) collective-permute-start(f32[160,1024]{1,0:T(8,128)S(1)} %get-tuple-element.52), channel_id=1, source_target_pairs={{0,8},{4,12},{8,16},{12,20},{16,24},{20,28},{9,17},{13,21}} | collective-permute-start | bytes 1966088 | tf_op jit(solution)/shard_map/ppermute | solution.py:507
  74.9 2.6 collective-permute-start.11
  75.6 11.6 %collective-permute-start.12 = (f32[80,1024]{1,0:T(8,128)S(1)}, f32[80,1024]{1,0:T(8,128)S(1)}, u32[]{:S(2)}, u32[]{:S(2)}) collective-permute-start(f32[80,1024]{1,0:T(8,128)S(1)} %get-tuple-element.51), channel_id=1, source_target_pairs={{0,0},{8,9},{12,13},{16,17},{20,21},{24,25},{28,29},{17,18},{21,22... | collective-permute-start | bytes 983048 | tf_op jit(solution)/shard_map/ppermute | solution.py:507
  88.0 13.2 %collective-permute-start.16 = (f32[160,1024]{1,0:T(8,128)S(1)}, f32[160,1024]{1,0:T(8,128)S(1)}, u32[]{:S(2)}, u32[]{:S(2)}) collective-permute-start(f32[160,1024]{1,0:T(8,128)S(1)} %get-tuple-element.55), channel_id=1, source_target_pairs={{0,8},{4,12},{8,16},{12,20},{16,24},{20,28},{9,17},{13,21},{17,25}... | collective-permute-start | bytes 1966088 | tf_op jit(solution)/shard_map/ppermute | solution.py:507
  88.7 2.8 collective-permute-start.14
  89.4 11.8 %collective-permute-start.15 = (f32[80,1024]{1,0:T(8,128)S(1)}, f32[80,1024]{1,0:T(8,128)S(1)}, u32[]{:S(2)}, u32[]{:S(2)}) collective-permute-start(f32[80,1024]{1,0:T(8,128)S(1)} %get-tuple-element.54), channel_id=1, source_target_pairs={{0,0},{8,9},{12,13},{16,17},{20,21},{24,25},{28,29},{17,18},{21,22... | collective-permute-start | bytes 983048 | tf_op jit(solution)/shard_map/ppermute | solution.py:507
  101.9 21.7 %collective-permute-start.19 = (f32[160,1024]{1,0:T(8,128)S(1)}, f32[160,1024]{1,0:T(8,128)S(1)}, u32[]{:S(2)}, u32[]{:S(2)}) collective-permute-start(f32[160,1024]{1,0:T(8,128)S(1)} %get-tuple-element.58), channel_id=1, source_target_pairs={{8,16},{12,20},{16,24},{20,28},{9,17},{13,21},{17,25},{21,29},{18,... | collective-permute-start | bytes 1966088 | tf_op jit(solution)/shard_map/ppermute | solution.py:507
  102.6 2.6 collective-permute-start.17
  103.3 20.3 %collective-permute-start.18 = (f32[80,1024]{1,0:T(8,128)S(1)}, f32[80,1024]{1,0:T(8,128)S(1)}, u32[]{:S(2)}, u32[]{:S(2)}) collective-permute-start(f32[80,1024]{1,0:T(8,128)S(1)} %get-tuple-element.57), channel_id=1, source_target_pairs={{0,0},{8,9},{12,13},{16,17},{20,21},{24,25},{28,29},{17,18},{21,22... | collective-permute-start | bytes 983048 | tf_op jit(solution)/shard_map/ppermute | solution.py:507
  125.1 20.4 %collective-permute-start.22 = (f32[160,1024]{1,0:T(8,128)S(1)}, f32[160,1024]{1,0:T(8,128)S(1)}, u32[]{:S(2)}, u32[]{:S(2)}) collective-permute-start(f32[160,1024]{1,0:T(8,128)S(1)} %get-tuple-element.61), channel_id=1, source_target_pairs={{16,24},{20,28},{9,17},{13,21},{17,25},{21,29},{18,26},{22,30}} | collective-permute-start | bytes 1966088 | tf_op jit(solution)/shard_map/ppermute | solution.py:507
  125.8 2.6 collective-permute-start.20
  126.5 19.0 %collective-permute-start.21 = (f32[80,1024]{1,0:T(8,128)S(1)}, f32[80,1024]{1,0:T(8,128)S(1)}, u32[]{:S(2)}, u32[]{:S(2)}) collective-permute-start(f32[80,1024]{1,0:T(8,128)S(1)} %get-tuple-element.60), channel_id=1, source_target_pairs={{0,0},{8,9},{12,13},{16,17},{20,21},{24,25},{28,29},{17,18},{21,22... | collective-permute-start | bytes 983048 | tf_op jit(solution)/shard_map/ppermute | solution.py:507
  146.9 20.4 %collective-permute-start.25 = (f32[160,1024]{1,0:T(8,128)S(1)}, f32[160,1024]{1,0:T(8,128)S(1)}, u32[]{:S(2)}, u32[]{:S(2)}) collective-permute-start(f32[160,1024]{1,0:T(8,128)S(1)} %get-tuple-element.64), channel_id=1, source_target_pairs={{17,25},{21,29},{18,26},{22,30}} | collective-permute-start | bytes 1966088 | tf_op jit(solution)/shard_map/ppermute | solution.py:507
  147.6 2.6 collective-permute-start.23
  148.3 19.0 %collective-permute-start.24 = (f32[80,1024]{1,0:T(8,128)S(1)}, f32[80,1024]{1,0:T(8,128)S(1)}, u32[]{:S(2)}, u32[]{:S(2)}) collective-permute-start(f32[80,1024]{1,0:T(8,128)S(1)} %get-tuple-element.63), channel_id=1, source_target_pairs={{0,0},{8,9},{12,13},{16,17},{20,21},{24,25},{28,29},{17,18},{21,22... | collective-permute-start | bytes 983048 | tf_op jit(solution)/shard_map/ppermute | solution.py:507
  168.8 21.9 %collective-permute-start.28 = (f32[160,1024]{1,0:T(8,128)S(1)}, f32[160,1024]{1,0:T(8,128)S(1)}, u32[]{:S(2)}, u32[]{:S(2)}) collective-permute-start(f32[160,1024]{1,0:T(8,128)S(1)} %get-tuple-element.67), channel_id=1, source_target_pairs={{18,26},{22,30}} | collective-permute-start | bytes 1966088 | tf_op jit(solution)/shard_map/ppermute | solution.py:507
  169.5 4.0 %collective-permute-start.29 = (f32[80,1024]{1,0:T(8,128)S(1)}, f32[80,1024]{1,0:T(8,128)S(1)}, u32[]{:S(2)}, u32[]{:S(2)}) collective-permute-start(f32[80,1024]{1,0:T(8,128)S(1)} %get-tuple-element.63), channel_id=1, source_target_pairs={{27,3},{31,7}} | collective-permute-start | bytes 983048 | tf_op jit(solution)/shard_map/ppermute | solution.py:507
  170.2 4.0 %collective-permute-start.30 = (f32[80,1024]{1,0:T(8,128)S(1)}, f32[80,1024]{1,0:T(8,128)S(1)}, u32[]{:S(2)}, u32[]{:S(2)}) collective-permute-start(f32[80,1024]{1,0:T(8,128)S(1)} %get-tuple-element.63), channel_id=1, source_target_pairs={{27,11},{31,15}} | collective-permute-start | bytes 983048 | tf_op jit(solution)/shard_map/ppermute | solution.py:507
  170.9 4.0 %collective-permute-start.26 = (f32[80,1024]{1,0:T(8,128)S(1)}, f32[80,1024]{1,0:T(8,128)S(1)}, u32[]{:S(2)}, u32[]{:S(2)}) collective-permute-start(f32[80,1024]{1,0:T(8,128)S(1)} %get-tuple-element.66), channel_id=1, source_target_pairs={{0,4},{4,8},{8,13},{13,17},{17,22},{22,26},{26,31}} | collective-permute-start | bytes 983048 | tf_op jit(solution)/shard_map/ppermute | solution.py:507
  171.6 19.1 %collective-permute-start.27 = (f32[80,1024]{1,0:T(8,128)S(1)}, f32[80,1024]{1,0:T(8,128)S(1)}, u32[]{:S(2)}, u32[]{:S(2)}) collective-permute-start(f32[80,1024]{1,0:T(8,128)S(1)} %get-tuple-element.66), channel_id=1, source_target_pairs={{0,0},{8,9},{12,13},{16,17},{20,21},{24,25},{28,29},{17,18},{21,22... | collective-permute-start | bytes 983048 | tf_op jit(solution)/shard_map/ppermute | solution.py:507
  173.5 22.8 %collective-permute-start.33 = (f32[80,1024]{1,0:T(8,128)S(1)}, f32[80,1024]{1,0:T(8,128)S(1)}, u32[]{:S(2)}, u32[]{:S(2)}) collective-permute-start(f32[80,1024]{1,0:T(8,128)S(1)} %get-tuple-element.66), channel_id=1, source_target_pairs={{27,3},{31,7}} | collective-permute-start | bytes 983048 | tf_op jit(solution)/shard_map/ppermute | solution.py:507
  174.2 22.8 %collective-permute-start.34 = (f32[80,1024]{1,0:T(8,128)S(1)}, f32[80,1024]{1,0:T(8,128)S(1)}, u32[]{:S(2)}, u32[]{:S(2)}) collective-permute-start(f32[80,1024]{1,0:T(8,128)S(1)} %get-tuple-element.66), channel_id=1, source_target_pairs={{27,11},{31,15}} | collective-permute-start | bytes 983048 | tf_op jit(solution)/shard_map/ppermute | solution.py:507
  193.0 5.7 %collective-permute-start.31 = (f32[80,1024]{1,0:T(8,128)S(1)}, f32[80,1024]{1,0:T(8,128)S(1)}, u32[]{:S(2)}, u32[]{:S(2)}) collective-permute-start(f32[80,1024]{1,0:T(8,128)S(1)} %get-tuple-element.69), channel_id=1, source_target_pairs={{0,4},{4,8},{8,13},{13,17},{17,22},{22,26},{26,31}} | collective-permute-start | bytes 983048 | tf_op jit(solution)/shard_map/ppermute | solution.py:507
  193.7 14.7 %collective-permute-start.32 = (f32[80,1024]{1,0:T(8,128)S(1)}, f32[80,1024]{1,0:T(8,128)S(1)}, u32[]{:S(2)}, u32[]{:S(2)}) collective-permute-start(f32[80,1024]{1,0:T(8,128)S(1)} %get-tuple-element.69), channel_id=1, source_target_pairs={{0,0},{8,9},{12,13},{16,17},{20,21},{24,25},{28,29},{17,18},{21,22... | collective-permute-start | bytes 983048 | tf_op jit(solution)/shard_map/ppermute | solution.py:507
  195.6 18.5 %collective-permute-start.38 = (f32[80,1024]{1,0:T(8,128)S(1)}, f32[80,1024]{1,0:T(8,128)S(1)}, u32[]{:S(2)}, u32[]{:S(2)}) collective-permute-start(f32[80,1024]{1,0:T(8,128)S(1)} %get-tuple-element.69), channel_id=1, source_target_pairs={{27,3},{31,7}} | collective-permute-start | bytes 983048 | tf_op jit(solution)/shard_map/ppermute | solution.py:507
  196.3 19.8 %collective-permute-start.39 = (f32[80,1024]{1,0:T(8,128)S(1)}, f32[80,1024]{1,0:T(8,128)S(1)}, u32[]{:S(2)}, u32[]{:S(2)}) collective-permute-start(f32[80,1024]{1,0:T(8,128)S(1)} %get-tuple-element.69), channel_id=1, source_target_pairs={{27,11},{31,15}} | collective-permute-start | bytes 983048 | tf_op jit(solution)/shard_map/ppermute | solution.py:507
  210.0 6.1 %collective-permute-start.40 = (f32[80,1024]{1,0:T(8,128)S(1)}, f32[80,1024]{1,0:T(8,128)S(1)}, u32[]{:S(2)}, u32[]{:S(2)}) collective-permute-start(f32[80,1024]{1,0:T(8,128)S(1)} %get-tuple-element.76), channel_id=1, source_target_pairs={{27,3},{31,7}} | collective-permute-start | bytes 983048 | tf_op jit(solution)/shard_map/ppermute | solution.py:507
  210.7 5.4 %collective-permute-start.41 = (f32[80,1024]{1,0:T(8,128)S(1)}, f32[80,1024]{1,0:T(8,128)S(1)}, u32[]{:S(2)}, u32[]{:S(2)}) collective-permute-start(f32[80,1024]{1,0:T(8,128)S(1)} %get-tuple-element.76), channel_id=1, source_target_pairs={{27,11},{31,15}} | collective-permute-start | bytes 983048 | tf_op jit(solution)/shard_map/ppermute | solution.py:507
  211.4 4.7 %collective-permute-start.42 = (f32[80,1024]{1,0:T(8,128)S(1)}, f32[80,1024]{1,0:T(8,128)S(1)}, u32[]{:S(2)}, u32[]{:S(2)}) collective-permute-start(f32[80,1024]{1,0:T(8,128)S(1)} %get-tuple-element.76), channel_id=1, source_target_pairs={{27,19},{31,23}} | collective-permute-start | bytes 983048 | tf_op jit(solution)/shard_map/ppermute | solution.py:507
  214.2 18.5 %collective-permute-start.43 = (f32[160,1024]{1,0:T(8,128)S(1)}, f32[160,1024]{1,0:T(8,128)S(1)}, u32[]{:S(2)}, u32[]{:S(2)}) collective-permute-start(f32[160,1024]{1,0:T(8,128)S(1)} %shard_map.81.refs_6_.refs_5_.refs_1_), channel_id=1, source_target_pairs={{0,4},{4,0},{1,5},{5,1},{9,13},{13,9},{2,6},{6,2},{10,14},{14,10},... | collective-permute-start | bytes 1966088 | tf_op jit(solution)/shard_map/ppermute | solution.py:507
  217.8 22.9 %collective-permute-start.44 = (f32[160,1024]{1,0:T(8,128)S(1)}, f32[160,1024]{1,0:T(8,128)S(1)}, u32[]{:S(2)}, u32[]{:S(2)}) collective-permute-start(f32[160,1024]{1,0:T(8,128)S(1)} %shard_map.84.refs_2_), channel_id=1, source_target_pairs={{0,4},{4,0},{1,5},{5,1},{9,13},{13,9},{2,6},{6,2},{10,14},{14,10},... | collective-permute-start | bytes 1966088 | tf_op jit(solution)/shard_map/ppermute | solution.py:507
  221.7 2.8 collective-permute-start.35
  222.4 2.2 collective-permute-start.36
  223.1 8.5 %collective-permute-start.37 = (f32[320,256]{1,0:T(8,128)S(1)}, f32[320,256]{1,0:T(8,128)S(1)}, u32[]{:S(2)}, u32[]{:S(2)}) collective-permute-start(f32[320,256]{1,0:T(8,128)S(1)} %get-tuple-element.74), channel_id=1, source_target_pairs={{0,1},{4,5},{9,10},{13,14},{18,19},{22,23},{27,24},{31,28}} | collective-permute-start | bytes 983048 | tf_op jit(solution)/shard_map/ppermute | solution.py:507
  249.6 6.0 %collective-permute-start.45 = (f32[320,512]{1,0:T(8,128)S(1)}, f32[320,512]{1,0:T(8,128)S(1)}, u32[]{:S(2)}, u32[]{:S(2)}) collective-permute-start(f32[320,512]{1,0:T(8,128)S(1)} %shard_map.86.refs_5_), channel_id=1, source_target_pairs={{0,1},{1,0},{2,3},{3,2},{4,5},{5,4},{6,7},{7,6},{8,9},{9,8},{10,11... | collective-permute-start | bytes 1966088 | tf_op jit(solution)/shard_map/ppermute | solution.py:507
  256.5 17.4 %collective-permute-start.46 = (f32[320,512]{1,0:T(8,128)}, f32[320,512]{1,0:T(8,128)}, u32[]{:S(2)}, u32[]{:S(2)}) collective-permute-start(f32[320,512]{1,0:T(8,128)} %shard_map.88.refs_5_), channel_id=1, source_target_pairs={{0,2},{1,3},{2,0},{3,1},{4,6},{5,7},{6,4},{7,5},{8,10},{9,11},{10,... | collective-permute-start | bytes 1966088 | tf_op jit(solution)/shard_map/ppermute | solution.py:507
  263.3 18.8 %collective-permute-start.47 = (f32[320,512]{1,0:T(8,128)}, f32[320,512]{1,0:T(8,128)}, u32[]{:S(2)}, u32[]{:S(2)}) collective-permute-start(f32[320,512]{1,0:T(8,128)} %shard_map.89.refs_5_), channel_id=1, source_target_pairs={{0,1},{1,0},{2,3},{3,2},{4,5},{5,4},{6,7},{7,6},{8,9},{9,8},{10,11... | collective-permute-start | bytes 1966088 | tf_op jit(solution)/shard_map/ppermute | solution.py:507
  (10 other events, 103.3 us)

commit v3 on v2

--- a/solution.py
+++ b/solution.py
@@ -469,6 +469,23 @@
     )(info, *map(in_vmem, parts), in_vmem(place), in_hbm(panel), *waited)
 
 
+def solved_rows(info, shares, dates):
+    def kernel(info, *refs):
+        for index, ref in enumerate(refs[:-1]):
+            @pl.when(info[0] == index)
+            def _(ref=ref):
+                refs[-1][...] = ref[pl.ds(0, dates)]
+
+    whole = pl.BlockSpec(memory_space=pltpu.VMEM)
+    return pl.pallas_call(
+        kernel,
+        out_shape=jax.ShapeDtypeStruct((dates, shares[0].shape[1]), jnp.float32),
+        in_specs=[pl.BlockSpec(memory_space=pltpu.SMEM)] + [whole] * len(shares),
+        out_specs=whole,
+        compiler_params=pltpu.CompilerParams(vmem_limit_bytes=16 << 20),
+    )(info, *map(in_vmem, shares))
+
+
 def add_kernel(left_ref, right_ref, out_ref):
     out_ref[...] = left_ref[...] + right_ref[:, pl.ds(0, out_ref.shape[1])]
 
@@ -533,10 +550,8 @@
         local_order = point_order % group_rows
         block_order = lax.dynamic_slice(local_order, (slot_index * block,), (block,))
         place = (block_order // own_points - col) % col_count * own_points + block_order % own_points
-        first_direct = 2 * top + 2
-        arrived = jnp.where(origin, 0, jnp.where((col == top) & (level == top - 1), first_direct, 3 * col - level + 1))
-        from_direct = (col == top) & (level < top - 1)
-        stored_at = jnp.where(above, level + col + 1, jnp.where(from_direct, first_direct + 4 * chunks, arrived))
+        arrived = jnp.where(origin, 0, 3 * col - level + 1)
+        stored_at = jnp.where(above, level + col + 1, arrived)
         own_place = jnp.where(local_order // own_points != col, -1, local_order % own_points)[:, None]
         def pack(*values):
             return jnp.stack([jnp.asarray(value).astype(jnp.int32) for value in values])
@@ -557,13 +572,14 @@
             side,
             jnp.logical_not(origin),
         )
-        usual = jnp.where(from_direct, level + 1, 0)
-        fetch_info = pack(side, usual, usual)
-        late_info = pack(side, usual, jnp.where((col == top) & (level == top - 1), top, usual))
+        late_at = jnp.where((col == top) & (level < top), arrived - (STEPS - 1 + chunks - 1), -chunks)
+        early_info = pack(side, *[jnp.maximum(late_at + chunk, 0) for chunk in range(2)])
+        late_info = pack(side, *[jnp.maximum(late_at + chunk, 0) for chunk in range(2, 4)])
+        turn_info = pack((col - level) % col_count)
         solved_info = pack(side, *[(col + turn) % col_count for turn in range(col_count)])
         residual_info = pack(above, side, col ^ 3, col ^ 1, col ^ 2, col)
         place = place[None, :]
-        waited = [place, start_info, rest_info, slot_info, fetch_info, late_info, solved_info, residual_info, own_place]
+        waited = [place, start_info, rest_info, slot_info, early_info, late_info, turn_info, solved_info, residual_info, own_place]
 
         high, low = chain_factors(factor_info, diag_inverse, panel, per_tile, waited)
         start = start_values(start_info, shares, place, diag_inverse, chunks, width, [])
@@ -578,14 +594,10 @@
                         side_pairs.append((flat(z, y, c), flat(z, y, c + 1)))
                         continue
                     cross_pairs.append((flat(z, y, c), flat(z, 1 - y, c)))
-                    if z and (c < levels - 1 or z == c):
+                    if z:
                         down_pairs.append((flat(z, y, c), flat(z - 1, y, c)))
-        direct_pairs = [[(flat(top, y, top), flat(z, y, top)) for y in range(2)] for z in range(top)]
-        late_pairs = direct_pairs[top - 1]
-        mine, crossed, direct = [], [], []
-
-        def send_direct():
-            direct.append([send(out, direct_pairs[z]) for z in range(top - 1)])
+        late_pairs = [(source, target) for source, target in down_pairs if source % col_count == top]
+        mine, crossed = [], []
 
         def cross(info, arrays, waited):
             mine.append(fetch(2 * len(mine), info, store, arrays, mine[-1:] + waited))
@@ -601,23 +613,21 @@
                        for y in range(2) if busy(z + c + 1, slot - 1)]
                 received = [send(out, chain_pairs), send(out, side_pairs + down_pairs),
                             send(pair, ups) if ups else None]
-            if slot >= first_direct:
-                send_direct()
             out, pair, store = advance(slot, slot_info, received, start, start_rest, high, low, store,
-                                       mine[-1:] + (direct[-2] if len(direct) > 1 else []))
+                                       [])
             if slot == 0:
                 start_rest = start_values(rest_info, shares, place, diag_inverse, chunks, width, [out])
-            if slot == first_direct + 1:
-                cross(fetch_info, direct, [])
-
-        send_direct()
-        late = send(out, late_pairs)
+
+        late = [send(out, late_pairs)]
+        while len(late) < chunks - 1:
+            late.append(send(late[-1], late_pairs))
         pieces = solved_shares(solved_info, store, col_count)
         delivered = []
         for turn in range(1, col_count):
             pairs = [(flat(z, y, z), flat(z, y, (z + turn) % col_count)) for z in range(levels) for y in range(2)]
             delivered.append(send(pieces[turn], pairs))
-        cross(late_info, [direct[-2], direct[-1] + [late]], [pieces[0]])
+        cross(early_info, [[], late[:1]], [])
+        cross(late_info, [late[:2], late], [pieces[0]])
         near = [(at * col_count + here, at * col_count + (here ^ 1))
                 for at in range(row_count) for here in range(col_count)]
         far = [(at * col_count + here, at * col_count + (here ^ 2))
@@ -635,12 +645,9 @@
         give = share(1, [passed])
         moved = send(give, near)
         own = share(3, [give, moved_far])
-        solved = pieces[0]
-        for turn in range(1, col_count):
-            solved = jnp.where((col - level) % col_count == turn, delivered[turn - 1], solved)
-
+        solved = solved_rows(turn_info, [pieces[0]] + delivered, dates)
         residual = ((own + moved) + moved_far)[:dates]
-        return solved[:dates].T, residual.T
+        return solved.T, residual.T
 
     return body
 

time: 286 us -> 290 us (1.014)
  starting transfers between devices: 52.8 us -> 63.3 us
  other arithmetic: 5.36 us -> 2.05 us
    ppermute x48 -> x42, starting transfers between devices: 52.8 us -> 63.3 us  [send(): return lax.ppermute(value, ('rows', 'cols'), pairs)]
    transpose x2 -> x1, other arithmetic: 4.32 us -> 1.01 us  [body(): return (solved.T, residual.T)]
    ppermute x48 -> x42, waiting for transfers between devices: 164 us -> 162 us  [send(): return lax.ppermute(value, ('rows', 'cols'), pairs)]
  transfers between devices with their start and end apart: 48 -> 42, of which waited for: 15 -> 14; matrix products, arithmetic and copies ran while one was open for 2% -> 1% of each run, Pallas kernels for 12% -> 11%
where the time goes in v3:
time: 290 us; the launch traced here: 286 us
  waiting for transfers between devices  162 us (56%)
  starting transfers between devices  63.3 us (22%)
  Pallas kernels  54 us (19%)
  between operations  3.43 us (1%)
    ppermute x42, waiting for transfers between devices, send(): return lax.ppermute(value, ('rows', 'cols'), pairs)  162 us
    ppermute x42, starting transfers between devices, send(): return lax.ppermute(value, ('rows', 'cols'), pairs)  63.3 us
    pallas_call x4, Pallas kernels, residual_tiles(): pl.pallas_call(kernel, out_shape=vmem_shape((total, tiles * size), jnp.fl...  24.4 us
    pallas_call x11, Pallas kernels, advance(): pl.pallas_call(kernel, out_shape=[vmem_shape((width, block), jnp.float32)...  13.4 us
    pallas_call x1, Pallas kernels, chain_factors(): pl.pallas_call(factor_kernel, out_shape=[shape, shape], grid_spec=pltpu.P...  5.98 us
  transfers between devices with their start and end apart: 42, of which 14 were waited for; matrix products, arithmetic and copies ran while one was open for 1% of the time, Pallas kernels for 11%

profile of v3, /device:TPU:14, one launch (start us, length us, event | category | flops | bytes accessed | tf_op | source)
XLA Modules:
  0.0 286.3 jit_solution(5057948933594034041)
XLA Ops:
  2.0 3.1 %collective-permute-start = (f32[300,512]{1,0:T(8,128)}, f32[300,512]{1,0:T(8,128)S(1)}, u32[]{:S(2)}, u32[]{:S(2)}) collective-permute-start(f32[300,512]{1,0:T(8,128)} %refs_5_.5), channel_id=1, source_target_pairs={{1,0},{5,4},{9,8},{14,13},{18,17},{23,22},{27,26},{28,31}} | collective-permute-start | bytes 1843208 | tf_op jit(solution)/shard_map/ppermute | solution.py:524
  5.3 1.2 dynamic_slice.6
  10.3 6.0 %shard_map.69 = (bf16[2048,1024]{1,0:T(8,128)(2,1)S(1)}, bf16[2048,1024]{1,0:T(8,128)(2,1)S(1)}) custom-call(s32[2]{0:T(128)S(1)} %pad_add_fusion.1.info, f32[2048,1024]{1,0:T(8,128)} %refs_5_.4, f32[2048,2048]{1,0:T(8,128)} %refs_4_.7, s32[1,1024]{1,0:T(1,128)S(1)} %bitcast.35, s32[2]{0:T(128)S(1)} %get-tuple-element.82.info.rest_1_, ...), custom_call_target="tpu_custom_call" | custom-call | flops 12884901888 | bytes 20971520 | tf_op jit(solution)/shard_map/pallas_call | solution.py:80
  16.3 1.7 collective-permute-done.refs_1_
  18.6 1.5 shard_map.70
  20.0 1.9 collective-permute-start.4
  23.3 8.7 %collective-permute-done.4.refs_1_ = f32[80,1024]{1,0:T(8,128)S(1)} collective-permute-done((f32[80,1024]{1,0:T(8,128)S(1)}, f32[80,1024]{1,0:T(8,128)S(1)}, u32[]{:S(2)}, u32[]{:S(2)}) %collective-permute-start.4) | collective-permute-done | bytes 327712 | tf_op jit(solution)/shard_map/ppermute | solution.py:524
  33.4 1.9 collective-permute-start.6
  36.0 21.7 %collective-permute-done.6.refs_1_ = f32[80,1024]{1,0:T(8,128)S(1)} collective-permute-done((f32[80,1024]{1,0:T(8,128)S(1)}, f32[80,1024]{1,0:T(8,128)S(1)}, u32[]{:S(2)}, u32[]{:S(2)}) %collective-permute-start.6) | collective-permute-done | bytes 327712 | tf_op jit(solution)/shard_map/ppermute | solution.py:524
  59.1 1.9 collective-permute-start.9
  61.8 8.8 %collective-permute-done.9.refs_1_ = f32[80,1024]{1,0:T(8,128)S(1)} collective-permute-done((f32[80,1024]{1,0:T(8,128)S(1)}, f32[80,1024]{1,0:T(8,128)S(1)}, u32[]{:S(2)}, u32[]{:S(2)}) %collective-permute-start.9) | collective-permute-done | bytes 327712 | tf_op jit(solution)/shard_map/ppermute | solution.py:524
  72.0 1.9 collective-permute-start.12
  74.7 9.6 %collective-permute-done.12.refs_1_ = f32[80,1024]{1,0:T(8,128)S(1)} collective-permute-done((f32[80,1024]{1,0:T(8,128)S(1)}, f32[80,1024]{1,0:T(8,128)S(1)}, u32[]{:S(2)}, u32[]{:S(2)}) %collective-permute-start.12) | collective-permute-done | bytes 327712 | tf_op jit(solution)/shard_map/ppermute | solution.py:524
  85.7 1.9 collective-permute-start.15
  87.7 0.9 collective-permute-start.14
  88.5 12.7 %collective-permute-done.15.refs_1_ = f32[80,1024]{1,0:T(8,128)S(1)} collective-permute-done((f32[80,1024]{1,0:T(8,128)S(1)}, f32[80,1024]{1,0:T(8,128)S(1)}, u32[]{:S(2)}, u32[]{:S(2)}) %collective-permute-start.15) | collective-permute-done | bytes 327712 | tf_op jit(solution)/shard_map/ppermute | solution.py:524
  102.7 1.9 collective-permute-start.18
  105.3 21.1 %collective-permute-done.18.refs_1_ = f32[80,1024]{1,0:T(8,128)S(1)} collective-permute-done((f32[80,1024]{1,0:T(8,128)S(1)}, f32[80,1024]{1,0:T(8,128)S(1)}, u32[]{:S(2)}, u32[]{:S(2)}) %collective-permute-start.18) | collective-permute-done | bytes 327712 | tf_op jit(solution)/shard_map/ppermute | solution.py:524
  126.4 1.5 shard_map.77
  128.6 1.9 collective-permute-start.21
  131.2 17.0 %collective-permute-done.21.refs_1_ = f32[80,1024]{1,0:T(8,128)S(1)} collective-permute-done((f32[80,1024]{1,0:T(8,128)S(1)}, f32[80,1024]{1,0:T(8,128)S(1)}, u32[]{:S(2)}, u32[]{:S(2)}) %collective-permute-start.21) | collective-permute-done | bytes 327712 | tf_op jit(solution)/shard_map/ppermute | solution.py:524
  148.3 1.5 shard_map.78
  150.5 1.9 collective-permute-start.24
  153.1 17.0 %collective-permute-done.24.refs_1_ = f32[80,1024]{1,0:T(8,128)S(1)} collective-permute-done((f32[80,1024]{1,0:T(8,128)S(1)}, f32[80,1024]{1,0:T(8,128)S(1)}, u32[]{:S(2)}, u32[]{:S(2)}) %collective-permute-start.24) | collective-permute-done | bytes 327712 | tf_op jit(solution)/shard_map/ppermute | solution.py:524
  170.1 1.5 shard_map.79
  172.2 1.9 collective-permute-start.27
  174.9 15.7 %collective-permute-done.27.refs_1_ = f32[80,1024]{1,0:T(8,128)S(1)} collective-permute-done((f32[80,1024]{1,0:T(8,128)S(1)}, f32[80,1024]{1,0:T(8,128)S(1)}, u32[]{:S(2)}, u32[]{:S(2)}) %collective-permute-start.27) | collective-permute-done | bytes 327712 | tf_op jit(solution)/shard_map/ppermute | solution.py:524
  190.6 2.3 shard_map.80
  192.9 1.9 collective-permute-start.30
  195.5 8.7 %collective-permute-done.30.refs_1_ = f32[80,1024]{1,0:T(8,128)S(1)} collective-permute-done((f32[80,1024]{1,0:T(8,128)S(1)}, f32[80,1024]{1,0:T(8,128)S(1)}, u32[]{:S(2)}, u32[]{:S(2)}) %collective-permute-start.30) | collective-permute-done | bytes 327712 | tf_op jit(solution)/shard_map/ppermute | solution.py:524
  204.2 1.5 shard_map.81
  207.8 2.1 shard_map.82
  209.9 1.6 shard_map.84.refs_5_.refs_1_
  211.5 1.9 collective-permute-start.37
  213.5 1.6 shard_map.85.refs_2_
  215.1 3.9 %collective-permute-start.38 = (f32[160,1024]{1,0:T(8,128)S(1)}, f32[160,1024]{1,0:T(8,128)S(1)}, u32[]{:S(2)}, u32[]{:S(2)}) collective-permute-start(f32[160,1024]{1,0:T(8,128)S(1)} %shard_map.85.refs_2_), channel_id=1, source_target_pairs={{0,4},{4,0},{1,5},{5,1},{9,13},{13,9},{2,6},{6,2},{10,14},{14,10},... | collective-permute-start | bytes 1966088 | tf_op jit(solution)/shard_map/ppermute | solution.py:524
  219.1 1.3 collective-permute-start.31
  221.7 5.8 %collective-permute-done.31.refs_1_.refs_6_ = f32[320,256]{1,0:T(8,128)S(1)} collective-permute-done((f32[320,256]{1,0:T(8,128)S(1)}, f32[320,256]{1,0:T(8,128)S(1)}, u32[]{:S(2)}, u32[]{:S(2)}) %collective-permute-start.31) | collective-permute-done | bytes 327712 | tf_op jit(solution)/shard_map/ppermute | solution.py:524
  227.6 3.5 %collective-permute-done.38.refs_4_ = f32[160,1024]{1,0:T(8,128)S(1)} collective-permute-done((f32[160,1024]{1,0:T(8,128)S(1)}, f32[160,1024]{1,0:T(8,128)S(1)}, u32[]{:S(2)}, u32[]{:S(2)}) %collective-permute-start.38) | collective-permute-done | bytes 655392 | tf_op jit(solution)/shard_map/ppermute | solution.py:524
  231.0 2.9 shard_map.86
  233.9 6.1 %shard_map.87.refs_5_ = f32[320,512]{1,0:T(8,128)S(1)} custom-call(s32[6]{0:T(128)S(1)} %stack.189.rest_8_.info, bf16[2048,768]{1,0:T(8,128)(2,1)S(1)} %get-tuple-element.77.refs_0_, bf16[512,384]{1,0:T(8,128)(2,1)S(1)} %get-tuple-element.78.refs_1_, bf16[512,384]{1,0:T(8,128)(2,1)S(1)} %get-tuple-element.79.refs_2_, s32[2048,1]{1,0:T(8,128)S(1)} %copy.17.rest_9_.refs_3_, ...), custom_call_target="tpu_custom_call" | custom-call | flops 2013265920 | bytes 4194304 | tf_op jit(solution)/shard_map/pallas_call | solution.py:459
  240.0 16.3 %collective-permute-start.39 = (f32[320,512]{1,0:T(8,128)S(1)}, f32[320,512]{1,0:T(8,128)S(1)}, u32[]{:S(2)}, u32[]{:S(2)}) collective-permute-start(f32[320,512]{1,0:T(8,128)S(1)} %shard_map.87.refs_5_), channel_id=1, source_target_pairs={{0,1},{1,0},{2,3},{3,2},{4,5},{5,4},{6,7},{7,6},{8,9},{9,8},{10,11... | collective-permute-start | bytes 1966088 | tf_op jit(solution)/shard_map/ppermute | solution.py:524
  256.3 6.1 %shard_map.88.left_ref = f32[320,512]{1,0:T(8,128)S(1)} custom-call(s32[6]{0:T(128)S(1)} %stack.189.rest_8_.info, bf16[2048,768]{1,0:T(8,128)(2,1)S(1)} %get-tuple-element.77.refs_0_, bf16[512,384]{1,0:T(8,128)(2,1)S(1)} %get-tuple-element.78.refs_1_, bf16[512,384]{1,0:T(8,128)(2,1)S(1)} %get-tuple-element.79.refs_2_, s32[2048,1]{1,0:T(8,128)S(1)} %copy.17.rest_9_.refs_3_, ...), custom_call_target="tpu_custom_call" | custom-call | flops 2013265920 | bytes 4194304 | tf_op jit(solution)/shard_map/pallas_call | solution.py:459
  262.6 6.1 %shard_map.90.refs_5_ = f32[320,512]{1,0:T(8,128)S(1)} custom-call(s32[6]{0:T(128)S(1)} %stack.189.rest_8_.info, bf16[2048,768]{1,0:T(8,128)(2,1)S(1)} %get-tuple-element.77.refs_0_, bf16[512,384]{1,0:T(8,128)(2,1)S(1)} %get-tuple-element.78.refs_1_, bf16[512,384]{1,0:T(8,128)(2,1)S(1)} %get-tuple-element.79.refs_2_, s32[2048,1]{1,0:T(8,128)S(1)} %copy.17.rest_9_.refs_3_, ...), custom_call_target="tpu_custom_call" | custom-call | flops 2013265920 | bytes 4194304 | tf_op jit(solution)/shard_map/pallas_call | solution.py:459
  268.7 0.8 shard_map.83
  269.5 9.7 %collective-permute-done.40.refs_6_ = f32[320,512]{1,0:T(8,128)S(1)} collective-permute-done((f32[320,512]{1,0:T(8,128)S(1)}, f32[320,512]{1,0:T(8,128)S(1)}, u32[]{:S(2)}, u32[]{:S(2)}) %collective-permute-start.40) | collective-permute-done | bytes 655392 | tf_op jit(solution)/shard_map/ppermute | solution.py:524
  279.2 6.1 %shard_map.91 = f32[320,512]{1,0:T(8,128)S(1)} custom-call(s32[6]{0:T(128)S(1)} %stack.189.rest_8_.info, bf16[2048,768]{1,0:T(8,128)(2,1)S(1)} %get-tuple-element.77.refs_0_, bf16[512,384]{1,0:T(8,128)(2,1)S(1)} %get-tuple-element.78.refs_1_, bf16[512,384]{1,0:T(8,128)(2,1)S(1)} %get-tuple-element.79.refs_2_, s32[2048,1]{1,0:T(8,128)S(1)} %copy.17.rest_9_.refs_3_, ...), custom_call_target="tpu_custom_call" | custom-call | flops 2013265920 | bytes 4194304 | tf_op jit(solution)/shard_map/pallas_call | solution.py:459
  285.3 1.0 fusion
  (74 shorter events, 23.4 us)
Async XLA Ops:
  0.6 15.6 %collective-permute-start.2 = (f32[300,512]{1,0:T(8,128)}, f32[300,512]{1,0:T(8,128)S(1)}, u32[]{:S(2)}, u32[]{:S(2)}) collective-permute-start(f32[300,512]{1,0:T(8,128)} %refs_5_.5), channel_id=1, source_target_pairs={{3,0},{7,4},{11,8},{12,13},{16,17},{21,22},{25,26},{30,31}} | collective-permute-start | bytes 1843208 | tf_op jit(solution)/shard_map/ppermute | solution.py:524
  1.3 14.9 %collective-permute-start.1 = (f32[300,512]{1,0:T(8,128)}, f32[300,512]{1,0:T(8,128)S(1)}, u32[]{:S(2)}, u32[]{:S(2)}) collective-permute-start(f32[300,512]{1,0:T(8,128)} %refs_5_.5), channel_id=1, source_target_pairs={{2,0},{6,4},{10,8},{15,13},{19,17},{20,22},{24,26},{29,31}} | collective-permute-start | bytes 1843208 | tf_op jit(solution)/shard_map/ppermute | solution.py:524
  2.0 15.9 %collective-permute-start = (f32[300,512]{1,0:T(8,128)}, f32[300,512]{1,0:T(8,128)S(1)}, u32[]{:S(2)}, u32[]{:S(2)}) collective-permute-start(f32[300,512]{1,0:T(8,128)} %refs_5_.5), channel_id=1, source_target_pairs={{1,0},{5,4},{9,8},{14,13},{18,17},{23,22},{27,26},{28,31}} | collective-permute-start | bytes 1843208 | tf_op jit(solution)/shard_map/ppermute | solution.py:524
  10.3 7.7 %copy-start = (f32[300,512]{1,0:T(8,128)S(1)}, f32[300,512]{1,0:T(8,128)}, u32[]{:S(2)}) copy-start(f32[300,512]{1,0:T(8,128)} %refs_5_.5) | copy-start | bytes 1843204
  20.0 11.9 %collective-permute-start.4 = (f32[80,1024]{1,0:T(8,128)S(1)}, f32[80,1024]{1,0:T(8,128)S(1)}, u32[]{:S(2)}, u32[]{:S(2)}) collective-permute-start(f32[80,1024]{1,0:T(8,128)S(1)} %get-tuple-element.43.refs_6_), channel_id=1, source_target_pairs={{0,0},{8,9},{12,13},{16,17},{20,21},{24,25},{28,29},{17,18},{21,22... | collective-permute-start | bytes 983048 | tf_op jit(solution)/shard_map/ppermute | solution.py:524
  22.0 10.0 %collective-permute-start.3 = (f32[80,1024]{1,0:T(8,128)S(1)}, f32[80,1024]{1,0:T(8,128)S(1)}, u32[]{:S(2)}, u32[]{:S(2)}) collective-permute-start(f32[80,1024]{1,0:T(8,128)S(1)} %get-tuple-element.43.refs_6_), channel_id=1, source_target_pairs={{0,4},{4,8},{8,13},{13,17},{17,22},{22,26},{26,31}} | collective-permute-start | bytes 983048 | tf_op jit(solution)/shard_map/ppermute | solution.py:524
  32.7 25.0 %collective-permute-start.7 = (f32[160,1024]{1,0:T(8,128)S(1)}, f32[160,1024]{1,0:T(8,128)S(1)}, u32[]{:S(2)}, u32[]{:S(2)}) collective-permute-start(f32[160,1024]{1,0:T(8,128)S(1)} %get-tuple-element.46), channel_id=1, source_target_pairs={{0,8},{4,12}} | collective-permute-start | bytes 1966088 | tf_op jit(solution)/shard_map/ppermute | solution.py:524
  33.4 24.3 %collective-permute-start.6 = (f32[80,1024]{1,0:T(8,128)S(1)}, f32[80,1024]{1,0:T(8,128)S(1)}, u32[]{:S(2)}, u32[]{:S(2)}) collective-permute-start(f32[80,1024]{1,0:T(8,128)S(1)} %get-tuple-element.45), channel_id=1, source_target_pairs={{0,0},{8,9},{12,13},{16,17},{20,21},{24,25},{28,29},{17,18},{21,22... | collective-permute-start | bytes 983048 | tf_op jit(solution)/shard_map/ppermute | solution.py:524
  35.3 22.4 %collective-permute-start.5 = (f32[80,1024]{1,0:T(8,128)S(1)}, f32[80,1024]{1,0:T(8,128)S(1)}, u32[]{:S(2)}, u32[]{:S(2)}) collective-permute-start(f32[80,1024]{1,0:T(8,128)S(1)} %get-tuple-element.45), channel_id=1, source_target_pairs={{0,4},{4,8},{8,13},{13,17},{17,22},{22,26},{26,31}} | collective-permute-start | bytes 983048 | tf_op jit(solution)/shard_map/ppermute | solution.py:524
  58.4 12.1 %collective-permute-start.10 = (f32[160,1024]{1,0:T(8,128)S(1)}, f32[160,1024]{1,0:T(8,128)S(1)}, u32[]{:S(2)}, u32[]{:S(2)}) collective-permute-start(f32[160,1024]{1,0:T(8,128)S(1)} %get-tuple-element.49), channel_id=1, source_target_pairs={{0,8},{4,12},{8,16},{12,20}} | collective-permute-start | bytes 1966088 | tf_op jit(solution)/shard_map/ppermute | solution.py:524
  59.1 11.4 %collective-permute-start.9 = (f32[80,1024]{1,0:T(8,128)S(1)}, f32[80,1024]{1,0:T(8,128)S(1)}, u32[]{:S(2)}, u32[]{:S(2)}) collective-permute-start(f32[80,1024]{1,0:T(8,128)S(1)} %get-tuple-element.48), channel_id=1, source_target_pairs={{0,0},{8,9},{12,13},{16,17},{20,21},{24,25},{28,29},{17,18},{21,22... | collective-permute-start | bytes 983048 | tf_op jit(solution)/shard_map/ppermute | solution.py:524
  61.1 9.5 %collective-permute-start.8 = (f32[80,1024]{1,0:T(8,128)S(1)}, f32[80,1024]{1,0:T(8,128)S(1)}, u32[]{:S(2)}, u32[]{:S(2)}) collective-permute-start(f32[80,1024]{1,0:T(8,128)S(1)} %get-tuple-element.48), channel_id=1, source_target_pairs={{0,4},{4,8},{8,13},{13,17},{17,22},{22,26},{26,31}} | collective-permute-start | bytes 983048 | tf_op jit(solution)/shard_map/ppermute | solution.py:524
  71.3 12.9 %collective-permute-start.13 = (f32[160,1024]{1,0:T(8,128)S(1)}, f32[160,1024]{1,0:T(8,128)S(1)}, u32[]{:S(2)}, u32[]{:S(2)}) collective-permute-start(f32[160,1024]{1,0:T(8,128)S(1)} %get-tuple-element.52), channel_id=1, source_target_pairs={{0,8},{4,12},{8,16},{12,20},{16,24},{20,28},{9,17},{13,21}} | collective-permute-start | bytes 1966088 | tf_op jit(solution)/shard_map/ppermute | solution.py:524
  72.0 12.2 %collective-permute-start.12 = (f32[80,1024]{1,0:T(8,128)S(1)}, f32[80,1024]{1,0:T(8,128)S(1)}, u32[]{:S(2)}, u32[]{:S(2)}) collective-permute-start(f32[80,1024]{1,0:T(8,128)S(1)} %get-tuple-element.51), channel_id=1, source_target_pairs={{0,0},{8,9},{12,13},{16,17},{20,21},{24,25},{28,29},{17,18},{21,22... | collective-permute-start | bytes 983048 | tf_op jit(solution)/shard_map/ppermute | solution.py:524
  74.0 10.3 %collective-permute-start.11 = (f32[80,1024]{1,0:T(8,128)S(1)}, f32[80,1024]{1,0:T(8,128)S(1)}, u32[]{:S(2)}, u32[]{:S(2)}) collective-permute-start(f32[80,1024]{1,0:T(8,128)S(1)} %get-tuple-element.51), channel_id=1, source_target_pairs={{0,4},{4,8},{8,13},{13,17},{17,22},{22,26},{26,31}} | collective-permute-start | bytes 983048 | tf_op jit(solution)/shard_map/ppermute | solution.py:524
  85.0 16.2 %collective-permute-start.16 = (f32[160,1024]{1,0:T(8,128)S(1)}, f32[160,1024]{1,0:T(8,128)S(1)}, u32[]{:S(2)}, u32[]{:S(2)}) collective-permute-start(f32[160,1024]{1,0:T(8,128)S(1)} %get-tuple-element.55), channel_id=1, source_target_pairs={{0,8},{4,12},{8,16},{12,20},{16,24},{20,28},{9,17},{13,21},{17,25}... | collective-permute-start | bytes 1966088 | tf_op jit(solution)/shard_map/ppermute | solution.py:524
  85.7 15.5 %collective-permute-start.15 = (f32[80,1024]{1,0:T(8,128)S(1)}, f32[80,1024]{1,0:T(8,128)S(1)}, u32[]{:S(2)}, u32[]{:S(2)}) collective-permute-start(f32[80,1024]{1,0:T(8,128)S(1)} %get-tuple-element.54), channel_id=1, source_target_pairs={{0,0},{8,9},{12,13},{16,17},{20,21},{24,25},{28,29},{17,18},{21,22... | collective-permute-start | bytes 983048 | tf_op jit(solution)/shard_map/ppermute | solution.py:524
  87.7 13.5 %collective-permute-start.14 = (f32[80,1024]{1,0:T(8,128)S(1)}, f32[80,1024]{1,0:T(8,128)S(1)}, u32[]{:S(2)}, u32[]{:S(2)}) collective-permute-start(f32[80,1024]{1,0:T(8,128)S(1)} %get-tuple-element.54), channel_id=1, source_target_pairs={{0,4},{4,8},{8,13},{13,17},{17,22},{22,26},{26,31}} | collective-permute-start | bytes 983048 | tf_op jit(solution)/shard_map/ppermute | solution.py:524
  102.0 24.5 %collective-permute-start.19 = (f32[160,1024]{1,0:T(8,128)S(1)}, f32[160,1024]{1,0:T(8,128)S(1)}, u32[]{:S(2)}, u32[]{:S(2)}) collective-permute-start(f32[160,1024]{1,0:T(8,128)S(1)} %get-tuple-element.58), channel_id=1, source_target_pairs={{8,16},{12,20},{16,24},{20,28},{9,17},{13,21},{17,25},{21,29},{18,... | collective-permute-start | bytes 1966088 | tf_op jit(solution)/shard_map/ppermute | solution.py:524
  102.7 23.8 %collective-permute-start.18 = (f32[80,1024]{1,0:T(8,128)S(1)}, f32[80,1024]{1,0:T(8,128)S(1)}, u32[]{:S(2)}, u32[]{:S(2)}) collective-permute-start(f32[80,1024]{1,0:T(8,128)S(1)} %get-tuple-element.57), channel_id=1, source_target_pairs={{0,0},{8,9},{12,13},{16,17},{20,21},{24,25},{28,29},{17,18},{21,22... | collective-permute-start | bytes 983048 | tf_op jit(solution)/shard_map/ppermute | solution.py:524
  104.6 21.8 %collective-permute-start.17 = (f32[80,1024]{1,0:T(8,128)S(1)}, f32[80,1024]{1,0:T(8,128)S(1)}, u32[]{:S(2)}, u32[]{:S(2)}) collective-permute-start(f32[80,1024]{1,0:T(8,128)S(1)} %get-tuple-element.57), channel_id=1, source_target_pairs={{0,4},{4,8},{8,13},{13,17},{17,22},{22,26},{26,31}} | collective-permute-start | bytes 983048 | tf_op jit(solution)/shard_map/ppermute | solution.py:524
  127.9 20.4 %collective-permute-start.22 = (f32[160,1024]{1,0:T(8,128)S(1)}, f32[160,1024]{1,0:T(8,128)S(1)}, u32[]{:S(2)}, u32[]{:S(2)}) collective-permute-start(f32[160,1024]{1,0:T(8,128)S(1)} %get-tuple-element.61), channel_id=1, source_target_pairs={{16,24},{20,28},{9,17},{13,21},{17,25},{21,29},{18,26},{22,30}} | collective-permute-start | bytes 1966088 | tf_op jit(solution)/shard_map/ppermute | solution.py:524
  128.6 19.6 %collective-permute-start.21 = (f32[80,1024]{1,0:T(8,128)S(1)}, f32[80,1024]{1,0:T(8,128)S(1)}, u32[]{:S(2)}, u32[]{:S(2)}) collective-permute-start(f32[80,1024]{1,0:T(8,128)S(1)} %get-tuple-element.60), channel_id=1, source_target_pairs={{0,0},{8,9},{12,13},{16,17},{20,21},{24,25},{28,29},{17,18},{21,22... | collective-permute-start | bytes 983048 | tf_op jit(solution)/shard_map/ppermute | solution.py:524
  130.6 17.7 %collective-permute-start.20 = (f32[80,1024]{1,0:T(8,128)S(1)}, f32[80,1024]{1,0:T(8,128)S(1)}, u32[]{:S(2)}, u32[]{:S(2)}) collective-permute-start(f32[80,1024]{1,0:T(8,128)S(1)} %get-tuple-element.60), channel_id=1, source_target_pairs={{0,4},{4,8},{8,13},{13,17},{17,22},{22,26},{26,31}} | collective-permute-start | bytes 983048 | tf_op jit(solution)/shard_map/ppermute | solution.py:524
  149.8 20.3 %collective-permute-start.25 = (f32[160,1024]{1,0:T(8,128)S(1)}, f32[160,1024]{1,0:T(8,128)S(1)}, u32[]{:S(2)}, u32[]{:S(2)}) collective-permute-start(f32[160,1024]{1,0:T(8,128)S(1)} %get-tuple-element.64), channel_id=1, source_target_pairs={{17,25},{21,29},{18,26},{22,30}} | collective-permute-start | bytes 1966088 | tf_op jit(solution)/shard_map/ppermute | solution.py:524
  150.5 19.6 %collective-permute-start.24 = (f32[80,1024]{1,0:T(8,128)S(1)}, f32[80,1024]{1,0:T(8,128)S(1)}, u32[]{:S(2)}, u32[]{:S(2)}) collective-permute-start(f32[80,1024]{1,0:T(8,128)S(1)} %get-tuple-element.63), channel_id=1, source_target_pairs={{0,0},{8,9},{12,13},{16,17},{20,21},{24,25},{28,29},{17,18},{21,22... | collective-permute-start | bytes 983048 | tf_op jit(solution)/shard_map/ppermute | solution.py:524
  152.4 17.7 %collective-permute-start.23 = (f32[80,1024]{1,0:T(8,128)S(1)}, f32[80,1024]{1,0:T(8,128)S(1)}, u32[]{:S(2)}, u32[]{:S(2)}) collective-permute-start(f32[80,1024]{1,0:T(8,128)S(1)} %get-tuple-element.63), channel_id=1, source_target_pairs={{0,4},{4,8},{8,13},{13,17},{17,22},{22,26},{26,31}} | collective-permute-start | bytes 983048 | tf_op jit(solution)/shard_map/ppermute | solution.py:524
  171.5 19.0 %collective-permute-start.28 = (f32[160,1024]{1,0:T(8,128)S(1)}, f32[160,1024]{1,0:T(8,128)S(1)}, u32[]{:S(2)}, u32[]{:S(2)}) collective-permute-start(f32[160,1024]{1,0:T(8,128)S(1)} %get-tuple-element.67), channel_id=1, source_target_pairs={{18,26},{22,30}} | collective-permute-start | bytes 1966088 | tf_op jit(solution)/shard_map/ppermute | solution.py:524
  172.2 18.3 %collective-permute-start.27 = (f32[80,1024]{1,0:T(8,128)S(1)}, f32[80,1024]{1,0:T(8,128)S(1)}, u32[]{:S(2)}, u32[]{:S(2)}) collective-permute-start(f32[80,1024]{1,0:T(8,128)S(1)} %get-tuple-element.66), channel_id=1, source_target_pairs={{0,0},{8,9},{12,13},{16,17},{20,21},{24,25},{28,29},{17,18},{21,22... | collective-permute-start | bytes 983048 | tf_op jit(solution)/shard_map/ppermute | solution.py:524
  174.2 16.4 %collective-permute-start.26 = (f32[80,1024]{1,0:T(8,128)S(1)}, f32[80,1024]{1,0:T(8,128)S(1)}, u32[]{:S(2)}, u32[]{:S(2)}) collective-permute-start(f32[80,1024]{1,0:T(8,128)S(1)} %get-tuple-element.66), channel_id=1, source_target_pairs={{0,4},{4,8},{8,13},{13,17},{17,22},{22,26},{26,31}} | collective-permute-start | bytes 983048 | tf_op jit(solution)/shard_map/ppermute | solution.py:524
  192.9 11.3 %collective-permute-start.30 = (f32[80,1024]{1,0:T(8,128)S(1)}, f32[80,1024]{1,0:T(8,128)S(1)}, u32[]{:S(2)}, u32[]{:S(2)}) collective-permute-start(f32[80,1024]{1,0:T(8,128)S(1)} %get-tuple-element.69), channel_id=1, source_target_pairs={{0,0},{8,9},{12,13},{16,17},{20,21},{24,25},{28,29},{17,18},{21,22... | collective-permute-start | bytes 983048 | tf_op jit(solution)/shard_map/ppermute | solution.py:524
  194.8 9.4 %collective-permute-start.29 = (f32[80,1024]{1,0:T(8,128)S(1)}, f32[80,1024]{1,0:T(8,128)S(1)}, u32[]{:S(2)}, u32[]{:S(2)}) collective-permute-start(f32[80,1024]{1,0:T(8,128)S(1)} %get-tuple-element.69), channel_id=1, source_target_pairs={{0,4},{4,8},{8,13},{13,17},{17,22},{22,26},{26,31}} | collective-permute-start | bytes 983048 | tf_op jit(solution)/shard_map/ppermute | solution.py:524
  205.7 0.7 collective-permute-start.34
  206.4 0.7 collective-permute-start.35
  207.1 6.3 %collective-permute-start.36 = (f32[80,1024]{1,0:T(8,128)S(1)}, f32[80,1024]{1,0:T(8,128)S(1)}, u32[]{:S(2)}, u32[]{:S(2)}) collective-permute-start(f32[80,1024]{1,0:T(8,128)S(1)} %collective-permute-done.35.refs_1_.refs_3_), channel_id=1, source_target_pairs={{11,3},{15,7},{19,11},{23,15},{27,19},{31,23}} | collective-permute-start | bytes 983048 | tf_op jit(solution)/shard_map/ppermute | solution.py:524
  211.5 16.0 %collective-permute-start.37 = (f32[160,1024]{1,0:T(8,128)S(1)}, f32[160,1024]{1,0:T(8,128)S(1)}, u32[]{:S(2)}, u32[]{:S(2)}) collective-permute-start(f32[160,1024]{1,0:T(8,128)S(1)} %shard_map.84.refs_5_.refs_1_), channel_id=1, source_target_pairs={{0,4},{4,0},{1,5},{5,1},{9,13},{13,9},{2,6},{6,2},{10,14},{14,10},... | collective-permute-start | bytes 1966088 | tf_op jit(solution)/shard_map/ppermute | solution.py:524
  215.1 15.9 %collective-permute-start.38 = (f32[160,1024]{1,0:T(8,128)S(1)}, f32[160,1024]{1,0:T(8,128)S(1)}, u32[]{:S(2)}, u32[]{:S(2)}) collective-permute-start(f32[160,1024]{1,0:T(8,128)S(1)} %shard_map.85.refs_2_), channel_id=1, source_target_pairs={{0,4},{4,0},{1,5},{5,1},{9,13},{13,9},{2,6},{6,2},{10,14},{14,10},... | collective-permute-start | bytes 1966088 | tf_op jit(solution)/shard_map/ppermute | solution.py:524
  219.1 8.5 %collective-permute-start.31 = (f32[320,256]{1,0:T(8,128)S(1)}, f32[320,256]{1,0:T(8,128)S(1)}, u32[]{:S(2)}, u32[]{:S(2)}) collective-permute-start(f32[320,256]{1,0:T(8,128)S(1)} %get-tuple-element.73), channel_id=1, source_target_pairs={{0,1},{4,5},{9,10},{13,14},{18,19},{22,23},{27,24},{31,28}} | collective-permute-start | bytes 983048 | tf_op jit(solution)/shard_map/ppermute | solution.py:524
  220.4 7.2 %collective-permute-start.32 = (f32[320,256]{1,0:T(8,128)S(1)}, f32[320,256]{1,0:T(8,128)S(1)}, u32[]{:S(2)}, u32[]{:S(2)}) collective-permute-start(f32[320,256]{1,0:T(8,128)S(1)} %get-tuple-element.74), channel_id=1, source_target_pairs={{0,2},{4,6},{9,11},{13,15},{18,16},{22,20},{27,25},{31,29}} | collective-permute-start | bytes 983048 | tf_op jit(solution)/shard_map/ppermute | solution.py:524
  221.0 6.5 %collective-permute-start.33 = (f32[320,256]{1,0:T(8,128)S(1)}, f32[320,256]{1,0:T(8,128)S(1)}, u32[]{:S(2)}, u32[]{:S(2)}) collective-permute-start(f32[320,256]{1,0:T(8,128)S(1)} %get-tuple-element.75), channel_id=1, source_target_pairs={{0,3},{4,7},{9,8},{13,12},{18,17},{22,21},{27,26},{31,30}} | collective-permute-start | bytes 983048 | tf_op jit(solution)/shard_map/ppermute | solution.py:524
  240.0 22.4 %collective-permute-start.39 = (f32[320,512]{1,0:T(8,128)S(1)}, f32[320,512]{1,0:T(8,128)S(1)}, u32[]{:S(2)}, u32[]{:S(2)}) collective-permute-start(f32[320,512]{1,0:T(8,128)S(1)} %shard_map.87.refs_5_), channel_id=1, source_target_pairs={{0,1},{1,0},{2,3},{3,2},{4,5},{5,4},{6,7},{7,6},{8,9},{9,8},{10,11... | collective-permute-start | bytes 1966088 | tf_op jit(solution)/shard_map/ppermute | solution.py:524
  262.5 16.7 %collective-permute-start.40 = (f32[320,512]{1,0:T(8,128)S(1)}, f32[320,512]{1,0:T(8,128)S(1)}, u32[]{:S(2)}, u32[]{:S(2)}) collective-permute-start(f32[320,512]{1,0:T(8,128)S(1)} %shard_map.89.refs_5_), channel_id=1, source_target_pairs={{0,2},{1,3},{2,0},{3,1},{4,6},{5,7},{6,4},{7,5},{8,10},{9,11},{10,... | collective-permute-start | bytes 1966088 | tf_op jit(solution)/shard_map/ppermute | solution.py:524
  268.7 16.6 %collective-permute-start.41 = (f32[320,512]{1,0:T(8,128)S(1)}, f32[320,512]{1,0:T(8,128)S(1)}, u32[]{:S(2)}, u32[]{:S(2)}) collective-permute-start(f32[320,512]{1,0:T(8,128)S(1)} %shard_map.90.refs_5_), channel_id=1, source_target_pairs={{0,1},{1,0},{2,3},{3,2},{4,5},{5,4},{6,7},{7,6},{8,9},{9,8},{10,11... | collective-permute-start | bytes 1966088 | tf_op jit(solution)/shard_map/ppermute | solution.py:524

commit v4 on v2

--- a/solution.py
+++ b/solution.py
@@ -469,6 +469,23 @@
     )(info, *map(in_vmem, parts), in_vmem(place), in_hbm(panel), *waited)
 
 
+def solved_rows(info, shares, dates):
+    def kernel(info, *refs):
+        for index, ref in enumerate(refs[:-1]):
+            @pl.when(info[0] == index)
+            def _(ref=ref):
+                refs[-1][...] = ref[pl.ds(0, dates)]
+
+    whole = pl.BlockSpec(memory_space=pltpu.VMEM)
+    return pl.pallas_call(
+        kernel,
+        out_shape=jax.ShapeDtypeStruct((dates, shares[0].shape[1]), jnp.float32),
+        in_specs=[pl.BlockSpec(memory_space=pltpu.SMEM)] + [whole] * len(shares),
+        out_specs=whole,
+        compiler_params=pltpu.CompilerParams(vmem_limit_bytes=16 << 20),
+    )(info, *map(in_vmem, shares))
+
+
 def add_kernel(left_ref, right_ref, out_ref):
     out_ref[...] = left_ref[...] + right_ref[:, pl.ds(0, out_ref.shape[1])]
 
@@ -559,11 +576,12 @@
         )
         usual = jnp.where(from_direct, level + 1, 0)
         fetch_info = pack(side, usual, usual)
+        turn_info = pack((col - level) % col_count)
         late_info = pack(side, usual, jnp.where((col == top) & (level == top - 1), top, usual))
         solved_info = pack(side, *[(col + turn) % col_count for turn in range(col_count)])
         residual_info = pack(above, side, col ^ 3, col ^ 1, col ^ 2, col)
         place = place[None, :]
-        waited = [place, start_info, rest_info, slot_info, fetch_info, late_info, solved_info, residual_info, own_place]
+        waited = [place, start_info, rest_info, slot_info, fetch_info, late_info, turn_info, solved_info, residual_info, own_place]
 
         high, low = chain_factors(factor_info, diag_inverse, panel, per_tile, waited)
         start = start_values(start_info, shares, place, diag_inverse, chunks, width, [])
@@ -635,12 +653,9 @@
         give = share(1, [passed])
         moved = send(give, near)
         own = share(3, [give, moved_far])
-        solved = pieces[0]
-        for turn in range(1, col_count):
-            solved = jnp.where((col - level) % col_count == turn, delivered[turn - 1], solved)
-
+        solved = solved_rows(turn_info, [pieces[0]] + delivered, dates)
         residual = ((own + moved) + moved_far)[:dates]
-        return solved[:dates].T, residual.T
+        return solved.T, residual.T
 
     return body
 

time: 286 us -> 281 us (0.983)
  other arithmetic: 5.36 us -> 2.06 us
    transpose x2 -> x1, other arithmetic: 4.32 us -> 1.01 us  [body(): return (solved.T, residual.T)]
  transfers between devices with their start and end apart: 48 -> 48, of which waited for: 15 -> 15; matrix products, arithmetic and copies ran while one was open for 2% -> 1% of each run, Pallas kernels for 12% -> 12%
where the time goes in v4:
time: 281 us; the launch traced here: 280 us
  waiting for transfers between devices  166 us (59%)
  Pallas kernels  54 us (19%)
  starting transfers between devices  52.8 us (19%)
  between operations  3.52 us (1%)
    ppermute x48, waiting for transfers between devices, send(): return lax.ppermute(value, ('rows', 'cols'), pairs)  166 us
    ppermute x48, starting transfers between devices, send(): return lax.ppermute(value, ('rows', 'cols'), pairs)  52.8 us
    pallas_call x4, Pallas kernels, residual_tiles(): pl.pallas_call(kernel, out_shape=vmem_shape((total, tiles * size), jnp.fl...  24.4 us
    pallas_call x11, Pallas kernels, advance(): pl.pallas_call(kernel, out_shape=[vmem_shape((width, block), jnp.float32)...  13.4 us
    pallas_call x1, Pallas kernels, chain_factors(): pl.pallas_call(factor_kernel, out_shape=[shape, shape], grid_spec=pltpu.P...  5.98 us
  transfers between devices with their start and end apart: 48, of which 15 were waited for; matrix products, arithmetic and copies ran while one was open for 1% of the time, Pallas kernels for 12%

profile of v4, /device:TPU:14, one launch (start us, length us, event | category | flops | bytes accessed | tf_op | source)
XLA Modules:
  0.0 280.2 jit_solution(4406343043383745499)
XLA Ops:
  0.6 1.9 collective-permute-start
  4.0 1.2 dynamic_slice.6
  9.0 6.0 %shard_map.69 = (bf16[2048,1024]{1,0:T(8,128)(2,1)S(1)}, bf16[2048,1024]{1,0:T(8,128)(2,1)S(1)}) custom-call(s32[2]{0:T(128)S(1)} %pad_add_fusion.1.info, f32[2048,1024]{1,0:T(8,128)} %refs_5_.4, f32[2048,2048]{1,0:T(8,128)} %refs_4_.7, s32[1,1024]{1,0:T(1,128)S(1)} %bitcast.33, s32[2]{0:T(128)S(1)} %get-tuple-element.82.info.rest_1_, ...), custom_call_target="tpu_custom_call" | custom-call | flops 12884901888 | bytes 20971520 | tf_op jit(solution)/shard_map/pallas_call | solution.py:80
  15.0 1.5 collective-permute-done.refs_1_
  17.2 1.5 shard_map.70
  19.3 4.2 %collective-permute-start.4 = (f32[80,1024]{1,0:T(8,128)S(1)}, f32[80,1024]{1,0:T(8,128)S(1)}, u32[]{:S(2)}, u32[]{:S(2)}) collective-permute-start(f32[80,1024]{1,0:T(8,128)S(1)} %get-tuple-element.43.refs_6_), channel_id=1, source_target_pairs={{0,0},{8,9},{12,13},{16,17},{20,21},{24,25},{28,29},{17,18},{21,22... | collective-permute-start | bytes 983048 | tf_op jit(solution)/shard_map/ppermute | solution.py:524
  24.1 18.6 %collective-permute-done.4.refs_1_ = f32[80,1024]{1,0:T(8,128)S(1)} collective-permute-done((f32[80,1024]{1,0:T(8,128)S(1)}, f32[80,1024]{1,0:T(8,128)S(1)}, u32[]{:S(2)}, u32[]{:S(2)}) %collective-permute-start.4) | collective-permute-done | bytes 327712 | tf_op jit(solution)/shard_map/ppermute | solution.py:524
  44.9 1.9 collective-permute-start.6
  46.8 12.9 %collective-permute-done.6.refs_1_ = f32[80,1024]{1,0:T(8,128)S(1)} collective-permute-done((f32[80,1024]{1,0:T(8,128)S(1)}, f32[80,1024]{1,0:T(8,128)S(1)}, u32[]{:S(2)}, u32[]{:S(2)}) %collective-permute-start.6) | collective-permute-done | bytes 327712 | tf_op jit(solution)/shard_map/ppermute | solution.py:524
  59.7 0.7 shard_map.73
  61.9 1.9 collective-permute-start.9
  63.8 9.7 %collective-permute-done.9.refs_1_ = f32[80,1024]{1,0:T(8,128)S(1)} collective-permute-done((f32[80,1024]{1,0:T(8,128)S(1)}, f32[80,1024]{1,0:T(8,128)S(1)}, u32[]{:S(2)}, u32[]{:S(2)}) %collective-permute-start.9) | collective-permute-done | bytes 327712 | tf_op jit(solution)/shard_map/ppermute | solution.py:524
  75.6 1.9 collective-permute-start.12
  77.6 9.7 %collective-permute-done.12.refs_1_ = f32[80,1024]{1,0:T(8,128)S(1)} collective-permute-done((f32[80,1024]{1,0:T(8,128)S(1)}, f32[80,1024]{1,0:T(8,128)S(1)}, u32[]{:S(2)}, u32[]{:S(2)}) %collective-permute-start.12) | collective-permute-done | bytes 327712 | tf_op jit(solution)/shard_map/ppermute | solution.py:524
  89.4 2.1 collective-permute-start.15
  91.5 9.7 %collective-permute-done.15.refs_1_ = f32[80,1024]{1,0:T(8,128)S(1)} collective-permute-done((f32[80,1024]{1,0:T(8,128)S(1)}, f32[80,1024]{1,0:T(8,128)S(1)}, u32[]{:S(2)}, u32[]{:S(2)}) %collective-permute-start.15) | collective-permute-done | bytes 327712 | tf_op jit(solution)/shard_map/ppermute | solution.py:524
  103.3 1.9 collective-permute-start.18
  105.2 18.4 %collective-permute-done.18.refs_1_ = f32[80,1024]{1,0:T(8,128)S(1)} collective-permute-done((f32[80,1024]{1,0:T(8,128)S(1)}, f32[80,1024]{1,0:T(8,128)S(1)}, u32[]{:S(2)}, u32[]{:S(2)}) %collective-permute-start.18) | collective-permute-done | bytes 327712 | tf_op jit(solution)/shard_map/ppermute | solution.py:524
  123.7 1.5 shard_map.77
  126.5 1.9 collective-permute-start.21
  128.5 17.1 %collective-permute-done.21.refs_1_ = f32[80,1024]{1,0:T(8,128)S(1)} collective-permute-done((f32[80,1024]{1,0:T(8,128)S(1)}, f32[80,1024]{1,0:T(8,128)S(1)}, u32[]{:S(2)}, u32[]{:S(2)}) %collective-permute-start.21) | collective-permute-done | bytes 327712 | tf_op jit(solution)/shard_map/ppermute | solution.py:524
  145.6 1.5 shard_map.78
  148.5 1.9 collective-permute-start.24
  150.4 16.9 %collective-permute-done.24.refs_1_ = f32[80,1024]{1,0:T(8,128)S(1)} collective-permute-done((f32[80,1024]{1,0:T(8,128)S(1)}, f32[80,1024]{1,0:T(8,128)S(1)}, u32[]{:S(2)}, u32[]{:S(2)}) %collective-permute-start.24) | collective-permute-done | bytes 327712 | tf_op jit(solution)/shard_map/ppermute | solution.py:524
  167.3 1.5 shard_map.79
  171.6 1.9 collective-permute-start.27
  174.9 15.8 %collective-permute-done.27.refs_1_ = f32[80,1024]{1,0:T(8,128)S(1)} collective-permute-done((f32[80,1024]{1,0:T(8,128)S(1)}, f32[80,1024]{1,0:T(8,128)S(1)}, u32[]{:S(2)}, u32[]{:S(2)}) %collective-permute-start.27) | collective-permute-done | bytes 327712 | tf_op jit(solution)/shard_map/ppermute | solution.py:524
  190.7 2.3 shard_map.80
  193.7 1.9 collective-permute-start.32
  197.1 1.6 shard_map.81.refs_6_.refs_5_.refs_1_
  198.7 9.7 %collective-permute-done.32.refs_1_ = f32[80,1024]{1,0:T(8,128)S(1)} collective-permute-done((f32[80,1024]{1,0:T(8,128)S(1)}, f32[80,1024]{1,0:T(8,128)S(1)}, u32[]{:S(2)}, u32[]{:S(2)}) %collective-permute-start.32) | collective-permute-done | bytes 327712 | tf_op jit(solution)/shard_map/ppermute | solution.py:524
  208.4 1.5 shard_map.82
  212.0 2.1 shard_map.83
  214.1 1.9 collective-permute-start.43
  216.0 1.6 shard_map.85.refs_2_
  217.7 3.9 %collective-permute-start.44 = (f32[160,1024]{1,0:T(8,128)S(1)}, f32[160,1024]{1,0:T(8,128)S(1)}, u32[]{:S(2)}, u32[]{:S(2)}) collective-permute-start(f32[160,1024]{1,0:T(8,128)S(1)} %shard_map.85.refs_2_), channel_id=1, source_target_pairs={{0,4},{4,0},{1,5},{5,1},{9,13},{13,9},{2,6},{6,2},{10,14},{14,10},... | collective-permute-start | bytes 1966088 | tf_op jit(solution)/shard_map/ppermute | solution.py:524
  221.6 1.3 collective-permute-start.35
  224.3 5.7 %collective-permute-done.35.refs_1_.refs_6_ = f32[320,256]{1,0:T(8,128)S(1)} collective-permute-done((f32[320,256]{1,0:T(8,128)S(1)}, f32[320,256]{1,0:T(8,128)S(1)}, u32[]{:S(2)}, u32[]{:S(2)}) %collective-permute-start.35) | collective-permute-done | bytes 327712 | tf_op jit(solution)/shard_map/ppermute | solution.py:524
  230.0 2.5 collective-permute-done.43.refs_3_
  232.5 8.1 %collective-permute-done.44.refs_4_ = f32[160,1024]{1,0:T(8,128)S(1)} collective-permute-done((f32[160,1024]{1,0:T(8,128)S(1)}, f32[160,1024]{1,0:T(8,128)S(1)}, u32[]{:S(2)}, u32[]{:S(2)}) %collective-permute-start.44) | collective-permute-done | bytes 655392 | tf_op jit(solution)/shard_map/ppermute | solution.py:524
  240.6 2.9 %shard_map.86 = (bf16[2048,768]{1,0:T(8,128)(2,1)S(1)}, bf16[512,384]{1,0:T(8,128)(2,1)S(1)}, bf16[512,384]{1,0:T(8,128)(2,1)S(1)}) custom-call(s32[6]{0:T(128)S(1)} %stack.183.rest_8_.info, f32[4,2,80,1024]{3,2,1,0:T(8,128)} %get-tuple-element.71.store_ref.refs_0_, f32[160,1024]{1,0:T(8,128)S(1)} %shard_map.81.refs_6_.refs_5_.refs_1_, ...), custom_call_target="tpu_custom_call" | custom-call | tf_op jit(solution)/shard_map/pallas_call | solution.py:401
  243.5 6.1 %shard_map.87.refs_5_ = f32[320,512]{1,0:T(8,128)S(1)} custom-call(s32[6]{0:T(128)S(1)} %stack.183.rest_8_.info, bf16[2048,768]{1,0:T(8,128)(2,1)S(1)} %get-tuple-element.77.refs_0_, bf16[512,384]{1,0:T(8,128)(2,1)S(1)} %get-tuple-element.78.refs_1_, bf16[512,384]{1,0:T(8,128)(2,1)S(1)} %get-tuple-element.79.refs_2_, s32[2048,1]{1,0:T(8,128)S(1)} %copy.17.rest_9_.refs_3_, ...), custom_call_target="tpu_custom_call" | custom-call | flops 2013265920 | bytes 4194304 | tf_op jit(solution)/shard_map/pallas_call | solution.py:459
  249.6 6.1 %shard_map.88.left_ref = f32[320,512]{1,0:T(8,128)S(1)} custom-call(s32[6]{0:T(128)S(1)} %stack.183.rest_8_.info, bf16[2048,768]{1,0:T(8,128)(2,1)S(1)} %get-tuple-element.77.refs_0_, bf16[512,384]{1,0:T(8,128)(2,1)S(1)} %get-tuple-element.78.refs_1_, bf16[512,384]{1,0:T(8,128)(2,1)S(1)} %get-tuple-element.79.refs_2_, s32[2048,1]{1,0:T(8,128)S(1)} %copy.17.rest_9_.refs_3_, ...), custom_call_target="tpu_custom_call" | custom-call | flops 2013265920 | bytes 4194304 | tf_op jit(solution)/shard_map/pallas_call | solution.py:459
  255.9 6.1 %shard_map.90.refs_5_ = f32[320,512]{1,0:T(8,128)S(1)} custom-call(s32[6]{0:T(128)S(1)} %stack.183.rest_8_.info, bf16[2048,768]{1,0:T(8,128)(2,1)S(1)} %get-tuple-element.77.refs_0_, bf16[512,384]{1,0:T(8,128)(2,1)S(1)} %get-tuple-element.78.refs_1_, bf16[512,384]{1,0:T(8,128)(2,1)S(1)} %get-tuple-element.79.refs_2_, s32[2048,1]{1,0:T(8,128)S(1)} %copy.17.rest_9_.refs_3_, ...), custom_call_target="tpu_custom_call" | custom-call | flops 2013265920 | bytes 4194304 | tf_op jit(solution)/shard_map/pallas_call | solution.py:459
  262.6 0.8 shard_map.84
  263.3 9.7 %collective-permute-done.46.refs_6_ = f32[320,512]{1,0:T(8,128)S(1)} collective-permute-done((f32[320,512]{1,0:T(8,128)S(1)}, f32[320,512]{1,0:T(8,128)S(1)}, u32[]{:S(2)}, u32[]{:S(2)}) %collective-permute-start.46) | collective-permute-done | bytes 655392 | tf_op jit(solution)/shard_map/ppermute | solution.py:524
  273.0 6.1 %shard_map.91 = f32[320,512]{1,0:T(8,128)S(1)} custom-call(s32[6]{0:T(128)S(1)} %stack.183.rest_8_.info, bf16[2048,768]{1,0:T(8,128)(2,1)S(1)} %get-tuple-element.77.refs_0_, bf16[512,384]{1,0:T(8,128)(2,1)S(1)} %get-tuple-element.78.refs_1_, bf16[512,384]{1,0:T(8,128)(2,1)S(1)} %get-tuple-element.79.refs_2_, s32[2048,1]{1,0:T(8,128)S(1)} %copy.17.rest_9_.refs_3_, ...), custom_call_target="tpu_custom_call" | custom-call | flops 2013265920 | bytes 4194304 | tf_op jit(solution)/shard_map/pallas_call | solution.py:459
  279.1 1.0 fusion
  (86 shorter events, 28.0 us)
Async XLA Ops:
  0.6 15.9 %collective-permute-start = (f32[300,512]{1,0:T(8,128)}, f32[300,512]{1,0:T(8,128)S(1)}, u32[]{:S(2)}, u32[]{:S(2)}) collective-permute-start(f32[300,512]{1,0:T(8,128)} %refs_5_.5), channel_id=1, source_target_pairs={{1,0},{5,4},{9,8},{14,13},{18,17},{23,22},{27,26},{28,31}} | collective-permute-start | bytes 1843208 | tf_op jit(solution)/shard_map/ppermute | solution.py:524
  2.6 14.0 %collective-permute-start.1 = (f32[300,512]{1,0:T(8,128)}, f32[300,512]{1,0:T(8,128)S(1)}, u32[]{:S(2)}, u32[]{:S(2)}) collective-permute-start(f32[300,512]{1,0:T(8,128)} %refs_5_.5), channel_id=1, source_target_pairs={{2,0},{6,4},{10,8},{15,13},{19,17},{20,22},{24,26},{29,31}} | collective-permute-start | bytes 1843208 | tf_op jit(solution)/shard_map/ppermute | solution.py:524
  3.3 13.3 %collective-permute-start.2 = (f32[300,512]{1,0:T(8,128)}, f32[300,512]{1,0:T(8,128)S(1)}, u32[]{:S(2)}, u32[]{:S(2)}) collective-permute-start(f32[300,512]{1,0:T(8,128)} %refs_5_.5), channel_id=1, source_target_pairs={{3,0},{7,4},{11,8},{12,13},{16,17},{21,22},{25,26},{30,31}} | collective-permute-start | bytes 1843208 | tf_op jit(solution)/shard_map/ppermute | solution.py:524
  18.6 5.5 %collective-permute-start.3 = (f32[80,1024]{1,0:T(8,128)S(1)}, f32[80,1024]{1,0:T(8,128)S(1)}, u32[]{:S(2)}, u32[]{:S(2)}) collective-permute-start(f32[80,1024]{1,0:T(8,128)S(1)} %get-tuple-element.43.refs_6_), channel_id=1, source_target_pairs={{0,4},{4,8},{8,13},{13,17},{17,22},{22,26},{26,31}} | collective-permute-start | bytes 983048 | tf_op jit(solution)/shard_map/ppermute | solution.py:524
  19.3 23.5 %collective-permute-start.4 = (f32[80,1024]{1,0:T(8,128)S(1)}, f32[80,1024]{1,0:T(8,128)S(1)}, u32[]{:S(2)}, u32[]{:S(2)}) collective-permute-start(f32[80,1024]{1,0:T(8,128)S(1)} %get-tuple-element.43.refs_6_), channel_id=1, source_target_pairs={{0,0},{8,9},{12,13},{16,17},{20,21},{24,25},{28,29},{17,18},{21,22... | collective-permute-start | bytes 983048 | tf_op jit(solution)/shard_map/ppermute | solution.py:524
  43.5 16.2 %collective-permute-start.7 = (f32[160,1024]{1,0:T(8,128)S(1)}, f32[160,1024]{1,0:T(8,128)S(1)}, u32[]{:S(2)}, u32[]{:S(2)}) collective-permute-start(f32[160,1024]{1,0:T(8,128)S(1)} %get-tuple-element.46), channel_id=1, source_target_pairs={{0,8},{4,12}} | collective-permute-start | bytes 1966088 | tf_op jit(solution)/shard_map/ppermute | solution.py:524
  44.2 2.6 collective-permute-start.5
  44.9 14.8 %collective-permute-start.6 = (f32[80,1024]{1,0:T(8,128)S(1)}, f32[80,1024]{1,0:T(8,128)S(1)}, u32[]{:S(2)}, u32[]{:S(2)}) collective-permute-start(f32[80,1024]{1,0:T(8,128)S(1)} %get-tuple-element.45), channel_id=1, source_target_pairs={{0,0},{8,9},{12,13},{16,17},{20,21},{24,25},{28,29},{17,18},{21,22... | collective-permute-start | bytes 983048 | tf_op jit(solution)/shard_map/ppermute | solution.py:524
  60.5 13.0 %collective-permute-start.10 = (f32[160,1024]{1,0:T(8,128)S(1)}, f32[160,1024]{1,0:T(8,128)S(1)}, u32[]{:S(2)}, u32[]{:S(2)}) collective-permute-start(f32[160,1024]{1,0:T(8,128)S(1)} %get-tuple-element.49), channel_id=1, source_target_pairs={{0,8},{4,12},{8,16},{12,20}} | collective-permute-start | bytes 1966088 | tf_op jit(solution)/shard_map/ppermute | solution.py:524
  61.2 2.6 collective-permute-start.8
  61.9 11.6 %collective-permute-start.9 = (f32[80,1024]{1,0:T(8,128)S(1)}, f32[80,1024]{1,0:T(8,128)S(1)}, u32[]{:S(2)}, u32[]{:S(2)}) collective-permute-start(f32[80,1024]{1,0:T(8,128)S(1)} %get-tuple-element.48), channel_id=1, source_target_pairs={{0,0},{8,9},{12,13},{16,17},{20,21},{24,25},{28,29},{17,18},{21,22... | collective-permute-start | bytes 983048 | tf_op jit(solution)/shard_map/ppermute | solution.py:524
  74.2 13.0 %collective-permute-start.13 = (f32[160,1024]{1,0:T(8,128)S(1)}, f32[160,1024]{1,0:T(8,128)S(1)}, u32[]{:S(2)}, u32[]{:S(2)}) collective-permute-start(f32[160,1024]{1,0:T(8,128)S(1)} %get-tuple-element.52), channel_id=1, source_target_pairs={{0,8},{4,12},{8,16},{12,20},{16,24},{20,28},{9,17},{13,21}} | collective-permute-start | bytes 1966088 | tf_op jit(solution)/shard_map/ppermute | solution.py:524
  74.9 2.6 collective-permute-start.11
  75.6 11.6 %collective-permute-start.12 = (f32[80,1024]{1,0:T(8,128)S(1)}, f32[80,1024]{1,0:T(8,128)S(1)}, u32[]{:S(2)}, u32[]{:S(2)}) collective-permute-start(f32[80,1024]{1,0:T(8,128)S(1)} %get-tuple-element.51), channel_id=1, source_target_pairs={{0,0},{8,9},{12,13},{16,17},{20,21},{24,25},{28,29},{17,18},{21,22... | collective-permute-start | bytes 983048 | tf_op jit(solution)/shard_map/ppermute | solution.py:524
  88.0 13.2 %collective-permute-start.16 = (f32[160,1024]{1,0:T(8,128)S(1)}, f32[160,1024]{1,0:T(8,128)S(1)}, u32[]{:S(2)}, u32[]{:S(2)}) collective-permute-start(f32[160,1024]{1,0:T(8,128)S(1)} %get-tuple-element.55), channel_id=1, source_target_pairs={{0,8},{4,12},{8,16},{12,20},{16,24},{20,28},{9,17},{13,21},{17,25}... | collective-permute-start | bytes 1966088 | tf_op jit(solution)/shard_map/ppermute | solution.py:524
  88.7 2.8 collective-permute-start.14
  89.4 11.8 %collective-permute-start.15 = (f32[80,1024]{1,0:T(8,128)S(1)}, f32[80,1024]{1,0:T(8,128)S(1)}, u32[]{:S(2)}, u32[]{:S(2)}) collective-permute-start(f32[80,1024]{1,0:T(8,128)S(1)} %get-tuple-element.54), channel_id=1, source_target_pairs={{0,0},{8,9},{12,13},{16,17},{20,21},{24,25},{28,29},{17,18},{21,22... | collective-permute-start | bytes 983048 | tf_op jit(solution)/shard_map/ppermute | solution.py:524
  101.9 21.8 %collective-permute-start.19 = (f32[160,1024]{1,0:T(8,128)S(1)}, f32[160,1024]{1,0:T(8,128)S(1)}, u32[]{:S(2)}, u32[]{:S(2)}) collective-permute-start(f32[160,1024]{1,0:T(8,128)S(1)} %get-tuple-element.58), channel_id=1, source_target_pairs={{8,16},{12,20},{16,24},{20,28},{9,17},{13,21},{17,25},{21,29},{18,... | collective-permute-start | bytes 1966088 | tf_op jit(solution)/shard_map/ppermute | solution.py:524
  102.6 2.6 collective-permute-start.17
  103.3 20.4 %collective-permute-start.18 = (f32[80,1024]{1,0:T(8,128)S(1)}, f32[80,1024]{1,0:T(8,128)S(1)}, u32[]{:S(2)}, u32[]{:S(2)}) collective-permute-start(f32[80,1024]{1,0:T(8,128)S(1)} %get-tuple-element.57), channel_id=1, source_target_pairs={{0,0},{8,9},{12,13},{16,17},{20,21},{24,25},{28,29},{17,18},{21,22... | collective-permute-start | bytes 983048 | tf_op jit(solution)/shard_map/ppermute | solution.py:524
  125.1 20.4 %collective-permute-start.22 = (f32[160,1024]{1,0:T(8,128)S(1)}, f32[160,1024]{1,0:T(8,128)S(1)}, u32[]{:S(2)}, u32[]{:S(2)}) collective-permute-start(f32[160,1024]{1,0:T(8,128)S(1)} %get-tuple-element.61), channel_id=1, source_target_pairs={{16,24},{20,28},{9,17},{13,21},{17,25},{21,29},{18,26},{22,30}} | collective-permute-start | bytes 1966088 | tf_op jit(solution)/shard_map/ppermute | solution.py:524
  125.8 2.6 collective-permute-start.20
  126.5 19.0 %collective-permute-start.21 = (f32[80,1024]{1,0:T(8,128)S(1)}, f32[80,1024]{1,0:T(8,128)S(1)}, u32[]{:S(2)}, u32[]{:S(2)}) collective-permute-start(f32[80,1024]{1,0:T(8,128)S(1)} %get-tuple-element.60), channel_id=1, source_target_pairs={{0,0},{8,9},{12,13},{16,17},{20,21},{24,25},{28,29},{17,18},{21,22... | collective-permute-start | bytes 983048 | tf_op jit(solution)/shard_map/ppermute | solution.py:524
  147.1 20.3 %collective-permute-start.25 = (f32[160,1024]{1,0:T(8,128)S(1)}, f32[160,1024]{1,0:T(8,128)S(1)}, u32[]{:S(2)}, u32[]{:S(2)}) collective-permute-start(f32[160,1024]{1,0:T(8,128)S(1)} %get-tuple-element.64), channel_id=1, source_target_pairs={{17,25},{21,29},{18,26},{22,30}} | collective-permute-start | bytes 1966088 | tf_op jit(solution)/shard_map/ppermute | solution.py:524
  147.8 2.6 collective-permute-start.23
  148.5 18.9 %collective-permute-start.24 = (f32[80,1024]{1,0:T(8,128)S(1)}, f32[80,1024]{1,0:T(8,128)S(1)}, u32[]{:S(2)}, u32[]{:S(2)}) collective-permute-start(f32[80,1024]{1,0:T(8,128)S(1)} %get-tuple-element.63), channel_id=1, source_target_pairs={{0,0},{8,9},{12,13},{16,17},{20,21},{24,25},{28,29},{17,18},{21,22... | collective-permute-start | bytes 983048 | tf_op jit(solution)/shard_map/ppermute | solution.py:524
  168.8 22.0 %collective-permute-start.28 = (f32[160,1024]{1,0:T(8,128)S(1)}, f32[160,1024]{1,0:T(8,128)S(1)}, u32[]{:S(2)}, u32[]{:S(2)}) collective-permute-start(f32[160,1024]{1,0:T(8,128)S(1)} %get-tuple-element.67), channel_id=1, source_target_pairs={{18,26},{22,30}} | collective-permute-start | bytes 1966088 | tf_op jit(solution)/shard_map/ppermute | solution.py:524
  169.5 4.0 %collective-permute-start.29 = (f32[80,1024]{1,0:T(8,128)S(1)}, f32[80,1024]{1,0:T(8,128)S(1)}, u32[]{:S(2)}, u32[]{:S(2)}) collective-permute-start(f32[80,1024]{1,0:T(8,128)S(1)} %get-tuple-element.63), channel_id=1, source_target_pairs={{27,3},{31,7}} | collective-permute-start | bytes 983048 | tf_op jit(solution)/shard_map/ppermute | solution.py:524
  170.2 4.0 %collective-permute-start.30 = (f32[80,1024]{1,0:T(8,128)S(1)}, f32[80,1024]{1,0:T(8,128)S(1)}, u32[]{:S(2)}, u32[]{:S(2)}) collective-permute-start(f32[80,1024]{1,0:T(8,128)S(1)} %get-tuple-element.63), channel_id=1, source_target_pairs={{27,11},{31,15}} | collective-permute-start | bytes 983048 | tf_op jit(solution)/shard_map/ppermute | solution.py:524
  170.9 4.0 %collective-permute-start.26 = (f32[80,1024]{1,0:T(8,128)S(1)}, f32[80,1024]{1,0:T(8,128)S(1)}, u32[]{:S(2)}, u32[]{:S(2)}) collective-permute-start(f32[80,1024]{1,0:T(8,128)S(1)} %get-tuple-element.66), channel_id=1, source_target_pairs={{0,4},{4,8},{8,13},{13,17},{17,22},{22,26},{26,31}} | collective-permute-start | bytes 983048 | tf_op jit(solution)/shard_map/ppermute | solution.py:524
  171.6 19.2 %collective-permute-start.27 = (f32[80,1024]{1,0:T(8,128)S(1)}, f32[80,1024]{1,0:T(8,128)S(1)}, u32[]{:S(2)}, u32[]{:S(2)}) collective-permute-start(f32[80,1024]{1,0:T(8,128)S(1)} %get-tuple-element.66), channel_id=1, source_target_pairs={{0,0},{8,9},{12,13},{16,17},{20,21},{24,25},{28,29},{17,18},{21,22... | collective-permute-start | bytes 983048 | tf_op jit(solution)/shard_map/ppermute | solution.py:524
  173.5 22.8 %collective-permute-start.33 = (f32[80,1024]{1,0:T(8,128)S(1)}, f32[80,1024]{1,0:T(8,128)S(1)}, u32[]{:S(2)}, u32[]{:S(2)}) collective-permute-start(f32[80,1024]{1,0:T(8,128)S(1)} %get-tuple-element.66), channel_id=1, source_target_pairs={{27,3},{31,7}} | collective-permute-start | bytes 983048 | tf_op jit(solution)/shard_map/ppermute | solution.py:524
  174.2 22.8 %collective-permute-start.34 = (f32[80,1024]{1,0:T(8,128)S(1)}, f32[80,1024]{1,0:T(8,128)S(1)}, u32[]{:S(2)}, u32[]{:S(2)}) collective-permute-start(f32[80,1024]{1,0:T(8,128)S(1)} %get-tuple-element.66), channel_id=1, source_target_pairs={{27,11},{31,15}} | collective-permute-start | bytes 983048 | tf_op jit(solution)/shard_map/ppermute | solution.py:524
  193.0 5.7 %collective-permute-start.31 = (f32[80,1024]{1,0:T(8,128)S(1)}, f32[80,1024]{1,0:T(8,128)S(1)}, u32[]{:S(2)}, u32[]{:S(2)}) collective-permute-start(f32[80,1024]{1,0:T(8,128)S(1)} %get-tuple-element.69), channel_id=1, source_target_pairs={{0,4},{4,8},{8,13},{13,17},{17,22},{22,26},{26,31}} | collective-permute-start | bytes 983048 | tf_op jit(solution)/shard_map/ppermute | solution.py:524
  193.7 14.6 %collective-permute-start.32 = (f32[80,1024]{1,0:T(8,128)S(1)}, f32[80,1024]{1,0:T(8,128)S(1)}, u32[]{:S(2)}, u32[]{:S(2)}) collective-permute-start(f32[80,1024]{1,0:T(8,128)S(1)} %get-tuple-element.69), channel_id=1, source_target_pairs={{0,0},{8,9},{12,13},{16,17},{20,21},{24,25},{28,29},{17,18},{21,22... | collective-permute-start | bytes 983048 | tf_op jit(solution)/shard_map/ppermute | solution.py:524
  195.7 18.4 %collective-permute-start.38 = (f32[80,1024]{1,0:T(8,128)S(1)}, f32[80,1024]{1,0:T(8,128)S(1)}, u32[]{:S(2)}, u32[]{:S(2)}) collective-permute-start(f32[80,1024]{1,0:T(8,128)S(1)} %get-tuple-element.69), channel_id=1, source_target_pairs={{27,3},{31,7}} | collective-permute-start | bytes 983048 | tf_op jit(solution)/shard_map/ppermute | solution.py:524
  196.4 19.6 %collective-permute-start.39 = (f32[80,1024]{1,0:T(8,128)S(1)}, f32[80,1024]{1,0:T(8,128)S(1)}, u32[]{:S(2)}, u32[]{:S(2)}) collective-permute-start(f32[80,1024]{1,0:T(8,128)S(1)} %get-tuple-element.69), channel_id=1, source_target_pairs={{27,11},{31,15}} | collective-permute-start | bytes 983048 | tf_op jit(solution)/shard_map/ppermute | solution.py:524
  209.9 6.1 %collective-permute-start.40 = (f32[80,1024]{1,0:T(8,128)S(1)}, f32[80,1024]{1,0:T(8,128)S(1)}, u32[]{:S(2)}, u32[]{:S(2)}) collective-permute-start(f32[80,1024]{1,0:T(8,128)S(1)} %get-tuple-element.76), channel_id=1, source_target_pairs={{27,3},{31,7}} | collective-permute-start | bytes 983048 | tf_op jit(solution)/shard_map/ppermute | solution.py:524
  210.6 5.4 %collective-permute-start.41 = (f32[80,1024]{1,0:T(8,128)S(1)}, f32[80,1024]{1,0:T(8,128)S(1)}, u32[]{:S(2)}, u32[]{:S(2)}) collective-permute-start(f32[80,1024]{1,0:T(8,128)S(1)} %get-tuple-element.76), channel_id=1, source_target_pairs={{27,11},{31,15}} | collective-permute-start | bytes 983048 | tf_op jit(solution)/shard_map/ppermute | solution.py:524
  211.3 4.7 %collective-permute-start.42 = (f32[80,1024]{1,0:T(8,128)S(1)}, f32[80,1024]{1,0:T(8,128)S(1)}, u32[]{:S(2)}, u32[]{:S(2)}) collective-permute-start(f32[80,1024]{1,0:T(8,128)S(1)} %get-tuple-element.76), channel_id=1, source_target_pairs={{27,19},{31,23}} | collective-permute-start | bytes 983048 | tf_op jit(solution)/shard_map/ppermute | solution.py:524
  214.1 18.4 %collective-permute-start.43 = (f32[160,1024]{1,0:T(8,128)S(1)}, f32[160,1024]{1,0:T(8,128)S(1)}, u32[]{:S(2)}, u32[]{:S(2)}) collective-permute-start(f32[160,1024]{1,0:T(8,128)S(1)} %shard_map.81.refs_6_.refs_5_.refs_1_), channel_id=1, source_target_pairs={{0,4},{4,0},{1,5},{5,1},{9,13},{13,9},{2,6},{6,2},{10,14},{14,10},... | collective-permute-start | bytes 1966088 | tf_op jit(solution)/shard_map/ppermute | solution.py:524
  217.7 22.9 %collective-permute-start.44 = (f32[160,1024]{1,0:T(8,128)S(1)}, f32[160,1024]{1,0:T(8,128)S(1)}, u32[]{:S(2)}, u32[]{:S(2)}) collective-permute-start(f32[160,1024]{1,0:T(8,128)S(1)} %shard_map.85.refs_2_), channel_id=1, source_target_pairs={{0,4},{4,0},{1,5},{5,1},{9,13},{13,9},{2,6},{6,2},{10,14},{14,10},... | collective-permute-start | bytes 1966088 | tf_op jit(solution)/shard_map/ppermute | solution.py:524
  221.6 8.4 %collective-permute-start.35 = (f32[320,256]{1,0:T(8,128)S(1)}, f32[320,256]{1,0:T(8,128)S(1)}, u32[]{:S(2)}, u32[]{:S(2)}) collective-permute-start(f32[320,256]{1,0:T(8,128)S(1)} %get-tuple-element.73), channel_id=1, source_target_pairs={{0,1},{4,5},{9,10},{13,14},{18,19},{22,23},{27,24},{31,28}} | collective-permute-start | bytes 983048 | tf_op jit(solution)/shard_map/ppermute | solution.py:524
  222.9 7.1 %collective-permute-start.36 = (f32[320,256]{1,0:T(8,128)S(1)}, f32[320,256]{1,0:T(8,128)S(1)}, u32[]{:S(2)}, u32[]{:S(2)}) collective-permute-start(f32[320,256]{1,0:T(8,128)S(1)} %get-tuple-element.74), channel_id=1, source_target_pairs={{0,2},{4,6},{9,11},{13,15},{18,16},{22,20},{27,25},{31,29}} | collective-permute-start | bytes 983048 | tf_op jit(solution)/shard_map/ppermute | solution.py:524
  223.6 6.4 %collective-permute-start.37 = (f32[320,256]{1,0:T(8,128)S(1)}, f32[320,256]{1,0:T(8,128)S(1)}, u32[]{:S(2)}, u32[]{:S(2)}) collective-permute-start(f32[320,256]{1,0:T(8,128)S(1)} %get-tuple-element.75), channel_id=1, source_target_pairs={{0,3},{4,7},{9,8},{13,12},{18,17},{22,21},{27,26},{31,30}} | collective-permute-start | bytes 983048 | tf_op jit(solution)/shard_map/ppermute | solution.py:524
  249.6 6.2 %collective-permute-start.45 = (f32[320,512]{1,0:T(8,128)S(1)}, f32[320,512]{1,0:T(8,128)S(1)}, u32[]{:S(2)}, u32[]{:S(2)}) collective-permute-start(f32[320,512]{1,0:T(8,128)S(1)} %shard_map.87.refs_5_), channel_id=1, source_target_pairs={{0,1},{1,0},{2,3},{3,2},{4,5},{5,4},{6,7},{7,6},{8,9},{9,8},{10,11... | collective-permute-start | bytes 1966088 | tf_op jit(solution)/shard_map/ppermute | solution.py:524
  255.8 17.2 %collective-permute-start.46 = (f32[320,512]{1,0:T(8,128)S(1)}, f32[320,512]{1,0:T(8,128)S(1)}, u32[]{:S(2)}, u32[]{:S(2)}) collective-permute-start(f32[320,512]{1,0:T(8,128)S(1)} %shard_map.89.refs_5_), channel_id=1, source_target_pairs={{0,2},{1,3},{2,0},{3,1},{4,6},{5,7},{6,4},{7,5},{8,10},{9,11},{10,... | collective-permute-start | bytes 1966088 | tf_op jit(solution)/shard_map/ppermute | solution.py:524
  262.0 17.1 %collective-permute-start.47 = (f32[320,512]{1,0:T(8,128)S(1)}, f32[320,512]{1,0:T(8,128)S(1)}, u32[]{:S(2)}, u32[]{:S(2)}) collective-permute-start(f32[320,512]{1,0:T(8,128)S(1)} %shard_map.90.refs_5_), channel_id=1, source_target_pairs={{0,1},{1,0},{2,3},{3,2},{4,5},{5,4},{6,7},{7,6},{8,9},{9,8},{10,11... | collective-permute-start | bytes 1966088 | tf_op jit(solution)/shard_map/ppermute | solution.py:524
  (1 other events, 7.5 us)
